TPU v7x, 32 devices: a whole 2x2x4 slice. The times are simulated.
32 devices in a mesh: dp: 16 (over z, x, core), pair: 2 (over y).
Axes of the slice: x: 2, y: 2, z: 4, core: 2. Of those that a mesh axis runs over, the one named last changes fastest.
Arguments:
- tokens: bfloat16 [65536, 512], P(('dp', 'pair')), may hold values from -12 to 12
- cotangent: bfloat16 [65536, 512], P(('dp', 'pair')), may hold values from -6 to 6
- counts: int32 [128], P(('dp', 'pair')), may hold values from 12 to 64, as said below
- shifts: int32 [128, 2], P(('dp', 'pair')), may hold values from 0 to 3
- qkv_weight: bfloat16 [512, 1536], P(('dp', 'pair')), may hold values from -0.25 to 0.25
- proj_weight: bfloat16 [512, 512], P(('dp', 'pair')), may hold values from -1 to 1
- up_weight: bfloat16 [512, 2048], P(('dp', 'pair')), may hold values from -0.25 to 0.25
- down_weight: bfloat16 [2048, 512], P(('dp', 'pair')), may hold values from -0.1875 to 0.1875
- first_gain: bfloat16 [512], P(('dp', 'pair')), may hold values from 0.099609375 to 1.8984375
- first_bias: bfloat16 [512], P(('dp', 'pair')), may hold values from -3 to 3
- second_gain: bfloat16 [512], P(('dp', 'pair')), may hold values from 0.099609375 to 1.8984375
- second_bias: bfloat16 [512], P(('dp', 'pair')), may hold values from -3 to 3
- query_bias: bfloat16 [512], P(('dp', 'pair')), may hold values from -3 to 3
- value_bias: bfloat16 [512], P(('dp', 'pair')), may hold values from -3 to 3
- proj_bias: bfloat16 [512], P(('dp', 'pair')), may hold values from -3 to 3
- up_bias: bfloat16 [2048], P(('dp', 'pair')), may hold values from -3 to 3
- down_bias: bfloat16 [512], P(('dp', 'pair')), may hold values from -3 to 3
- rel_table: bfloat16 [49, 16], replicated, may hold values from -6 to 6
Outputs:
- out: bfloat16 [65536, 512], P(('dp', 'pair'))
- grad_tokens: float32 [65536, 512], P(('dp', 'pair'))
- grad_qkv_weight: float32 [512, 1536], P(('dp', 'pair'))
- grad_proj_weight: float32 [512, 512], P(('dp', 'pair'))
- grad_up_weight: float32 [512, 2048], P(('dp', 'pair'))
- grad_down_weight: float32 [2048, 512], P(('dp', 'pair'))
- grad_first_gain: float32 [512], P(('dp', 'pair'))
- grad_first_bias: float32 [512], P(('dp', 'pair'))
- grad_second_gain: float32 [512], P(('dp', 'pair'))
- grad_second_bias: float32 [512], P(('dp', 'pair'))
- grad_query_bias: float32 [512], P(('dp', 'pair'))
- grad_value_bias: float32 [512], P(('dp', 'pair'))
- grad_proj_bias: float32 [512], P(('dp', 'pair'))
- grad_up_bias: float32 [2048], P(('dp', 'pair'))
- grad_down_bias: float32 [512], P(('dp', 'pair'))
- grad_rel_table: float32 [49, 16], replicated
Inputs may be any that keep to these rules, and one draw needn't show every extreme that they name: `counts`: patch rows at or beyond a clip's count are padding; some clip has all 64 rows visible.
All inputs are finite; a program needn't handle non-finite values.
Results may differ from a plain program's by a relative error of at most 0.014.
Values may be sent and summed in bfloat16 or wider, within the bound.
No kernel may reach another device: no remote copies, remote signals or barrier semaphores. Data moves between devices by JAX's collectives and lax.ppermute only.
A program may use at most 192 MiB of HBM per device.

v0:
```python
import functools

import jax
import jax.numpy as jnp
import numpy as np
from jax import lax
from jax.experimental import pallas as pl
from jax.experimental.pallas import tpu as pltpu
from jax.sharding import PartitionSpec as P

HEADS = 16
GRID_T = 64
GRID_F = 8
WIN = 4
PLACES = WIN * WIN
PATCHES = GRID_T * GRID_F
BLOCK = 64
BLOCKS = PATCHES // BLOCK
AXES = ("dp", "pair")
UNIT = 16
SHARDS = 32
RELS = (2 * WIN - 1) ** 2
CORE = (2,)
PLANE = (4, 1, 5)
COLUMN = (8, 16, 24)

EPS = 1e-06
HIGH = lax.Precision.HIGHEST
NEGATIVE = -1e30
F32 = jnp.float32
BF16 = jnp.bfloat16
LOG2_E = float(np.log2(np.e))
LOG_BELL = float(np.log2(2.0 / np.sqrt(2.0 * np.pi)))
VMEM_BYTES = 60 * 1024 * 1024
ROWS = 32


def dot_nn(a, b):
    return lax.dot_general(a, b, (((1,), (0,)), ((), ())), preferred_element_type=F32)


def dot_nt(a, b):
    return lax.dot_general(a, b, (((1,), (1,)), ((), ())), preferred_element_type=F32)


def dot_tn(a, b):
    return lax.dot_general(a, b, (((0,), (0,)), ((), ())), preferred_element_type=F32)


def norm_stats(values):
    row_mean = jnp.mean(values, -1, keepdims=True)
    centred = values - row_mean
    inv_std = lax.rsqrt(jnp.mean(centred * centred, -1, keepdims=True) + EPS)
    return centred * inv_std, inv_std


def norm_back(grad_out, normed, inv_std, gain):
    grad_normed = grad_out * gain
    return inv_std * (
        grad_normed
        - jnp.mean(grad_normed, -1, keepdims=True)
        - normed * jnp.mean(grad_normed * normed, -1, keepdims=True)
    )


def iota(shape, dim):
    return lax.broadcasted_iota(jnp.int32, shape, dim)


def fill_perm(perm_ref, s, u, to_windows):
    for r0 in range(0, PATCHES, BLOCK):
        row = iota((BLOCK, 128), 0) + r0
        if to_windows:
            a = (row >> 2) & 3
            b = row & 3
            t = (4 * (row >> 5) + a + s) & (GRID_T - 1)
            f = (4 * ((row >> 4) & 1) + b + u) & (GRID_F - 1)
            source = t * GRID_F + f
        else:
            r = ((row >> 3) - s) & (GRID_T - 1)
            q = ((row & 7) - u) & (GRID_F - 1)
            source = (r >> 2) * 32 + (q >> 2) * 16 + (r & 3) * 4 + (q & 3)
        lane = iota((BLOCK, 128), 1)
        for c0 in range(0, PATCHES, 128):
            perm_ref[r0 : r0 + BLOCK, c0 : c0 + 128] = jnp.where(
                source == lane + c0, 1.0, 0.0
            ).astype(BF16)


def compact_code(rows):
    row = iota((rows, 128), 0)
    lane = iota((rows, 128), 1)
    return ((lane >> 4) - (row >> 4) - (lane >> 6)) & 3


def head_lanes(dtype):
    lane = iota((16, 128), 1) >> 5
    return [jnp.where(lane == hh, 1.0, 0.0).astype(dtype) for hh in range(4)]


def expand_rows(tile, g, lanes):
    parts = []
    for hh in range(4):
        half, ab = hh & 1, hh >> 1
        for slot in range(4):
            w = (slot - half - g - 2 * ab) % 4
            parts.append(tile[16 * w : 16 * w + 16, :] * lanes[hh])
    return jnp.concatenate(parts, axis=0)


def compact(code, s0, s1):
    return jnp.where(
        code == 0,
        s0[:, :128],
        jnp.where(code == 1, s1[:, :128], jnp.where(code == 2, s0[:, 128:], s1[:, 128:])),
    )


def parts_of(x, count):
    parts = []
    for _ in range(count):
        parts.append(x.astype(BF16))
        x = x - parts[-1].astype(F32)
    return parts


def group_matrix(count, first_only):
    row = iota((128 * count, 128), 0) & 127
    same = (row >> 4) == (iota((128 * count, 128), 1) >> 4)
    if first_only:
        same = same & ((row & 15) == 0)
    return jnp.where(same, 1.0, 0.0).astype(BF16)


def put_parts(part_ref, rows, x, count):
    for i, part in enumerate(parts_of(x, count)):
        part_ref[rows, 128 * i : 128 * i + 128] = part


def allowed_tile(block, s, u, count):
    row = iota((BLOCK, 128), 0)
    key = iota((BLOCK, 128), 1) & 15
    band = 4 * (2 * block + (row >> 5))
    side = 4 * ((row >> 4) & 1)
    r_i = band + ((row >> 2) & 3) + s
    q_i = side + (row & 3) + u
    r_j = band + (key >> 2) + s
    q_j = side + (key & 3) + u
    wrap_i = (r_i >> 6) * 2 + (q_i >> 3)
    wrap_j = (r_j >> 6) * 2 + (q_j >> 3)
    visible = ((r_j & (GRID_T - 1)) < count) | ((row & 15) == key)
    return (wrap_i == wrap_j) & visible


def device_id():
    return lax.axis_index("dp") * lax.axis_size("pair") + lax.axis_index("pair")


def place_code():
    row = iota((PLACES, 256), 0)
    key = iota((PLACES, 256), 1) & 15
    return ((row >> 2) - (key >> 2) + WIN - 1) * (2 * WIN - 1) + ((row & 3) - (key & 3) + WIN - 1)


def head_select(w):
    row = iota((256, 256), 0)
    lane = iota((256, 256), 1)
    half = (lane >> 6) & 1
    e = ((lane >> 4) - w - half) & 3
    head = 8 * (lane >> 7) + 4 * (e & 1) + 2 * (e >> 1) + half
    return jnp.where((row & 15 == lane & 15) & (row >> 4 == head), 1.0, 0.0).astype(BF16)


def head_repeat():
    return jnp.where(iota((HEADS, 256), 0) == iota((HEADS, 256), 1) >> 4, 1.0, 0.0).astype(BF16)


def fill_positions(pos_ref, table_ref):
    spread = dot_tn(table_ref[...], head_repeat())
    code = place_code()
    rows = jnp.zeros((PLACES, 256), F32)
    for e in range(RELS):
        rows = jnp.where(code == e, spread[e : e + 1, :], rows)
    rows = rows.astype(BF16)
    for w in range(4):
        pos_ref[16 * w : 16 * w + 16, :] = dot_nn(rows, head_select(w))


def table_rows(gpos, scratch_ref):
    rows = jnp.zeros((PLACES, 256), F32)
    for w in range(4):
        select = head_select(w)
        for part in parts_of(gpos[16 * w : 16 * w + 16, :], 2):
            rows = rows + dot_nt(part, select)
    code = place_code()
    scratch_ref[...] = jnp.zeros_like(scratch_ref)
    for e in range(RELS):
        scratch_ref[e : e + 1, :] = jnp.sum(jnp.where(code == e, rows, 0.0), 0, keepdims=True)
    repeat = head_repeat()
    high, low = parts_of(scratch_ref[...], 2)
    return dot_nt(repeat, high) + dot_nt(repeat, low)


def mix_matrix():
    row = iota((512, 512), 0)
    lane = iota((512, 512), 1)
    return jnp.where(row == 128 * ((lane >> 4) & 3) + 16 * (lane >> 6) + (lane & 15), 1.0, 0.0).astype(BF16)


def fetch_blocks(piece_refs, masks, full_ref, sems):
    if masks is None:
        copies = [pltpu.make_async_copy(piece_refs[0], full_ref, sems.at[0])]
    else:
        me = device_id()
        copies = []
        for piece, (start, piece_masks) in zip(piece_refs, masks):
            cols = pl.ds(start, piece.shape[1])
            for j, mask in enumerate(piece_masks):
                at = pl.multiple_of((me ^ mask) * UNIT, UNIT)
                copies.append(
                    pltpu.make_async_copy(
                        piece.at[pl.ds(j * UNIT, UNIT), :], full_ref.at[pl.ds(at, UNIT), cols], sems.at[len(copies)]
                    )
                )
    for copy in copies:
        copy.start()
    return copies


def block_device(place, relative):
    if not relative:
        return place
    plane = (place >> 2) & 3
    return device_id() ^ (2 * (place >> 4) + 4 * (plane & 1) + (plane >> 1) + 8 * (place & 3))


def block_rows(place, relative):
    return pl.ds(pl.multiple_of(block_device(place, relative) * UNIT, UNIT), UNIT)


def put_block(send_refs, place, block):
    rows = send_refs[0].shape[0]
    at = place * UNIT
    send_refs[at // rows][at % rows : at % rows + UNIT, :] = block


def pack_kernel(*refs):
    vectors, (qkv_ref, proj_ref, up_ref, down_ref, first_ref, second_ref) = refs[:9], refs[9:]
    width = proj_ref.shape[1]
    first_ref[:, : 3 * width] = qkv_ref[...]
    rows = [v[...].astype(F32).reshape(1, UNIT) for v in vectors[:8]]
    bias = vectors[8][...].astype(F32).reshape(1, 4 * UNIT)
    rows += [bias[:, UNIT * q : UNIT * q + UNIT] for q in range(4)]
    rows = jnp.concatenate(rows + [jnp.zeros((116, UNIT), F32)], axis=0)
    first_ref[:, 3 * width :] = jnp.transpose(rows).astype(BF16)
    second_ref[:, :width] = proj_ref[...]
    second_ref[:, width : 5 * width] = up_ref[...]
    for q in range(4):
        second_ref[:, (5 + q) * width : (6 + q) * width] = down_ref[UNIT * q : UNIT * q + UNIT, :]


def pack(vectors, weights):
    width = weights[1].shape[1]
    return pl.pallas_call(
        pack_kernel,
        out_shape=[struct((UNIT, cols * width + more), BF16) for cols, more in ((3, 128), (9, 0))],
        compiler_params=pltpu.CompilerParams(vmem_limit_bytes=VMEM_BYTES),
        name="pack",
    )(*vectors, *weights)


def attend_kernel(
    masks, shift_ref, count_ref, tok_ref, table_ref, *refs
):
    pieces = refs[: 1 if masks is None else len(masks)]
    (
        qkv_ref, prob_ref, ctx_ref, w_ref, vec_ref,
        perm_ref, rows_ref, act_ref, score_ref, low_ref, ctxw_ref, pos_ref, group_ref, *part_refs, sems,
    ) = refs[len(pieces) :]
    width = tok_ref.shape[1]
    scale = (width // HEADS) ** (-0.5)
    clip = pl.program_id(0)
    s = shift_ref[0, clip]
    u = shift_ref[1, clip]
    count = count_ref[clip]

    @pl.when(clip == 0)
    def _():
        copies = fetch_blocks(pieces, masks, w_ref, sems)
        fill_positions(pos_ref, table_ref)
        for copy in copies:
            copy.wait()
        vec_ref[...] = jnp.transpose(w_ref[:, 3 * width :].astype(F32))[:16, :]
        flat = vec_ref[8:16, :].astype(BF16)
        flat = jnp.concatenate(
            [
                jnp.concatenate([flat[q : q + 1, 128 * c : 128 * c + 128] for q in range(4)], axis=1)
                for c in range(4)
            ]
            + [jnp.zeros((12, width), BF16)],
            axis=0,
        )
        vec_ref[8:16, :] = dot_nn(flat, mix_matrix())[:8, :]

    fill_perm(perm_ref, s, u, True)
    rows_ref[...] = dot_nn(perm_ref[...], tok_ref[...])
    for r in range(0, PATCHES, ROWS):
        normed, _ = norm_stats(rows_ref[r : r + ROWS, :])
        act_ref[r : r + ROWS, :] = (normed * vec_ref[0:1, :] + vec_ref[1:2, :]).astype(BF16)
    for c in range(3):
        cols = slice(c * width, (c + 1) * width)
        out = dot_nn(act_ref[...], w_ref[:, cols])
        if c == 0:
            out = out + vec_ref[2:3, :]
        if c == 2:
            out = out + vec_ref[3:4, :]
        qkv_ref[:, cols] = out.astype(BF16)
    lanes = head_lanes(BF16)
    code = compact_code(BLOCK)
    for b in range(BLOCKS):
        rows = slice(b * BLOCK, (b + 1) * BLOCK)
        for p in range(2):
            parts = []
            for g in range(2):
                c0 = 128 * (2 * p + g)
                keys = expand_rows(qkv_ref[rows, width + c0 : width + c0 + 128], g, lanes)
                parts.append(dot_nt(qkv_ref[rows, c0 : c0 + 128], keys))
            score_ref[rows, 128 * p : 128 * p + 128] = compact(code, *parts)
    first_lane = group_matrix(3, True)
    all_lanes = group_matrix(2, False)
    blocks = [slice(b * BLOCK, (b + 1) * BLOCK) for b in range(BLOCKS)]
    pairs = [slice(128 * p, 128 * p + 128) for p in range(2)]
    for b, rows in enumerate(blocks):
        allowed = allowed_tile(b, s, u, count)
        for p, cols in enumerate(pairs):
            logits = score_ref[rows, cols] * scale + pos_ref[:, cols]
            logits = jnp.where(allowed, logits, NEGATIVE)
            score_ref[rows, cols] = logits
            for k in (1, 2, 4, 8):
                logits = jnp.maximum(logits, pltpu.roll(logits, 128 - k, 1))
            put_parts(part_refs[p], rows, logits, 3)
    for p, cols in enumerate(pairs):
        group_ref[:, cols] = dot_nn(part_refs[p][...], first_lane)
    for p, cols in enumerate(pairs):
        for rows in blocks:
            e = jnp.exp(score_ref[rows, cols] - group_ref[rows, cols])
            score_ref[rows, cols] = e
            put_parts(part_refs[p], rows, e, 2)
    for p, cols in enumerate(pairs):
        group_ref[:, cols] = dot_nn(part_refs[p][:, :256], all_lanes)
    for p, cols in enumerate(pairs):
        for rows in blocks:
            prob = score_ref[rows, cols] * pl.reciprocal(group_ref[rows, cols])
            prob_ref[rows, cols] = prob
            low_ref[rows, cols] = prob.astype(BF16)
    spread = [jnp.where(code == e, 1.0, 0.0).astype(BF16) for e in range(4)]
    for b in range(BLOCKS):
        rows = slice(b * BLOCK, (b + 1) * BLOCK)
        for p in range(2):
            low = low_ref[rows, 128 * p : 128 * p + 128]
            for g in range(2):
                c0 = 128 * (2 * p + g)
                values = expand_rows(qkv_ref[rows, 2 * width + c0 : 2 * width + c0 + 128], g, lanes)
                wide = jnp.concatenate([low * spread[g], low * spread[2 + g]], axis=1)
                ctxw_ref[rows, c0 : c0 + 128] = dot_nn(wide, values).astype(BF16)
    fill_perm(perm_ref, s, u, False)
    ctx_ref[...] = dot_nn(perm_ref[...], ctxw_ref[...]).astype(BF16)


def weave(first, second):
    done = 0
    for i, step in enumerate(first):
        step()
        upto = (i + 1) * len(second) // len(first)
        for other in second[done:upto]:
            other()
        done = upto
    for other in second[done:]:
        other()


def mlp_kernel(
    masks, relative, tok_ref, ctx_ref, cot_ref, vec_ref, *refs
):
    pieces = refs[: 1 if masks is None else len(masks)]
    (
        *gelu_refs, gmid_ref, gctx_ref, small_ref, wp_out_ref, wd_out_ref,
    ) = refs[len(pieces) : len(pieces) + 9]
    *send_refs, w_ref, wd_ref, accp_ref, accu_ref, accd_ref, mid_ref, act_ref, branch_ref, gact_ref = refs[
        len(pieces) + 9 : -13
    ]
    hid_refs, gg_refs, gh_refs, sems = refs[-13:-9], refs[-9:-5], refs[-5:-1], refs[-1]
    keeps = [
        pltpu.make_async_copy(w_ref.at[:, : tok_ref.shape[1]], wp_out_ref, sems.at[0]),
        pltpu.make_async_copy(wd_ref, wd_out_ref, sems.at[1]),
    ]
    step = pl.program_id(0)
    tile, width = tok_ref.shape
    ff = 4 * width
    chunk = 512

    @pl.when(step == 0)
    def _():
        copies = fetch_blocks(pieces, masks, w_ref, sems)
        accp_ref[...] = jnp.zeros_like(accp_ref)
        accu_ref[...] = jnp.zeros_like(accu_ref)
        accd_ref[...] = jnp.zeros_like(accd_ref)
        small_ref[...] = jnp.zeros_like(small_ref)
        for copy in copies:
            copy.wait()
        for i in range(SHARDS):
            for q in range(4):
                at = UNIT * (4 * i + q)
                weight = w_ref[UNIT * i : UNIT * i + UNIT, (5 + q) * width : (6 + q) * width]
                wd_ref[at : at + UNIT, :] = weight * jnp.asarray(0.5, BF16)
        for keep in keeps:
            keep.start()

    gain = vec_ref[4:5, :]
    bias = vec_ref[5:6, :]
    half = chunk // 2
    count = ff // chunk
    sums = [jnp.zeros((1, width), F32) for _ in range(4)]

    def norm_rows(r):
        rows = slice(r, r + ROWS)
        mid = mid_ref[rows, :] + tok_ref[rows, :].astype(F32) + vec_ref[6:7, :]
        mid_ref[rows, :] = mid
        normed, _ = norm_stats(mid)
        act_ref[rows, :] = (normed * gain + bias).astype(BF16)

    def back_rows(r):
        rows = slice(r, r + ROWS)
        normed, inv = norm_stats(mid_ref[rows, :])
        g_act = gact_ref[rows, :]
        cot = cot_ref[rows, :].astype(F32)
        g_mid = cot + norm_back(g_act, normed, inv, gain)
        gmid_ref[rows, :] = g_mid
        g_branch = g_mid.astype(BF16)
        branch_ref[rows, :] = g_branch
        for i, part in enumerate((g_act * normed, g_act, g_branch.astype(F32), cot)):
            sums[i] = sums[i] + jnp.sum(part, 0, keepdims=True)

    totals = {}

    def bend(c, k, r):
        lanes = slice(k, k + 128)
        rows = slice(r, r + 64)
        h = hid_refs[c][rows, lanes] + vec_ref[8 + c : 9 + c, lanes]
        z = h * (0.5**0.5)
        double_phi = 1.0 + lax.erf(z)
        double_bell = jnp.exp2(LOG_BELL - (z * z) * LOG2_E)
        gelu_refs[c][rows, lanes] = (h * double_phi).astype(BF16)
        g_hidden = gg_refs[c][rows, lanes] * (double_phi + h * double_bell)
        gh_refs[c][rows, lanes] = g_hidden.astype(BF16)
        part = jnp.sum(g_hidden.reshape(8, 8, 128), 0)
        totals[c, k] = part if r == 0 else totals[c, k] + part
        if r + 64 == tile:
            small_ref[8 + c : 9 + c, lanes] += jnp.sum(totals[c, k], 0, keepdims=True)

    def up(c, m, k):
        at = width + c * chunk + k
        hid_refs[c][m : m + half, k : k + half] = dot_nn(act_ref[m : m + half, :], w_ref[:, at : at + half])

    def down_back(c, m, k):
        at = c * chunk + k
        gg_refs[c][m : m + half, k : k + half] = dot_nt(cot_ref[m : m + half, :], wd_ref[at : at + half, :])

    def up_back(c, m, k):
        weight = w_ref[k : k + half, width + c * chunk : width + (c + 1) * chunk]
        part = dot_nt(gh_refs[c][m : m + half, :], weight)
        if c == 0:
            gact_ref[m : m + half, k : k + half] = part
        else:
            gact_ref[m : m + half, k : k + half] += part

    def down_grad(c, m, k):
        at = c * chunk + m
        accd_ref[at : at + half, k : k + half] += dot_tn(gelu_refs[c][:, m : m + half], cot_ref[:, k : k + half])

    def up_grad(c, m, k):
        at = c * chunk + k
        accu_ref[m : m + half, at : at + half] += dot_tn(act_ref[:, m : m + half], gh_refs[c][:, k : k + half])

    def all_of(fn, c):
        return [functools.partial(fn, c, m, k) for k in (0, half) for m in (0, half)]

    always = step >= 0

    @pl.when(always)
    def _():
        mid_ref[...] = dot_nn(ctx_ref[...], w_ref[:, :width])
        weave(
            all_of(down_back, 0) + all_of(down_back, 1),
            [functools.partial(norm_rows, r) for r in range(0, tile, ROWS)],
        )
        weave(all_of(up, 0), [])

    for c in range(count):

        @pl.when(always)
        def _(c=c):
            products = []
            if c + 1 < count:
                products += all_of(up, c + 1)
            if c > 0:
                products += all_of(up_back, c - 1)
            if c + 2 < count:
                products += all_of(down_back, c + 2)
            if c > 1:
                products += all_of(down_grad, c - 2) + all_of(up_grad, c - 2)
            weave(products, [functools.partial(bend, c, k, r) for k in range(0, chunk, 128) for r in range(0, tile, 64)])

    @pl.when(always)
    def _():
        weave(all_of(up_back, count - 1), [])
        weave(
            all_of(down_grad, count - 2)
            + all_of(up_grad, count - 2)
            + all_of(down_grad, count - 1)
            + all_of(up_grad, count - 1),
            [functools.partial(back_rows, r) for r in range(0, tile, ROWS)],
        )
        for i in range(4):
            small_ref[4 + i : 5 + i, :] += sums[i]
        gctx_ref[...] = dot_nt(branch_ref[...], w_ref[:, :width]).astype(BF16)
        accp_ref[...] += dot_tn(ctx_ref[...], branch_ref[...])

    @pl.when(step == pl.num_programs(0) - 1)
    def _():
        for place in range(SHARDS):
            rows = block_rows(place, relative)
            block = [accp_ref[rows, :], accu_ref[rows, :]]
            down = pl.multiple_of(block_device(place, relative) * (4 * UNIT), 4 * UNIT)
            block += [accd_ref[pl.ds(down + UNIT * q, UNIT), :] * 0.5 for q in range(4)]
            put_block(send_refs, place, jnp.concatenate(block, axis=1).astype(BF16))
        for keep in keeps:
            keep.wait()


def attend_back_kernel(
    start, shift_ref, qkv_ref, prob_ref, gctx_ref, _, gqn_ref, gpos_ref,
    perm_ref, do_ref, dp_ref, low_ref, gs_ref, lowt_ref, gst_ref, gqw_ref, group_ref, *part_refs,
):
    width = gctx_ref.shape[1]
    scale = (width // HEADS) ** (-0.5)
    step = pl.program_id(0)
    s = shift_ref[0, step + start]
    u = shift_ref[1, step + start]

    @pl.when(step == 0)
    def _():
        gpos_ref[...] = jnp.zeros_like(gpos_ref)

    fill_perm(perm_ref, s, u, True)
    do_ref[...] = dot_nn(perm_ref[...], gctx_ref[...]).astype(BF16)
    lanes = head_lanes(BF16)
    code = compact_code(BLOCK)
    for b in range(BLOCKS):
        rows = slice(b * BLOCK, (b + 1) * BLOCK)
        for p in range(2):
            parts = []
            for g in range(2):
                c0 = 128 * (2 * p + g)
                values = expand_rows(qkv_ref[rows, 2 * width + c0 : 2 * width + c0 + 128], g, lanes)
                parts.append(dot_nt(do_ref[rows, c0 : c0 + 128], values))
            dp_ref[rows, 128 * p : 128 * p + 128] = compact(code, *parts)
    all_lanes = group_matrix(2, False)
    blocks = [slice(b * BLOCK, (b + 1) * BLOCK) for b in range(BLOCKS)]
    pairs = [slice(128 * p, 128 * p + 128) for p in range(2)]
    for p, cols in enumerate(pairs):
        for rows in blocks:
            put_parts(part_refs[p], rows, prob_ref[rows, cols] * dp_ref[rows, cols], 2)
    for p, cols in enumerate(pairs):
        group_ref[:, cols] = dot_nn(part_refs[p][...], all_lanes)
    for p, cols in enumerate(pairs):
        total = jnp.zeros((BLOCK, 128), F32)
        for rows in blocks:
            prob = prob_ref[rows, cols]
            g_scores = (prob * (dp_ref[rows, cols] - group_ref[rows, cols])).astype(BF16)
            gs_ref[rows, cols] = g_scores
            low_ref[rows, cols] = prob.astype(BF16)
            total = total + g_scores.astype(F32)
        gpos_ref[:, cols] += total
    spread = [jnp.where(code == e, 1.0, 0.0).astype(BF16) for e in range(4)]
    for b in range(BLOCKS):
        rows = slice(b * BLOCK, (b + 1) * BLOCK)
        for p in range(2):
            low = gs_ref[rows, 128 * p : 128 * p + 128]
            for g in range(2):
                c0 = 128 * (2 * p + g)
                keys = expand_rows(qkv_ref[rows, width + c0 : width + c0 + 128], g, lanes)
                wide = jnp.concatenate([low * spread[g], low * spread[2 + g]], axis=1)
                gqw_ref[rows, c0 : c0 + 128] = (dot_nn(wide, keys) * scale).astype(BF16)
    lowt_ref[...] = jnp.transpose(low_ref[...])
    gst_ref[...] = jnp.transpose(gs_ref[...])
    row_t = iota((BLOCK, 128), 0)
    lane_t = iota((BLOCK, 128), 1)
    code_t = ((row_t >> 4) - (lane_t >> 4)) & 3
    spread_t = [
        [jnp.where((code_t == d) & ((lane_t >> 6) == blk), 1.0, 0.0).astype(BF16) for d in range(4)]
        for blk in range(2)
    ]
    lane16 = iota((16, 128), 1) >> 5
    for source_ref, other_ref, other_at, out_at, factor in (
        (gst_ref, qkv_ref, 0, width, scale),
        (lowt_ref, do_ref, 0, 2 * width, 1.0),
    ):
        for two in range(BLOCKS // 2):
            places = slice(128 * two, 128 * two + 128)
            for p in range(2):
                halves = [source_ref[128 * p + 64 * h : 128 * p + 64 * h + 64, places] for h in range(2)]
                for g in range(2):
                    c0 = 128 * (2 * p + g)
                    parts = []
                    for blk in range(2):
                        for hh in range(4):
                            half, ab = hh & 1, hh >> 1
                            d = (g + 2 * ab + half) & 3
                            parts.append(halves[half] * spread_t[blk][d])
                    wide = dot_nn(
                        jnp.concatenate(parts, axis=0), other_ref[places, other_at + c0 : other_at + c0 + 128]
                    )
                    for blk in range(2):
                        for w in range(4):
                            pieces = []
                            for hh in range(4):
                                half, ab = hh & 1, hh >> 1
                                slot = (w + half + g + 2 * ab) & 3
                                at = 256 * blk + 64 * hh + 16 * slot
                                pieces.append(wide[at : at + 16, :])
                            total = jnp.where(
                                lane16 == 0,
                                pieces[0],
                                jnp.where(lane16 == 1, pieces[1], jnp.where(lane16 == 2, pieces[2], pieces[3])),
                            )
                            at = 128 * two + 64 * blk + 16 * w
                            gqw_ref[at : at + 16, out_at + c0 : out_at + c0 + 128] = (total * factor).astype(BF16)
    fill_perm(perm_ref, s, u, False)
    for c in range(3):
        cols = slice(c * width, (c + 1) * width)
        gqn_ref[:, cols] = dot_nn(perm_ref[...], gqw_ref[:, cols]).astype(BF16)


def project_back_kernel(
    relative, gqn_ref, tok_ref, w_ref, small_in_ref, gpos_a_ref, gpos_b_ref, *refs
):
    *send_refs, acc_ref, norm_ref, small_ref, sum_ref, scratch_ref, column_ref = refs
    width = tok_ref.shape[1]
    step = pl.program_id(0)

    @pl.when(step == 0)
    def _():
        acc_ref[...] = jnp.zeros_like(acc_ref)
        sum_ref[...] = jnp.zeros_like(sum_ref)
        small_ref[...] = jnp.zeros_like(small_ref)
        small_ref[:16, :] = small_in_ref[...]

    tile = tok_ref.shape[0]
    half = width // 2

    def norm_rows(r):
        rows = slice(r, r + ROWS)
        normed, _ = norm_stats(tok_ref[rows, :].astype(F32))
        norm_ref[rows, :] = normed.astype(BF16)

    def column_sums(c):
        total = jnp.zeros((8, 128), F32)
        for r in range(0, tile, 64):
            part = gqn_ref[r : r + 64, c : c + 128].astype(F32)
            total = total + jnp.sum(part.reshape(8, 8, 128), 0)
        sum_ref[0:1, c : c + 128] += jnp.sum(total, 0, keepdims=True)

    def product(m, n):
        acc_ref[m : m + half, n : n + half] += dot_tn(norm_ref[:, m : m + half], gqn_ref[:, n : n + half])

    weave([], [functools.partial(norm_rows, r) for r in range(0, tile, ROWS)])
    weave(
        [functools.partial(product, m, n) for n in range(0, 3 * width, half) for m in (0, half)],
        [functools.partial(column_sums, c) for c in range(0, 3 * width, 128)],
    )

    @pl.when(step == pl.num_programs(0) - 1)
    def _():
        small_ref[2:3, :] = sum_ref[0:1, :width]
        small_ref[3:4, :] = sum_ref[0:1, 2 * width :]
        bias = small_ref[8:16, :].astype(BF16)
        flat = dot_nt(bias, mix_matrix())
        for q in range(4):
            small_ref[8 + q : 9 + q, :] = jnp.concatenate(
                [flat[c : c + 1, 128 * q : 128 * q + 128] for c in range(4)], axis=1
            )
        table = table_rows(gpos_a_ref[...] + gpos_b_ref[...], scratch_ref)
        extra = jnp.concatenate([jnp.zeros((UNIT, 16), F32), table, jnp.zeros((UNIT, 48), F32)], axis=1)
        column_ref[...] = jnp.transpose(small_ref[...])
        lane = iota((UNIT, 128), 1)
        for place in range(SHARDS):
            rows = block_rows(place, relative)
            weight = w_ref[rows, : 3 * width].astype(F32)
            gain = w_ref[rows, 3 * width : 3 * width + 1].astype(F32)
            bias = w_ref[rows, 3 * width + 1 : 3 * width + 2].astype(F32)
            product = acc_ref[rows, :]
            total = sum_ref[0:1, :]
            g_gain = jnp.sum(product * weight, 1, keepdims=True)
            g_bias = jnp.sum(total * weight, 1, keepdims=True)
            tail = jnp.where(lane == 0, g_gain, jnp.where(lane == 1, g_bias, column_ref[rows, :] + extra))
            block = jnp.concatenate([gain * product + bias * total, tail], axis=1)
            put_block(send_refs, place, block.astype(BF16))


def token_back_kernel(gqn_ref, tok_ref, gmid_ref, w_ref, vec_ref, gtok_ref, *gact_refs):
    tile, width = tok_ref.shape
    half = tile // 2

    def product(h, n):
        rows = slice(h * half, (h + 1) * half)
        gact_refs[h][:, n : n + half] = dot_nt(gqn_ref[rows, :], w_ref[n : n + half, : 3 * width])

    def back_rows(h, r):
        rows = slice(h * half + r, h * half + r + ROWS)
        normed, inv = norm_stats(tok_ref[rows, :].astype(F32))
        g_act = gact_refs[h][r : r + ROWS, :]
        gtok_ref[rows, :] = gmid_ref[rows, :] + norm_back(g_act, normed, inv, vec_ref[0:1, :])

    steps = [[functools.partial(back_rows, h, r) for r in range(0, half, ROWS)] for h in range(2)]
    products = [[functools.partial(product, h, n) for n in range(0, width, half)] for h in range(2)]
    weave(products[0], [])
    weave(products[1], steps[0])
    weave([], steps[1])


def output_kernel(*refs):
    gelu_refs, (ctx_ref, tok_ref, wp_ref, wd_ref, vec_ref, out_ref) = refs[:4], refs[4:]
    tile, width = tok_ref.shape
    half = width // 2
    bias = vec_ref[6:7, :] + vec_ref[7:8, :]
    for n in (0, half):
        cols = slice(n, n + half)
        for m in range(0, tile, half):
            rows = slice(m, m + half)
            gelu = jnp.concatenate([ref[rows, :] for ref in gelu_refs], axis=1)
            total = dot_nn(gelu, wd_ref[:, cols]) + dot_nn(ctx_ref[rows, :], wp_ref[:, cols])
            out_ref[rows, cols] = (total + tok_ref[rows, cols].astype(F32) + bias[:, cols]).astype(BF16)


SMEM_SPEC = pl.BlockSpec(memory_space=pltpu.SMEM)
ANY_SPEC = pl.BlockSpec(memory_space=pl.ANY)


def rows_spec(rows, cols):
    return pl.BlockSpec((rows, cols), lambda i: (i, 0))


def whole_spec(shape):
    return pl.BlockSpec(shape, lambda i: (0,) * len(shape))


def struct(shape, dtype):
    return jax.ShapeDtypeStruct(shape, dtype)


def cost(flops, nbytes):
    return pl.CostEstimate(flops=flops, bytes_accessed=nbytes, transcendentals=0)


def params():
    return pltpu.CompilerParams(vmem_limit_bytes=VMEM_BYTES, dimension_semantics=("arbitrary",))


def clip_spec(cols, start):
    return pl.BlockSpec((PATCHES, cols), lambda i: (i + start, 0))


def attend(shifts, counts, tokens, table, pieces, masks):
    n, width = tokens.shape
    cols = 3 * width + 128
    return pl.pallas_call(
        functools.partial(attend_kernel, masks),
        grid=(n // PATCHES,),
        in_specs=[SMEM_SPEC, SMEM_SPEC, rows_spec(PATCHES, width), whole_spec(table.shape)] + [ANY_SPEC] * len(pieces),
        out_specs=[
            rows_spec(PATCHES, 3 * width), rows_spec(PATCHES, 256), rows_spec(PATCHES, width),
            whole_spec((width, cols)), whole_spec((16, width)),
        ],
        out_shape=[
            struct((n, 3 * width), BF16), struct((n, 256), F32), struct((n, width), BF16),
            struct((width, cols), BF16), struct((16, width), F32),
        ],
        scratch_shapes=[
            pltpu.VMEM((PATCHES, PATCHES), BF16),
            pltpu.VMEM((PATCHES, width), F32),
            pltpu.VMEM((PATCHES, width), BF16),
            pltpu.VMEM((PATCHES, 256), F32),
            pltpu.VMEM((PATCHES, 256), BF16),
            pltpu.VMEM((PATCHES, width), BF16),
            pltpu.VMEM((BLOCK, 256), F32),
            pltpu.VMEM((PATCHES, 256), F32),
            *[pltpu.VMEM((PATCHES, 384), BF16)] * 2,
            pltpu.SemaphoreType.DMA((SHARDS,)),
        ],
        compiler_params=params(),
        cost_estimate=cost(2800000000, n * width),
        name="attend",
    )(shifts, counts, tokens, table, *pieces)


def send_shapes(cols, relative):
    rows = SHARDS * UNIT
    return [struct((rows // 2, cols), BF16)] * 2 if relative else [struct((rows, cols), BF16)]


def mlp(tokens, ctx, cot, vec, pieces, masks, relative, tile=512):
    n, width = tokens.shape
    cols = 9 * width
    ff = 4 * width
    sends = send_shapes(cols, relative)
    return pl.pallas_call(
        functools.partial(mlp_kernel, masks, relative),
        grid=(n // tile,),
        in_specs=[rows_spec(tile, width)] * 3 + [whole_spec(vec.shape)] + [ANY_SPEC] * len(pieces),
        out_specs=[rows_spec(tile, width)] * 6
        + [whole_spec((16, width)), ANY_SPEC, ANY_SPEC]
        + [whole_spec(x.shape) for x in sends],
        out_shape=[struct((n, width), BF16)] * 4
        + [
            struct((n, width), F32), struct((n, width), BF16),
            struct((16, width), F32), struct((width, width), BF16), struct((ff, width), BF16),
        ]
        + sends,
        scratch_shapes=[
            pltpu.VMEM((width, cols), BF16),
            pltpu.VMEM((ff, width), BF16),
            pltpu.VMEM((width, width), F32),
            pltpu.VMEM((width, ff), F32),
            pltpu.VMEM((ff, width), F32),
            pltpu.VMEM((tile, width), F32),
            pltpu.VMEM((tile, width), BF16),
            pltpu.VMEM((tile, width), BF16),
            pltpu.VMEM((tile, width), F32),
            *[pltpu.VMEM((tile, width), F32)] * 8,
            *[pltpu.VMEM((tile, width), BF16)] * 4,
            pltpu.SemaphoreType.DMA((SHARDS,)),
        ],
        compiler_params=params(),
        cost_estimate=cost(5000000000, n * width),
        name="mlp",
    )(tokens, ctx, cot, vec, *pieces)


def attend_back(shifts, qkv, prob, gctx, into, start, clips):
    n, width = gctx.shape

    def spec(cols):
        return pl.BlockSpec((PATCHES, cols), lambda i: (i + start, 0))

    return pl.pallas_call(
        functools.partial(attend_back_kernel, start),
        grid=(clips,),
        in_specs=[SMEM_SPEC, spec(3 * width), spec(256), spec(width), ANY_SPEC],
        out_specs=[spec(3 * width), whole_spec((BLOCK, 256))],
        out_shape=[struct((n, 3 * width), BF16), struct((BLOCK, 256), F32)],
        scratch_shapes=[
            pltpu.VMEM((PATCHES, PATCHES), BF16),
            pltpu.VMEM((PATCHES, width), BF16),
            pltpu.VMEM((PATCHES, 256), F32),
            pltpu.VMEM((PATCHES, 256), BF16),
            pltpu.VMEM((PATCHES, 256), BF16),
            pltpu.VMEM((256, PATCHES), BF16),
            pltpu.VMEM((256, PATCHES), BF16),
            pltpu.VMEM((PATCHES, 3 * width), BF16),
            pltpu.VMEM((PATCHES, 256), F32),
            *[pltpu.VMEM((PATCHES, 256), BF16)] * 2,
        ],
        input_output_aliases={} if into is None else {4: 0},
        compiler_params=params(),
        cost_estimate=cost(700000000 * clips, n * width),
        name="attend_back",
    )(shifts, qkv, prob, gctx, prob if into is None else into)


def project_back(gqn, tokens, w_qkv, small, gpos_a, gpos_b, relative, tile=512):
    n, width = tokens.shape
    sends = send_shapes(w_qkv.shape[1], relative)
    return pl.pallas_call(
        functools.partial(project_back_kernel, relative),
        grid=(n // tile,),
        in_specs=[rows_spec(tile, 3 * width), rows_spec(tile, width)]
        + [whole_spec(x.shape) for x in (w_qkv, small, gpos_a, gpos_b)],
        out_specs=[whole_spec(x.shape) for x in sends],
        out_shape=sends,
        scratch_shapes=[
            pltpu.VMEM((width, 3 * width), F32),
            pltpu.VMEM((tile, width), BF16),
            pltpu.VMEM((128, width), F32),
            pltpu.VMEM((8, 3 * width), F32),
            pltpu.VMEM((64, 256), F32),
            pltpu.VMEM((width, 128), F32),
        ],
        compiler_params=params(),
        cost_estimate=cost(1000000000, n * width),
        name="project_back",
    )(gqn, tokens, w_qkv, small, gpos_a, gpos_b)


def token_back(gqn, tokens, gmid, w_qkv, vec, tile=512):
    n, width = tokens.shape
    return pl.pallas_call(
        token_back_kernel,
        grid=(n // tile,),
        in_specs=[rows_spec(tile, 3 * width), rows_spec(tile, width), rows_spec(tile, width)]
        + [whole_spec(w_qkv.shape), whole_spec(vec.shape)],
        out_specs=rows_spec(tile, width),
        out_shape=struct((n, width), F32),
        scratch_shapes=[pltpu.VMEM((tile // 2, width), F32)] * 2,
        compiler_params=params(),
        cost_estimate=cost(1000000000, n * width),
        name="token_back",
    )(gqn, tokens, gmid, w_qkv, vec)


def output(gelu, ctx, tokens, wp, wd, vec, tile=512):
    n, width = tokens.shape
    return pl.pallas_call(
        output_kernel,
        grid=(n // tile,),
        in_specs=[rows_spec(tile, width)] * 6
        + [whole_spec(x.shape) for x in (wp, wd, vec)],
        out_specs=rows_spec(tile, width),
        out_shape=struct((n, width), BF16),
        compiler_params=params(),
        cost_estimate=cost(1000000000, n * width),
        name="output",
    )(*gelu, ctx, tokens, wp, wd, vec)


def finish_kernel(*refs):
    first, second = refs[:4], refs[4:8]
    gqkv_ref, gproj_ref, gup_ref, gdown_ref, *vector_refs, table_ref = refs[8:]
    width = gproj_ref.shape[1]

    def total(parts, cols):
        a, b, c, d = (part[:, cols].astype(F32) for part in parts)
        return (a + b) + (c + d)

    gqkv_ref[...] = total(first, slice(0, 3 * width))
    gproj_ref[...] = total(second, slice(0, width))
    gup_ref[...] = total(second, slice(width, 5 * width))
    for q in range(4):
        gdown_ref[UNIT * q : UNIT * q + UNIT, :] = total(second, slice((5 + q) * width, (6 + q) * width))
    extra = total(first, slice(3 * width, 3 * width + 128))
    rows = jnp.transpose(extra)
    for i in range(8):
        vector_refs[i][...] = rows[i, :]
    vector_refs[8][...] = jnp.concatenate([rows[8 + q : 9 + q, :] for q in range(4)], axis=1)[0]
    table_ref[...] = extra[:, 16 : 16 + RELS]


def finish(first, second):
    width = second[0].shape[1] // 9
    return pl.pallas_call(
        finish_kernel,
        out_shape=[
            struct((UNIT, 3 * width), F32), struct((UNIT, width), F32), struct((UNIT, 4 * width), F32),
            struct((4 * UNIT, width), F32),
            *[struct((UNIT,), F32)] * 8, struct((4 * UNIT,), F32), struct((HEADS, RELS), F32),
        ],
        compiler_params=pltpu.CompilerParams(vmem_limit_bytes=VMEM_BYTES),
        name="finish",
    )(*first, *second)


def exchange(x, mask):
    size = lax.axis_size(AXES)
    return lax.ppermute(x, AXES, [(i, i ^ mask) for i in range(size)])


def spread_far(block, masks):
    return [block] + [exchange(block, m) for m in masks]


def spread_core(pieces):
    return pieces + [exchange(x, CORE[0]) for x in pieces]


def piece_masks(near, far, start):
    return tuple((start, tuple(n ^ f ^ core for n in (0,) + near)) for core in (0,) + CORE for f in (0,) + far)


def add(*parts):
    parts = [p.astype(F32) for p in parts]
    while len(parts) > 1:
        parts = [parts[i] + parts[i + 1] for i in range(0, len(parts), 2)]
    return parts[0].astype(BF16)


def meet_core(keep, send):
    got = exchange(send, CORE[0])
    quarter = keep.shape[0] // 4
    return [add(keep[quarter * k : quarter * (k + 1)], got[quarter * k : quarter * (k + 1)]) for k in range(4)]


def meet_far(groups, masks):
    return [groups[0]] + [exchange(group, mask) for group, mask in zip(groups[1:], masks)]


def add_blocks(parts):
    return [add(*[p[UNIT * k : UNIT * (k + 1)] for p in parts]) for k in range(4)]


def gather(x):
    return lax.all_gather(x, AXES, axis=0, tiled=True)


def scatter(x):
    return lax.psum_scatter(x, AXES, scatter_dimension=0, tiled=True)


def by_unit(x):
    return jnp.moveaxis(x.reshape((SHARDS, 4, UNIT) + x.shape[1:]), 1, 2).reshape((SHARDS * UNIT, 4) + x.shape[1:])


def by_row(x):
    return jnp.moveaxis(x.reshape((SHARDS, UNIT, 4) + x.shape[2:]), 2, 1).reshape((4 * SHARDS * UNIT,) + x.shape[2:])


def whole_weights(vectors, weights):
    columns = [gather(v)[:, None] for v in vectors[:8]] + [by_unit(gather(vectors[8]))]
    extra = jnp.concatenate(columns, axis=1)
    qkv, proj, up, down = (gather(w) for w in weights)
    first = jnp.concatenate([qkv, extra, jnp.zeros((qkv.shape[0], 128 - extra.shape[1]), BF16)], axis=1)
    second = jnp.concatenate([proj, up, by_unit(down).reshape(proj.shape[0], -1)], axis=1)
    return first, second


def whole_grads(first, second):
    width = second.shape[1] // 9
    mats = [first[:, : 3 * width], second[:, :width], second[:, width : 5 * width]]
    mats.append(by_row(second[:, 5 * width :].reshape(-1, 4, width)))
    extra = first[:, 3 * width :]
    vectors = [extra[:, k] for k in range(8)] + [by_row(extra[:, 8:12])]
    table = lax.psum(extra[:UNIT, 16 : 16 + RELS].astype(F32), AXES).T
    return [scatter(x).astype(F32) for x in mats] + [scatter(x.astype(F32)) for x in vectors] + [table]


def local_test(
    tokens, cotangent, counts, shifts, qkv, proj, up, down, vec1, vec2, ub, table,
):
    shifts, table = shifts.T, table.T
    extra = jnp.concatenate([vec1, vec2], axis=0).T
    extra = jnp.concatenate([extra, by_unit(ub[0]), jnp.zeros((512, 116))], axis=1).astype(BF16)
    first = jnp.concatenate([qkv, extra], axis=1)
    second = jnp.concatenate([proj, up, by_unit(down).reshape(512, -1)], axis=1)
    q, prob, ctx, w_qkv, vec = attend(shifts, counts, tokens, table, [first], None)
    *gelu, gmid, gctx, small, wp, wd, gsecond = mlp(tokens, ctx, cotangent, vec, [second], None, False)
    gqn, gpos_a = attend_back(shifts, q, prob, gctx, None, 0, 2)
    gqn, gpos_b = attend_back(shifts, q, prob, gctx, gqn, 2, 2)
    (gfirst,) = project_back(gqn, tokens, w_qkv, small, gpos_a, gpos_b, False)
    gtok = token_back(gqn, tokens, gmid, w_qkv, vec)
    out = output(gelu, ctx, tokens, wp, wd, vec)
    width = 512
    e = gfirst[:, 1536:]
    mats = [gfirst[:, :1536], gsecond[:, :width], gsecond[:, width : 5 * width], by_row(gsecond[:, 5 * width :].reshape(-1, 4, width))]
    v = [e[:, k] for k in range(8)]
    return [out, gtok] + mats + [v[0], v[1], v[4], v[5], v[2], v[3], v[6], by_row(e[:, 8:12]), v[7], e[:16, 16:65].T]


def on_device(
    tokens, cotangent, counts, shifts, qkv_weight, proj_weight, up_weight, down_weight,
    first_gain, first_bias, second_gain, second_bias, query_bias, value_bias, proj_bias, up_bias, down_bias,
    rel_table,
):
    shifts, rel_table = shifts.T, rel_table.T
    vectors = [first_gain, first_bias, query_bias, value_bias, second_gain, second_bias, proj_bias, down_bias, up_bias]
    weights = [qkv_weight, proj_weight, up_weight, down_weight]
    stepped = lax.axis_size(AXES) == SHARDS
    if stepped:
        first, second = pack(vectors, weights)
        masks = piece_masks(COLUMN, PLANE, 0)
        first = spread_far(first, COLUMN)
        second = spread_far(second, COLUMN)
        first = spread_far(jnp.concatenate(first), PLANE)
        first, second = lax.optimization_barrier((first, second))
        first, second = lax.optimization_barrier((spread_core(first), jnp.concatenate(second)))
        second = spread_far(second, PLANE)
    else:
        first, second = ([x] for x in whole_weights(vectors, weights))
        masks = None
    clips = counts.shape[0]
    qkv, prob, ctx, w_qkv, vec = attend(shifts, counts, tokens, rel_table, first, masks)
    if stepped:
        ctx, far = lax.optimization_barrier((ctx, second[1:]))
        second = spread_core(second[:1] + list(far))
    parts = mlp(tokens, ctx, cotangent, vec, second, masks, stepped)
    gelu, (gmid, gctx, small, wp, wd), gsecond = parts[:4], parts[4:9], parts[9:]
    half = max(1, clips // 4)
    gqn, gpos_a = attend_back(shifts, qkv, prob, gctx, None, 0, half)
    if stepped:
        gsecond = meet_core(*gsecond)
        gqn, gsecond = lax.optimization_barrier((gqn, gsecond))
        gsecond = meet_far(gsecond, PLANE)
    gqn, gpos_b = attend_back(shifts, qkv, prob, gctx, gqn, half, clips - half)
    gfirst = project_back(gqn, tokens, w_qkv, small, gpos_a, gpos_b, stepped)
    if stepped:
        gfirst, gsecond = lax.optimization_barrier((gfirst, gsecond))
        gsecond = meet_far(add_blocks(gsecond), COLUMN)
        gfirst = meet_core(*gfirst)
        gfirst, gqn = lax.optimization_barrier((gfirst, gqn))
        gfirst = meet_far(gfirst, PLANE)
    gtok = token_back(gqn, tokens, gmid, w_qkv, vec)
    if stepped:
        gfirst, gtok, gelu = lax.optimization_barrier((gfirst, gtok, gelu))
        gfirst = meet_far(add_blocks(gfirst), COLUMN)
    out = output(gelu, ctx, tokens, wp, wd, vec)
    if stepped:
        gfirst, gsecond, out = lax.optimization_barrier((gfirst, gsecond, out))
        grads = finish(gfirst, gsecond)
        grads = (*grads[:13], grads[13].T)
    else:
        grads = whole_grads(gfirst[0], gsecond[0])
    mats, vecs, table = grads[:4], grads[4:13], grads[13]
    return (
        out, gtok, *mats, vecs[0], vecs[1], vecs[4], vecs[5], vecs[2], vecs[3], vecs[6], vecs[8], vecs[7], table,
    )


def solution(mesh):
    sharded = P(AXES, None)
    line = P(AXES)
    in_specs = (sharded, sharded, line, sharded) + (sharded,) * 4 + (line,) * 9 + (P(),)
    out_specs = (sharded,) * 6 + (line,) * 9 + (P(),)
    return jax.shard_map(on_device, mesh=mesh, in_specs=in_specs, out_specs=out_specs, check_vma=False)
```

profile of v0, /device:TPU:0, one launch (start us, length us, event | category | flops | bytes accessed | tf_op | source)
XLA Modules:
  0.0 188.3 jit_solution(6846477197989084996)
XLA Ops:
  0.7 1.8 pack.1
  2.4 5.0 %collective-permute-start.2 = (bf16[16,1664]{1,0:T(8,128)(2,1)}, bf16[16,1664]{1,0:T(8,128)(2,1)S(1)}, u32[]{:S(2)}, u32[]{:S(2)}) collective-permute-start(bf16[16,1664]{1,0:T(8,128)(2,1)} %get-tuple-element.109), channel_id=1, source_target_pairs={{0,24},{1,25},{2,26},{3,27},{4,28},{5,29},{6,30},{7,31},{8,16},{9,... | collective-permute-start | bytes 159752 | tf_op jit(solution)/shard_map/ppermute | solution.py:974
  7.5 0.6 collective-permute-start
  8.1 3.8 %collective-permute-start.8 = (bf16[16,4608]{1,0:T(8,128)(2,1)}, bf16[16,4608]{1,0:T(8,128)(2,1)S(1)}, u32[]{:S(2)}, u32[]{:S(2)}) collective-permute-start(bf16[16,4608]{1,0:T(8,128)(2,1)} %get-tuple-element.115), channel_id=1, source_target_pairs={{0,24},{1,25},{2,26},{3,27},{4,28},{5,29},{6,30},{7,31},{8,16},{9,... | collective-permute-start | bytes 442376 | tf_op jit(solution)/shard_map/ppermute | solution.py:974
  11.9 0.8 constant_dynamic-update-slice_fusion.3
  12.7 3.8 %collective-permute-done.1 = bf16[16,1664]{1,0:T(8,128)(2,1)S(1)} collective-permute-done((bf16[16,1664]{1,0:T(8,128)(2,1)}, bf16[16,1664]{1,0:T(8,128)(2,1)S(1)}, u32[]{:S(2)}, u32[]{:S(2)}) %collective-permute-start.1) | collective-permute-done | bytes 53280 | tf_op jit(solution)/shard_map/ppermute | solution.py:974
  16.5 2.5 %collective-permute-start.5 = (bf16[64,1664]{1,0:T(8,128)(2,1)S(1)}, bf16[64,1664]{1,0:T(8,128)(2,1)S(1)}, u32[]{:S(2)}, u32[]{:S(2)}) collective-permute-start(bf16[64,1664]{1,0:T(8,128)(2,1)S(1)} %constant_dynamic-update-slice_fusion.refs_0_), channel_id=1, source_target_pairs={{0,5},{1,4},{2,7},{3,6},{4,1},{5,0},{6,3},{7,2},{8,13},{9,12},{10,... | collective-permute-start | bytes 638984 | tf_op jit(solution)/shard_map/ppermute | solution.py:974
  19.1 0.5 collective-permute-start.4
  19.6 0.5 collective-permute-start.3
  20.1 1.3 collective-permute-start.6
  21.4 5.0 %collective-permute-done.7 = bf16[16,4608]{1,0:T(8,128)(2,1)S(1)} collective-permute-done((bf16[16,4608]{1,0:T(8,128)(2,1)}, bf16[16,4608]{1,0:T(8,128)(2,1)S(1)}, u32[]{:S(2)}, u32[]{:S(2)}) %collective-permute-start.7) | collective-permute-done | bytes 147488 | tf_op jit(solution)/shard_map/ppermute | solution.py:974
  26.5 0.6 collective-permute-done.6
  27.2 0.5 collective-permute-start.10
  28.2 0.9 pad_maximum_fusion.refs_0_
  29.9 0.7 copy-done.21
  30.6 2.4 %collective-permute-start.15 = (bf16[64,4608]{1,0:T(8,128)(2,1)S(1)}, bf16[64,4608]{1,0:T(8,128)(2,1)S(1)}, u32[]{:S(2)}, u32[]{:S(2)}) collective-permute-start(bf16[64,4608]{1,0:T(8,128)(2,1)S(1)} %pad_maximum_fusion.refs_0_), channel_id=1, source_target_pairs={{0,5},{1,4},{2,7},{3,6},{4,1},{5,0},{6,3},{7,2},{8,13},{9,12},{10,... | collective-permute-start | bytes 1769480 | tf_op jit(solution)/shard_map/ppermute | solution.py:974
  33.0 0.5 collective-permute-start.14
  33.5 0.5 collective-permute-start.13
  34.1 20.9 %attend.1 = (bf16[2048,1536]{1,0:T(8,128)(2,1)}, f32[2048,256]{1,0:T(8,128)}, bf16[2048,512]{1,0:T(8,128)(2,1)}, bf16[512,1664]{1,0:T(8,128)(2,1)}, f32[16,512]{1,0:T(8,128)}) custom-call(s32[2,4]{1,0:T(2,128)} %bitcast.3, s32[4]{0:T(128)} %count_ref.1, bf16[2048,512]{1,0:T(8,128)(2,1)} %refs_5_.3, bf16[16,49]{1,0:T(8,128)(2,1)} %bitcast.7, ...), custom_call_target="tpu_custom_call" | custom-call | flops 2800000000 | bytes 1048576 | tf_op jit(solution)/shard_map/attend/pallas_call | solution.py:777
  55.1 4.4 %collective-permute-done.14.refs_2_ = bf16[64,4608]{1,0:T(8,128)(2,1)S(1)} collective-permute-done((bf16[64,4608]{1,0:T(8,128)(2,1)S(1)}, bf16[64,4608]{1,0:T(8,128)(2,1)S(1)}, u32[]{:S(2)}, u32[]{:S(2)}) %collective-permute-start.14) | collective-permute-done | bytes 589856 | tf_op jit(solution)/shard_map/ppermute | solution.py:974
  59.5 0.5 collective-permute-start.18
  60.1 1.4 collective-permute-done.17.refs_5_
  61.6 0.8 collective-permute-done.18.refs_6_
  62.4 0.8 collective-permute-done.19.refs_7_
  63.2 0.8 copy-done.15
  64.1 41.5 %mlp.1 = (bf16[2048,512]{1,0:T(8,128)(2,1)}, bf16[2048,512]{1,0:T(8,128)(2,1)}, bf16[2048,512]{1,0:T(8,128)(2,1)}, bf16[2048,512]{1,0:T(8,128)(2,1)}, f32[2048,5...) custom-call(bf16[2048,512]{1,0:T(8,128)(2,1)} %refs_5_.3, ...), custom_call_target="tpu_custom_call" | custom-call | flops 5000000000 | bytes 1048576 | tf_op jit(solution)/shard_map/mlp/pallas_call | solution.py:817
  105.8 7.5 %attend_back.2 = (bf16[2048,1536]{1,0:T(8,128)(2,1)}, f32[64,256]{1,0:T(8,128)}) custom-call(s32[2,4]{1,0:T(2,128)} %bitcast.4, bf16[2048,1536]{1,0:T(8,128)(2,1)} %get-tuple-element.127.qkv_ref, f32[2048,256]{1,0:T(8,128)} %get-tuple-element.128.prob_ref._, bf16[2048,512]{1,0:T(8,128)(2,1)} %get-tuple-element.136.gctx_ref, ...), custom_call_target="tpu_custom_call" | custom-call | flops 700000000 | bytes 1048576 | tf_op jit(solution)/shard_map/attend_back/pallas_call | solution.py:856
  113.3 3.0 %add_convert_fusion = (bf16[64,4608]{1,0:T(8,128)(2,1)S(1)}, bf16[64,4608]{1,0:T(8,128)(2,1)S(1)}, bf16[64,4608]{1,0:T(8,128)(2,1)}, bf16[64,4608]{1,0:T(8,128)(2,1)S(1)}) fusion(bf16[256,4608]{1,0:T(8,128)(2,1)} %collective-permute-done.20, bf16[256,4608]{1,0:T(8,128)(2,1)S(1)} %copy-done), kind=kLoop, calls=%fused_computation | loop fusion | flops 4718592 | bytes 7077888 | tf_op jit(solution)/shard_map/convert_element_type | solution.py:993
  116.3 1.5 collective-permute-start.21
  117.8 0.8 collective-permute-start.22
  118.6 1.2 collective-permute-start.23
  119.8 16.3 %attend_back.3 = (bf16[2048,1536]{1,0:T(8,128)(2,1)}, f32[64,256]{1,0:T(8,128)}) custom-call(s32[2,4]{1,0:T(2,128)} %bitcast.5, bf16[2048,1536]{1,0:T(8,128)(2,1)} %get-tuple-element.127.qkv_ref, f32[2048,256]{1,0:T(8,128)} %get-tuple-element.128.prob_ref._, bf16[2048,512]{1,0:T(8,128)(2,1)} %get-tuple-element.136.gctx_ref, ...), custom_call_target="tpu_custom_call", output_to_operand_aliasing={{0}: (4, {})} | custom-call | flops 2100000000 | bytes 1048576 | tf_op jit(solution)/shard_map/attend_back/pallas_call | solution.py:856
  136.1 10.9 %project_back.1 = (bf16[256,1664]{1,0:T(8,128)(2,1)}, bf16[256,1664]{1,0:T(8,128)(2,1)}) custom-call(bf16[2048,1536]{1,0:T(8,128)(2,1)} %get-tuple-element.158.gqn_ref, bf16[2048,512]{1,0:T(8,128)(2,1)} %refs_5_.3, bf16[512,1664]{1,0:T(8,128)(2,1)} %get-tuple-element.142.w_ref, f32[16,512]{1,0:T(8,128)} %get-tuple-element.143.small_in_ref, ...), custom_call_target="tpu_custom_call" | custom-call | flops 1000000000 | bytes 1048576 | tf_op jit(solution)/shard_map/project_back/pallas_call | solution.py:884
  147.1 2.6 %collective-permute-done.24 = bf16[256,1664]{1,0:T(8,128)(2,1)S(1)} collective-permute-done((bf16[256,1664]{1,0:T(8,128)(2,1)}, bf16[256,1664]{1,0:T(8,128)(2,1)S(1)}, u32[]{:S(2)}, u32[]{:S(2)}) %collective-permute-start.24) | collective-permute-done | bytes 852000 | tf_op jit(solution)/shard_map/ppermute | solution.py:974
  149.7 1.4 add_convert_fusion.4
  151.2 1.6 collective-permute-start.25
  152.7 0.8 collective-permute-start.26
  153.5 1.2 collective-permute-start.27
  154.7 1.0 add_convert_fusion.8
  155.7 2.3 %collective-permute-start.33 = (bf16[16,4608]{1,0:T(8,128)(2,1)}, bf16[16,4608]{1,0:T(8,128)(2,1)S(1)}, u32[]{:S(2)}, u32[]{:S(2)}) collective-permute-start(bf16[16,4608]{1,0:T(8,128)(2,1)} %get-tuple-element.206), channel_id=1, source_target_pairs={{0,24},{1,25},{2,26},{3,27},{4,28},{5,29},{6,30},{7,31},{8,16},{9,... | collective-permute-start | bytes 442376 | tf_op jit(solution)/shard_map/ppermute | solution.py:974
  158.0 9.7 %token_back.1 = f32[2048,512]{1,0:T(8,128)} custom-call(bf16[2048,1536]{1,0:T(8,128)(2,1)} %get-tuple-element.158.gqn_ref, bf16[2048,512]{1,0:T(8,128)(2,1)} %refs_5_.3, f32[2048,512]{1,0:T(8,128)} %get-tuple-element.159.gmid_ref, bf16[512,1664]{1,0:T(8,128)(2,1)} %get-tuple-element.142.w_ref, f32[16,512]{1,0:T(8,128)} %get-tuple-element.132.vec_ref.refs_8_), custom_call_target="tpu_custom_call" | custom-call | flops 1000000000 | bytes 1048576 | tf_op jit(solution)/shard_map/token_back/pallas_call | solution.py:907
  167.6 2.1 %collective-permute-start.31 = (bf16[16,4608]{1,0:T(8,128)(2,1)S(1)}, bf16[16,4608]{1,0:T(8,128)(2,1)S(1)}, u32[]{:S(2)}, u32[]{:S(2)}) collective-permute-start(bf16[16,4608]{1,0:T(8,128)(2,1)S(1)} %get-tuple-element.208), channel_id=1, source_target_pairs={{0,8},{1,9},{2,10},{3,11},{4,12},{5,13},{6,14},{7,15},{8,0},{9,1},... | collective-permute-start | bytes 442376 | tf_op jit(solution)/shard_map/ppermute | solution.py:974
  169.8 0.7 add_convert_fusion.12
  170.5 2.3 %collective-permute-start.30 = (bf16[16,1664]{1,0:T(8,128)(2,1)S(1)}, bf16[16,1664]{1,0:T(8,128)(2,1)S(1)}, u32[]{:S(2)}, u32[]{:S(2)}) collective-permute-start(bf16[16,1664]{1,0:T(8,128)(2,1)S(1)} %get-tuple-element.214), channel_id=1, source_target_pairs={{0,24},{1,25},{2,26},{3,27},{4,28},{5,29},{6,30},{7,31},{8,16},{9,... | collective-permute-start | bytes 159752 | tf_op jit(solution)/shard_map/ppermute | solution.py:974
  172.8 2.1 %collective-permute-start.28 = (bf16[16,1664]{1,0:T(8,128)(2,1)S(1)}, bf16[16,1664]{1,0:T(8,128)(2,1)S(1)}, u32[]{:S(2)}, u32[]{:S(2)}) collective-permute-start(bf16[16,1664]{1,0:T(8,128)(2,1)S(1)} %get-tuple-element.216), channel_id=1, source_target_pairs={{0,8},{1,9},{2,10},{3,11},{4,12},{5,13},{6,14},{7,15},{8,0},{9,1},... | collective-permute-start | bytes 159752 | tf_op jit(solution)/shard_map/ppermute | solution.py:974
  174.9 10.3 %output.1 = bf16[2048,512]{1,0:T(8,128)(2,1)} custom-call(bf16[2048,512]{1,0:T(8,128)(2,1)} %get-tuple-element.172.refs_0_, bf16[2048,512]{1,0:T(8,128)(2,1)} %get-tuple-element.173.refs_1_, bf16[2048,512]{1,0:T(8,128)(2,1)} %get-tuple-element.174.refs_2_, bf16[2048,512]{1,0:T(8,128)(2,1)} %get-tuple-element.175.refs_3_, ...), custom_call_target="tpu_custom_call" | custom-call | flops 1000000000 | bytes 1048576 | tf_op jit(solution)/shard_map/output/pallas_call | solution.py:923
  185.3 0.6 copy-done.3
  186.0 2.1 %finish.1 = (f32[16,1536]{1,0:T(8,128)}, f32[16,512]{1,0:T(8,128)}, f32[16,2048]{1,0:T(8,128)}, f32[64,512]{1,0:T(8,128)}, f32[16]{0:T(128)}, /*index=5*/f32[16]...) custom-call(bf16[16,1664]{1,0:T(8,128)(2,1)} %get-tuple-element.180., ...), custom_call_target="tpu_custom_call" | custom-call | tf_op jit(solution)/shard_map/finish/pallas_call | solution.py:960
  (82 shorter events, 2.0 us)
Async XLA Ops:
  2.4 14.1 %collective-permute-start.2 = (bf16[16,1664]{1,0:T(8,128)(2,1)}, bf16[16,1664]{1,0:T(8,128)(2,1)S(1)}, u32[]{:S(2)}, u32[]{:S(2)}) collective-permute-start(bf16[16,1664]{1,0:T(8,128)(2,1)} %get-tuple-element.109), channel_id=1, source_target_pairs={{0,24},{1,25},{2,26},{3,27},{4,28},{5,29},{6,30},{7,31},{8,16},{9,... | collective-permute-start | bytes 159752 | tf_op jit(solution)/shard_map/ppermute | solution.py:974
  7.5 9.0 %collective-permute-start.1 = (bf16[16,1664]{1,0:T(8,128)(2,1)}, bf16[16,1664]{1,0:T(8,128)(2,1)S(1)}, u32[]{:S(2)}, u32[]{:S(2)}) collective-permute-start(bf16[16,1664]{1,0:T(8,128)(2,1)} %get-tuple-element.109), channel_id=1, source_target_pairs={{0,16},{1,17},{2,18},{3,19},{4,20},{5,21},{6,22},{7,23},{8,24},{9,... | collective-permute-start | bytes 159752 | tf_op jit(solution)/shard_map/ppermute | solution.py:974
  7.5 5.2 %collective-permute-start = (bf16[16,1664]{1,0:T(8,128)(2,1)}, bf16[16,1664]{1,0:T(8,128)(2,1)S(1)}, u32[]{:S(2)}, u32[]{:S(2)}) collective-permute-start(bf16[16,1664]{1,0:T(8,128)(2,1)} %get-tuple-element.109), channel_id=1, source_target_pairs={{0,8},{1,9},{2,10},{3,11},{4,12},{5,13},{6,14},{7,15},{8,0},{9,1},... | collective-permute-start | bytes 159752 | tf_op jit(solution)/shard_map/ppermute | solution.py:974
  8.1 12.0 %collective-permute-start.8 = (bf16[16,4608]{1,0:T(8,128)(2,1)}, bf16[16,4608]{1,0:T(8,128)(2,1)S(1)}, u32[]{:S(2)}, u32[]{:S(2)}) collective-permute-start(bf16[16,4608]{1,0:T(8,128)(2,1)} %get-tuple-element.115), channel_id=1, source_target_pairs={{0,24},{1,25},{2,26},{3,27},{4,28},{5,29},{6,30},{7,31},{8,16},{9,... | collective-permute-start | bytes 442376 | tf_op jit(solution)/shard_map/ppermute | solution.py:974
  16.5 17.6 %copy-start.8 = (bf16[64,1664]{1,0:T(8,128)(2,1)}, bf16[64,1664]{1,0:T(8,128)(2,1)S(1)}, u32[]{:S(2)}) copy-start(bf16[64,1664]{1,0:T(8,128)(2,1)S(1)} %constant_dynamic-update-slice_fusion.refs_0_) | copy-start | bytes 638980
  16.5 10.5 %collective-permute-start.5 = (bf16[64,1664]{1,0:T(8,128)(2,1)S(1)}, bf16[64,1664]{1,0:T(8,128)(2,1)S(1)}, u32[]{:S(2)}, u32[]{:S(2)}) collective-permute-start(bf16[64,1664]{1,0:T(8,128)(2,1)S(1)} %constant_dynamic-update-slice_fusion.refs_0_), channel_id=1, source_target_pairs={{0,5},{1,4},{2,7},{3,6},{4,1},{5,0},{6,3},{7,2},{8,13},{9,12},{10,... | collective-permute-start | bytes 638984 | tf_op jit(solution)/shard_map/ppermute | solution.py:974
  19.1 8.0 %collective-permute-start.4 = (bf16[64,1664]{1,0:T(8,128)(2,1)S(1)}, bf16[64,1664]{1,0:T(8,128)(2,1)S(1)}, u32[]{:S(2)}, u32[]{:S(2)}) collective-permute-start(bf16[64,1664]{1,0:T(8,128)(2,1)S(1)} %constant_dynamic-update-slice_fusion.refs_0_), channel_id=1, source_target_pairs={{0,1},{1,0},{2,3},{3,2},{4,5},{5,4},{6,7},{7,6},{8,9},{9,8},{10,11... | collective-permute-start | bytes 638984 | tf_op jit(solution)/shard_map/ppermute | solution.py:974
  19.6 7.5 %collective-permute-start.3 = (bf16[64,1664]{1,0:T(8,128)(2,1)S(1)}, bf16[64,1664]{1,0:T(8,128)(2,1)S(1)}, u32[]{:S(2)}, u32[]{:S(2)}) collective-permute-start(bf16[64,1664]{1,0:T(8,128)(2,1)S(1)} %constant_dynamic-update-slice_fusion.refs_0_), channel_id=1, source_target_pairs={{0,4},{1,5},{2,6},{3,7},{4,0},{5,1},{6,2},{7,3},{8,12},{9,13},{10,... | collective-permute-start | bytes 638984 | tf_op jit(solution)/shard_map/ppermute | solution.py:974
  20.1 6.4 %collective-permute-start.7 = (bf16[16,4608]{1,0:T(8,128)(2,1)}, bf16[16,4608]{1,0:T(8,128)(2,1)S(1)}, u32[]{:S(2)}, u32[]{:S(2)}) collective-permute-start(bf16[16,4608]{1,0:T(8,128)(2,1)} %get-tuple-element.115), channel_id=1, source_target_pairs={{0,16},{1,17},{2,18},{3,19},{4,20},{5,21},{6,22},{7,23},{8,24},{9,... | collective-permute-start | bytes 442376 | tf_op jit(solution)/shard_map/ppermute | solution.py:974
  20.1 6.9 %collective-permute-start.6 = (bf16[16,4608]{1,0:T(8,128)(2,1)}, bf16[16,4608]{1,0:T(8,128)(2,1)S(1)}, u32[]{:S(2)}, u32[]{:S(2)}) collective-permute-start(bf16[16,4608]{1,0:T(8,128)(2,1)} %get-tuple-element.115), channel_id=1, source_target_pairs={{0,8},{1,9},{2,10},{3,11},{4,12},{5,13},{6,14},{7,15},{8,0},{9,1},... | collective-permute-start | bytes 442376 | tf_op jit(solution)/shard_map/ppermute | solution.py:974
  27.0 7.0 %copy-start.16 = (bf16[64,1664]{1,0:T(8,128)(2,1)}, bf16[64,1664]{1,0:T(8,128)(2,1)S(1)}, u32[]{:S(2)}) copy-start(bf16[64,1664]{1,0:T(8,128)(2,1)S(1)} %collective-permute-done.5.refs_3_) | copy-start | bytes 638980
  27.1 7.0 %copy-start.17 = (bf16[64,1664]{1,0:T(8,128)(2,1)}, bf16[64,1664]{1,0:T(8,128)(2,1)S(1)}, u32[]{:S(2)}) copy-start(bf16[64,1664]{1,0:T(8,128)(2,1)S(1)} %collective-permute-done.4.refs_2_) | copy-start | bytes 638980
  27.1 7.0 %copy-start.18 = (bf16[64,1664]{1,0:T(8,128)(2,1)}, bf16[64,1664]{1,0:T(8,128)(2,1)S(1)}, u32[]{:S(2)}) copy-start(bf16[64,1664]{1,0:T(8,128)(2,1)S(1)} %collective-permute-done.3.refs_1_) | copy-start | bytes 638980
  27.1 2.1 %collective-permute-start.9 = (bf16[64,1664]{1,0:T(8,128)(2,1)S(1)}, bf16[64,1664]{1,0:T(8,128)(2,1)S(1)}, u32[]{:S(2)}, u32[]{:S(2)}) collective-permute-start(bf16[64,1664]{1,0:T(8,128)(2,1)S(1)} %constant_dynamic-update-slice_fusion.refs_0_), channel_id=1, source_target_pairs={{0,2},{1,3},{2,0},{3,1},{4,6},{5,7},{6,4},{7,5},{8,10},{9,11},{10,... | collective-permute-start | bytes 638984 | tf_op jit(solution)/shard_map/ppermute | solution.py:974
  27.2 2.0 %collective-permute-start.10 = (bf16[64,1664]{1,0:T(8,128)(2,1)S(1)}, bf16[64,1664]{1,0:T(8,128)(2,1)S(1)}, u32[]{:S(2)}, u32[]{:S(2)}) collective-permute-start(bf16[64,1664]{1,0:T(8,128)(2,1)S(1)} %collective-permute-done.3.refs_1_), channel_id=1, source_target_pairs={{0,2},{1,3},{2,0},{3,1},{4,6},{5,7},{6,4},{7,5},{8,10},{9,11},{10,... | collective-permute-start | bytes 638984 | tf_op jit(solution)/shard_map/ppermute | solution.py:974
  27.7 1.9 collective-permute-start.11
  27.7 2.9 %collective-permute-start.12 = (bf16[64,1664]{1,0:T(8,128)(2,1)S(1)}, bf16[64,1664]{1,0:T(8,128)(2,1)}, u32[]{:S(2)}, u32[]{:S(2)}) collective-permute-start(bf16[64,1664]{1,0:T(8,128)(2,1)S(1)} %collective-permute-done.5.refs_3_), channel_id=1, source_target_pairs={{0,2},{1,3},{2,0},{3,1},{4,6},{5,7},{6,4},{7,5},{8,10},{9,11},{10,... | collective-permute-start | bytes 638984 | tf_op jit(solution)/shard_map/ppermute | solution.py:974
  29.1 25.9 %copy-start.1 = (bf16[64,4608]{1,0:T(8,128)(2,1)}, bf16[64,4608]{1,0:T(8,128)(2,1)S(1)}, u32[]{:S(2)}) copy-start(bf16[64,4608]{1,0:T(8,128)(2,1)S(1)} %pad_maximum_fusion.refs_0_) | copy-start | bytes 1769476
  29.1 5.0 %copy-start.19 = (bf16[64,1664]{1,0:T(8,128)(2,1)}, bf16[64,1664]{1,0:T(8,128)(2,1)S(1)}, u32[]{:S(2)}) copy-start(bf16[64,1664]{1,0:T(8,128)(2,1)S(1)} %collective-permute-done.9.refs_4_) | copy-start | bytes 638980
  30.6 24.5 %collective-permute-start.15 = (bf16[64,4608]{1,0:T(8,128)(2,1)S(1)}, bf16[64,4608]{1,0:T(8,128)(2,1)S(1)}, u32[]{:S(2)}, u32[]{:S(2)}) collective-permute-start(bf16[64,4608]{1,0:T(8,128)(2,1)S(1)} %pad_maximum_fusion.refs_0_), channel_id=1, source_target_pairs={{0,5},{1,4},{2,7},{3,6},{4,1},{5,0},{6,3},{7,2},{8,13},{9,12},{10,... | collective-permute-start | bytes 1769480 | tf_op jit(solution)/shard_map/ppermute | solution.py:974
  33.0 26.4 %collective-permute-start.14 = (bf16[64,4608]{1,0:T(8,128)(2,1)S(1)}, bf16[64,4608]{1,0:T(8,128)(2,1)S(1)}, u32[]{:S(2)}, u32[]{:S(2)}) collective-permute-start(bf16[64,4608]{1,0:T(8,128)(2,1)S(1)} %pad_maximum_fusion.refs_0_), channel_id=1, source_target_pairs={{0,1},{1,0},{2,3},{3,2},{4,5},{5,4},{6,7},{7,6},{8,9},{9,8},{10,11... | collective-permute-start | bytes 1769480 | tf_op jit(solution)/shard_map/ppermute | solution.py:974
  33.5 26.0 %collective-permute-start.13 = (bf16[64,4608]{1,0:T(8,128)(2,1)S(1)}, bf16[64,4608]{1,0:T(8,128)(2,1)S(1)}, u32[]{:S(2)}, u32[]{:S(2)}) collective-permute-start(bf16[64,4608]{1,0:T(8,128)(2,1)S(1)} %pad_maximum_fusion.refs_0_), channel_id=1, source_target_pairs={{0,4},{1,5},{2,6},{3,7},{4,0},{5,1},{6,2},{7,3},{8,12},{9,13},{10,... | collective-permute-start | bytes 1769480 | tf_op jit(solution)/shard_map/ppermute | solution.py:974
  34.1 26.0 %collective-permute-start.16 = (bf16[64,4608]{1,0:T(8,128)(2,1)S(1)}, bf16[64,4608]{1,0:T(8,128)(2,1)S(1)}, u32[]{:S(2)}, u32[]{:S(2)}) collective-permute-start(bf16[64,4608]{1,0:T(8,128)(2,1)S(1)} %pad_maximum_fusion.refs_0_), channel_id=1, source_target_pairs={{0,2},{1,3},{2,0},{3,1},{4,6},{5,7},{6,4},{7,5},{8,10},{9,11},{10,... | collective-permute-start | bytes 1769480 | tf_op jit(solution)/shard_map/ppermute | solution.py:974
  55.1 9.0 %copy-start.9 = (bf16[64,4608]{1,0:T(8,128)(2,1)}, bf16[64,4608]{1,0:T(8,128)(2,1)S(1)}, u32[]{:S(2)}) copy-start(bf16[64,4608]{1,0:T(8,128)(2,1)S(1)} %collective-permute-done.15.refs_3_) | copy-start | bytes 1769476
  59.4 4.6 %copy-start.10 = (bf16[64,4608]{1,0:T(8,128)(2,1)}, bf16[64,4608]{1,0:T(8,128)(2,1)S(1)}, u32[]{:S(2)}) copy-start(bf16[64,4608]{1,0:T(8,128)(2,1)S(1)} %collective-permute-done.14.refs_2_) | copy-start | bytes 1769476
  59.5 4.5 %copy-start.11 = (bf16[64,4608]{1,0:T(8,128)(2,1)}, bf16[64,4608]{1,0:T(8,128)(2,1)S(1)}, u32[]{:S(2)}) copy-start(bf16[64,4608]{1,0:T(8,128)(2,1)S(1)} %collective-permute-done.13.refs_1_) | copy-start | bytes 1769476
  59.5 2.0 %collective-permute-start.17 = (bf16[64,4608]{1,0:T(8,128)(2,1)S(1)}, bf16[64,4608]{1,0:T(8,128)(2,1)S(1)}, u32[]{:S(2)}, u32[]{:S(2)}) collective-permute-start(bf16[64,4608]{1,0:T(8,128)(2,1)S(1)} %collective-permute-done.13.refs_1_), channel_id=1, source_target_pairs={{0,2},{1,3},{2,0},{3,1},{4,6},{5,7},{6,4},{7,5},{8,10},{9,11},{10,... | collective-permute-start | bytes 1769480 | tf_op jit(solution)/shard_map/ppermute | solution.py:974
  59.5 2.8 %collective-permute-start.18 = (bf16[64,4608]{1,0:T(8,128)(2,1)S(1)}, bf16[64,4608]{1,0:T(8,128)(2,1)S(1)}, u32[]{:S(2)}, u32[]{:S(2)}) collective-permute-start(bf16[64,4608]{1,0:T(8,128)(2,1)S(1)} %collective-permute-done.14.refs_2_), channel_id=1, source_target_pairs={{0,2},{1,3},{2,0},{3,1},{4,6},{5,7},{6,4},{7,5},{8,10},{9,11},{10,... | collective-permute-start | bytes 1769480 | tf_op jit(solution)/shard_map/ppermute | solution.py:974
  60.1 3.2 %collective-permute-start.19 = (bf16[64,4608]{1,0:T(8,128)(2,1)S(1)}, bf16[64,4608]{1,0:T(8,128)(2,1)S(1)}, u32[]{:S(2)}, u32[]{:S(2)}) collective-permute-start(bf16[64,4608]{1,0:T(8,128)(2,1)S(1)} %collective-permute-done.15.refs_3_), channel_id=1, source_target_pairs={{0,2},{1,3},{2,0},{3,1},{4,6},{5,7},{6,4},{7,5},{8,10},{9,11},{10,... | collective-permute-start | bytes 1769480 | tf_op jit(solution)/shard_map/ppermute | solution.py:974
  60.1 4.0 %copy-start.12 = (bf16[64,4608]{1,0:T(8,128)(2,1)}, bf16[64,4608]{1,0:T(8,128)(2,1)S(1)}, u32[]{:S(2)}) copy-start(bf16[64,4608]{1,0:T(8,128)(2,1)S(1)} %collective-permute-done.16.refs_4_) | copy-start | bytes 1769476
  61.6 2.5 %copy-start.13 = (bf16[64,4608]{1,0:T(8,128)(2,1)}, bf16[64,4608]{1,0:T(8,128)(2,1)S(1)}, u32[]{:S(2)}) copy-start(bf16[64,4608]{1,0:T(8,128)(2,1)S(1)} %collective-permute-done.17.refs_5_) | copy-start | bytes 1769476
  62.4 0.8 copy-start.14
  105.6 7.7 %collective-permute-start.20 = (bf16[256,4608]{1,0:T(8,128)(2,1)}, bf16[256,4608]{1,0:T(8,128)(2,1)}, u32[]{:S(2)}, u32[]{:S(2)}) collective-permute-start(bf16[256,4608]{1,0:T(8,128)(2,1)} %get-tuple-element.139), channel_id=1, source_target_pairs={{0,2},{1,3},{2,0},{3,1},{4,6},{5,7},{6,4},{7,5},{8,10},{9,11},{10,... | collective-permute-start | bytes 7077896 | tf_op jit(solution)/shard_map/ppermute | solution.py:974
  105.8 7.5 %copy-start = (bf16[256,4608]{1,0:T(8,128)(2,1)S(1)}, bf16[256,4608]{1,0:T(8,128)(2,1)}, u32[]{:S(2)}) copy-start(bf16[256,4608]{1,0:T(8,128)(2,1)} %get-tuple-element.138) | copy-start | bytes 7077892
  116.3 30.7 %collective-permute-start.21 = (bf16[64,4608]{1,0:T(8,128)(2,1)}, bf16[64,4608]{1,0:T(8,128)(2,1)S(1)}, u32[]{:S(2)}, u32[]{:S(2)}) collective-permute-start(bf16[64,4608]{1,0:T(8,128)(2,1)} %get-tuple-element.149), channel_id=1, source_target_pairs={{0,4},{1,5},{2,6},{3,7},{4,0},{5,1},{6,2},{7,3},{8,12},{9,13},{10,... | collective-permute-start | bytes 1769480 | tf_op jit(solution)/shard_map/ppermute | solution.py:974
  117.8 29.2 %collective-permute-start.22 = (bf16[64,4608]{1,0:T(8,128)(2,1)S(1)}, bf16[64,4608]{1,0:T(8,128)(2,1)S(1)}, u32[]{:S(2)}, u32[]{:S(2)}) collective-permute-start(bf16[64,4608]{1,0:T(8,128)(2,1)S(1)} %get-tuple-element.150), channel_id=1, source_target_pairs={{0,1},{1,0},{2,3},{3,2},{4,5},{5,4},{6,7},{7,6},{8,9},{9,8},{10,11... | collective-permute-start | bytes 1769480 | tf_op jit(solution)/shard_map/ppermute | solution.py:974
  118.6 28.4 %collective-permute-start.23 = (bf16[64,4608]{1,0:T(8,128)(2,1)S(1)}, bf16[64,4608]{1,0:T(8,128)(2,1)S(1)}, u32[]{:S(2)}, u32[]{:S(2)}) collective-permute-start(bf16[64,4608]{1,0:T(8,128)(2,1)S(1)} %get-tuple-element.151), channel_id=1, source_target_pairs={{0,5},{1,4},{2,7},{3,6},{4,1},{5,0},{6,3},{7,2},{8,13},{9,12},{10,... | collective-permute-start | bytes 1769480 | tf_op jit(solution)/shard_map/ppermute | solution.py:974
  147.0 2.7 %collective-permute-start.24 = (bf16[256,1664]{1,0:T(8,128)(2,1)}, bf16[256,1664]{1,0:T(8,128)(2,1)S(1)}, u32[]{:S(2)}, u32[]{:S(2)}) collective-permute-start(bf16[256,1664]{1,0:T(8,128)(2,1)} %get-tuple-element.153), channel_id=1, source_target_pairs={{0,2},{1,3},{2,0},{3,1},{4,6},{5,7},{6,4},{7,5},{8,10},{9,11},{10,... | collective-permute-start | bytes 2555912 | tf_op jit(solution)/shard_map/ppermute | solution.py:974
  151.2 16.5 %collective-permute-start.25 = (bf16[64,1664]{1,0:T(8,128)(2,1)S(1)}, bf16[64,1664]{1,0:T(8,128)(2,1)S(1)}, u32[]{:S(2)}, u32[]{:S(2)}) collective-permute-start(bf16[64,1664]{1,0:T(8,128)(2,1)S(1)} %get-tuple-element.155), channel_id=1, source_target_pairs={{0,4},{1,5},{2,6},{3,7},{4,0},{5,1},{6,2},{7,3},{8,12},{9,13},{10,... | collective-permute-start | bytes 638984 | tf_op jit(solution)/shard_map/ppermute | solution.py:974
  152.7 17.0 %collective-permute-start.26 = (bf16[64,1664]{1,0:T(8,128)(2,1)S(1)}, bf16[64,1664]{1,0:T(8,128)(2,1)S(1)}, u32[]{:S(2)}, u32[]{:S(2)}) collective-permute-start(bf16[64,1664]{1,0:T(8,128)(2,1)S(1)} %get-tuple-element.156), channel_id=1, source_target_pairs={{0,1},{1,0},{2,3},{3,2},{4,5},{5,4},{6,7},{7,6},{8,9},{9,8},{10,11... | collective-permute-start | bytes 638984 | tf_op jit(solution)/shard_map/ppermute | solution.py:974
  153.5 16.3 %collective-permute-start.27 = (bf16[64,1664]{1,0:T(8,128)(2,1)S(1)}, bf16[64,1664]{1,0:T(8,128)(2,1)S(1)}, u32[]{:S(2)}, u32[]{:S(2)}) collective-permute-start(bf16[64,1664]{1,0:T(8,128)(2,1)S(1)} %get-tuple-element.157), channel_id=1, source_target_pairs={{0,5},{1,4},{2,7},{3,6},{4,1},{5,0},{6,3},{7,2},{8,13},{9,12},{10,... | collective-permute-start | bytes 638984 | tf_op jit(solution)/shard_map/ppermute | solution.py:974
  155.7 17.1 %collective-permute-start.33 = (bf16[16,4608]{1,0:T(8,128)(2,1)}, bf16[16,4608]{1,0:T(8,128)(2,1)S(1)}, u32[]{:S(2)}, u32[]{:S(2)}) collective-permute-start(bf16[16,4608]{1,0:T(8,128)(2,1)} %get-tuple-element.206), channel_id=1, source_target_pairs={{0,24},{1,25},{2,26},{3,27},{4,28},{5,29},{6,30},{7,31},{8,16},{9,... | collective-permute-start | bytes 442376 | tf_op jit(solution)/shard_map/ppermute | solution.py:974
  158.0 27.3 %collective-permute-start.32 = (bf16[16,4608]{1,0:T(8,128)(2,1)}, bf16[16,4608]{1,0:T(8,128)(2,1)S(1)}, u32[]{:S(2)}, u32[]{:S(2)}) collective-permute-start(bf16[16,4608]{1,0:T(8,128)(2,1)} %get-tuple-element.207), channel_id=1, source_target_pairs={{0,16},{1,17},{2,18},{3,19},{4,20},{5,21},{6,22},{7,23},{8,24},{9,... | collective-permute-start | bytes 442376 | tf_op jit(solution)/shard_map/ppermute | solution.py:974
  167.6 17.6 %collective-permute-start.31 = (bf16[16,4608]{1,0:T(8,128)(2,1)S(1)}, bf16[16,4608]{1,0:T(8,128)(2,1)S(1)}, u32[]{:S(2)}, u32[]{:S(2)}) collective-permute-start(bf16[16,4608]{1,0:T(8,128)(2,1)S(1)} %get-tuple-element.208), channel_id=1, source_target_pairs={{0,8},{1,9},{2,10},{3,11},{4,12},{5,13},{6,14},{7,15},{8,0},{9,1},... | collective-permute-start | bytes 442376 | tf_op jit(solution)/shard_map/ppermute | solution.py:974
  170.5 14.8 %collective-permute-start.30 = (bf16[16,1664]{1,0:T(8,128)(2,1)S(1)}, bf16[16,1664]{1,0:T(8,128)(2,1)S(1)}, u32[]{:S(2)}, u32[]{:S(2)}) collective-permute-start(bf16[16,1664]{1,0:T(8,128)(2,1)S(1)} %get-tuple-element.214), channel_id=1, source_target_pairs={{0,24},{1,25},{2,26},{3,27},{4,28},{5,29},{6,30},{7,31},{8,16},{9,... | collective-permute-start | bytes 159752 | tf_op jit(solution)/shard_map/ppermute | solution.py:974
  172.8 12.5 %collective-permute-start.29 = (bf16[16,1664]{1,0:T(8,128)(2,1)S(1)}, bf16[16,1664]{1,0:T(8,128)(2,1)S(1)}, u32[]{:S(2)}, u32[]{:S(2)}) collective-permute-start(bf16[16,1664]{1,0:T(8,128)(2,1)S(1)} %get-tuple-element.215), channel_id=1, source_target_pairs={{0,16},{1,17},{2,18},{3,19},{4,20},{5,21},{6,22},{7,23},{8,24},{9,... | collective-permute-start | bytes 159752 | tf_op jit(solution)/shard_map/ppermute | solution.py:974
  172.8 12.5 %copy-start.2 = (bf16[16,4608]{1,0:T(8,128)(2,1)}, bf16[16,4608]{1,0:T(8,128)(2,1)S(1)}, u32[]{:S(2)}) copy-start(bf16[16,4608]{1,0:T(8,128)(2,1)S(1)} %collective-permute-done.33.refs_7_) | copy-start | bytes 442372
  172.8 12.5 %collective-permute-start.28 = (bf16[16,1664]{1,0:T(8,128)(2,1)S(1)}, bf16[16,1664]{1,0:T(8,128)(2,1)S(1)}, u32[]{:S(2)}, u32[]{:S(2)}) collective-permute-start(bf16[16,1664]{1,0:T(8,128)(2,1)S(1)} %get-tuple-element.216), channel_id=1, source_target_pairs={{0,8},{1,9},{2,10},{3,11},{4,12},{5,13},{6,14},{7,15},{8,0},{9,1},... | collective-permute-start | bytes 159752 | tf_op jit(solution)/shard_map/ppermute | solution.py:974
  (8 other events, 5.7 us)
where the time goes:
time: 189 us; the launch traced here: 188 us
  Pallas kernels  121 us (64%)
  starting transfers between devices  35.5 us (19%)
  waiting for transfers between devices  20 us (11%)
  other arithmetic  7.08 us (4%)
  local copies, waits for them, and re-layouts  3.49 us (2%)
    pallas_call x1, Pallas kernels, mlp(): pl.pallas_call(functools.partial(mlp_kernel, masks, relative), grid=(n //...  41.5 us
    ppermute x34, starting transfers between devices, exchange(): return lax.ppermute(x, AXES, [(i, i ^ mask) for i in range(size)])  35.5 us
    pallas_call x2, Pallas kernels, attend_back(): pl.pallas_call(functools.partial(attend_back_kernel, start), grid=(clips,...  23.9 us
    pallas_call x1, Pallas kernels, attend(): pl.pallas_call(functools.partial(attend_kernel, masks), grid=(n // PATCHE...  20.9 us
    ppermute x34, waiting for transfers between devices, exchange(): return lax.ppermute(x, AXES, [(i, i ^ mask) for i in range(size)])  20 us
    pallas_call x1, Pallas kernels, project_back(): pl.pallas_call(functools.partial(project_back_kernel, relative), grid=(n...  10.9 us
    pallas_call x1, Pallas kernels, output(): pl.pallas_call(output_kernel, grid=(n // tile,), in_specs=[rows_spec(tile...  10.3 us
    pallas_call x1, Pallas kernels, token_back(): pl.pallas_call(token_back_kernel, grid=(n // tile,), in_specs=[rows_spec(...  9.67 us
  transfers between devices with their start and end apart: 34, of which 10 were waited for; matrix products, arithmetic and copies ran while one was open for 2% of the time, Pallas kernels for 40%

commit v1 on v0

--- a/solution.py
+++ b/solution.py
@@ -31,7 +31,6 @@
 BF16 = jnp.bfloat16
 LOG2_E = float(np.log2(np.e))
 LOG_BELL = float(np.log2(2.0 / np.sqrt(2.0 * np.pi)))
-VMEM_BYTES = 60 * 1024 * 1024
 ROWS = 32
 
 
@@ -67,24 +66,14 @@
     return lax.broadcasted_iota(jnp.int32, shape, dim)
 
 
-def fill_perm(perm_ref, s, u, to_windows):
+def fill_perm(perm_ref, s, u):
     for r0 in range(0, PATCHES, BLOCK):
         row = iota((BLOCK, 128), 0) + r0
-        if to_windows:
-            a = (row >> 2) & 3
-            b = row & 3
-            t = (4 * (row >> 5) + a + s) & (GRID_T - 1)
-            f = (4 * ((row >> 4) & 1) + b + u) & (GRID_F - 1)
-            source = t * GRID_F + f
-        else:
-            r = ((row >> 3) - s) & (GRID_T - 1)
-            q = ((row & 7) - u) & (GRID_F - 1)
-            source = (r >> 2) * 32 + (q >> 2) * 16 + (r & 3) * 4 + (q & 3)
-        lane = iota((BLOCK, 128), 1)
+        t = (4 * (row >> 5) + ((row >> 2) & 3) + s) & (GRID_T - 1)
+        f = (4 * ((row >> 4) & 1) + (row & 3) + u) & (GRID_F - 1)
+        source = t * GRID_F + f - iota((BLOCK, 128), 1)
         for c0 in range(0, PATCHES, 128):
-            perm_ref[r0 : r0 + BLOCK, c0 : c0 + 128] = jnp.where(
-                source == lane + c0, 1.0, 0.0
-            ).astype(BF16)
+            perm_ref[r0 : r0 + BLOCK, c0 : c0 + 128] = jnp.where(source == c0, 1.0, 0.0).astype(BF16)
 
 
 def compact_code(rows):
@@ -264,7 +253,7 @@
     return pl.pallas_call(
         pack_kernel,
         out_shape=[struct((UNIT, cols * width + more), BF16) for cols, more in ((3, 128), (9, 0))],
-        compiler_params=pltpu.CompilerParams(vmem_limit_bytes=VMEM_BYTES),
+        compiler_params=pltpu.CompilerParams(vmem_limit_bytes=60 * 1024 * 1024),
         name="pack",
     )(*vectors, *weights)
 
@@ -302,7 +291,7 @@
         )
         vec_ref[8:16, :] = dot_nn(flat, mix_matrix())[:8, :]
 
-    fill_perm(perm_ref, s, u, True)
+    fill_perm(perm_ref, s, u)
     rows_ref[...] = dot_nn(perm_ref[...], tok_ref[...])
     for r in range(0, PATCHES, ROWS):
         normed, _ = norm_stats(rows_ref[r : r + ROWS, :])
@@ -363,8 +352,7 @@
                 values = expand_rows(qkv_ref[rows, 2 * width + c0 : 2 * width + c0 + 128], g, lanes)
                 wide = jnp.concatenate([low * spread[g], low * spread[2 + g]], axis=1)
                 ctxw_ref[rows, c0 : c0 + 128] = dot_nn(wide, values).astype(BF16)
-    fill_perm(perm_ref, s, u, False)
-    ctx_ref[...] = dot_nn(perm_ref[...], ctxw_ref[...]).astype(BF16)
+    ctx_ref[...] = dot_tn(perm_ref[...], ctxw_ref[...]).astype(BF16)
 
 
 def weave(first, second):
@@ -552,7 +540,7 @@
     def _():
         gpos_ref[...] = jnp.zeros_like(gpos_ref)
 
-    fill_perm(perm_ref, s, u, True)
+    fill_perm(perm_ref, s, u)
     do_ref[...] = dot_nn(perm_ref[...], gctx_ref[...]).astype(BF16)
     lanes = head_lanes(BF16)
     code = compact_code(BLOCK)
@@ -636,10 +624,7 @@
                             )
                             at = 128 * two + 64 * blk + 16 * w
                             gqw_ref[at : at + 16, out_at + c0 : out_at + c0 + 128] = (total * factor).astype(BF16)
-    fill_perm(perm_ref, s, u, False)
-    for c in range(3):
-        cols = slice(c * width, (c + 1) * width)
-        gqn_ref[:, cols] = dot_nn(perm_ref[...], gqw_ref[:, cols]).astype(BF16)
+    gqn_ref[...] = dot_tn(perm_ref[...], gqw_ref[...]).astype(BF16)
 
 
 def project_back_kernel(
@@ -763,8 +748,8 @@
     return pl.CostEstimate(flops=flops, bytes_accessed=nbytes, transcendentals=0)
 
 
-def params():
-    return pltpu.CompilerParams(vmem_limit_bytes=VMEM_BYTES, dimension_semantics=("arbitrary",))
+def params(mib):
+    return pltpu.CompilerParams(vmem_limit_bytes=mib * 1024 * 1024, dimension_semantics=("arbitrary",))
 
 
 def clip_spec(cols, start):
@@ -798,7 +783,7 @@
             *[pltpu.VMEM((PATCHES, 384), BF16)] * 2,
             pltpu.SemaphoreType.DMA((SHARDS,)),
         ],
-        compiler_params=params(),
+        compiler_params=params(60),
         cost_estimate=cost(2800000000, n * width),
         name="attend",
     )(shifts, counts, tokens, table, *pieces)
@@ -841,7 +826,7 @@
             *[pltpu.VMEM((tile, width), BF16)] * 4,
             pltpu.SemaphoreType.DMA((SHARDS,)),
         ],
-        compiler_params=params(),
+        compiler_params=params(54),
         cost_estimate=cost(5000000000, n * width),
         name="mlp",
     )(tokens, ctx, cot, vec, *pieces)
@@ -872,7 +857,7 @@
             *[pltpu.VMEM((PATCHES, 256), BF16)] * 2,
         ],
         input_output_aliases={} if into is None else {4: 0},
-        compiler_params=params(),
+        compiler_params=params(24),
         cost_estimate=cost(700000000 * clips, n * width),
         name="attend_back",
     )(shifts, qkv, prob, gctx, prob if into is None else into)
@@ -896,7 +881,7 @@
             pltpu.VMEM((64, 256), F32),
             pltpu.VMEM((width, 128), F32),
         ],
-        compiler_params=params(),
+        compiler_params=params(24),
         cost_estimate=cost(1000000000, n * width),
         name="project_back",
     )(gqn, tokens, w_qkv, small, gpos_a, gpos_b)
@@ -912,7 +897,7 @@
         out_specs=rows_spec(tile, width),
         out_shape=struct((n, width), F32),
         scratch_shapes=[pltpu.VMEM((tile // 2, width), F32)] * 2,
-        compiler_params=params(),
+        compiler_params=params(24),
         cost_estimate=cost(1000000000, n * width),
         name="token_back",
     )(gqn, tokens, gmid, w_qkv, vec)
@@ -927,7 +912,7 @@
         + [whole_spec(x.shape) for x in (wp, wd, vec)],
         out_specs=rows_spec(tile, width),
         out_shape=struct((n, width), BF16),
-        compiler_params=params(),
+        compiler_params=params(24),
         cost_estimate=cost(1000000000, n * width),
         name="output",
     )(*gelu, ctx, tokens, wp, wd, vec)
@@ -964,7 +949,7 @@
             struct((4 * UNIT, width), F32),
             *[struct((UNIT,), F32)] * 8, struct((4 * UNIT,), F32), struct((HEADS, RELS), F32),
         ],
-        compiler_params=pltpu.CompilerParams(vmem_limit_bytes=VMEM_BYTES),
+        compiler_params=pltpu.CompilerParams(vmem_limit_bytes=60 * 1024 * 1024),
         name="finish",
     )(*first, *second)
 
@@ -1080,8 +1065,9 @@
         second = spread_far(second, COLUMN)
         first = spread_far(jnp.concatenate(first), PLANE)
         first, second = lax.optimization_barrier((first, second))
-        first, second = lax.optimization_barrier((spread_core(first), jnp.concatenate(second)))
+        first, second = lax.optimization_barrier((first, jnp.concatenate(second)))
         second = spread_far(second, PLANE)
+        first = spread_core(first)
     else:
         first, second = ([x] for x in whole_weights(vectors, weights))
         masks = None
@@ -1099,17 +1085,15 @@
         gqn, gsecond = lax.optimization_barrier((gqn, gsecond))
         gsecond = meet_far(gsecond, PLANE)
     gqn, gpos_b = attend_back(shifts, qkv, prob, gctx, gqn, half, clips - half)
+    gtok = token_back(gqn, tokens, gmid, w_qkv, vec)
+    gqn, gtok = lax.optimization_barrier((gqn, gtok))
     gfirst = project_back(gqn, tokens, w_qkv, small, gpos_a, gpos_b, stepped)
     if stepped:
         gfirst, gsecond = lax.optimization_barrier((gfirst, gsecond))
         gsecond = meet_far(add_blocks(gsecond), COLUMN)
-        gfirst = meet_core(*gfirst)
-        gfirst, gqn = lax.optimization_barrier((gfirst, gqn))
-        gfirst = meet_far(gfirst, PLANE)
-    gtok = token_back(gqn, tokens, gmid, w_qkv, vec)
-    if stepped:
-        gfirst, gtok, gelu = lax.optimization_barrier((gfirst, gtok, gelu))
-        gfirst = meet_far(add_blocks(gfirst), COLUMN)
+        gfirst = meet_far(meet_core(*gfirst), PLANE)
+        gfirst, gelu = lax.optimization_barrier((add_blocks(gfirst), gelu))
+        gfirst = meet_far(gfirst, COLUMN)
     out = output(gelu, ctx, tokens, wp, wd, vec)
     if stepped:
         gfirst, gsecond, out = lax.optimization_barrier((gfirst, gsecond, out))

time: 189 us -> 173 us (0.915)
  Pallas kernels: 121 us -> 105 us
  waiting for transfers between devices: 20 us -> 24.7 us
  other arithmetic: 7.08 us -> 3.54 us
    pallas_call x2, Pallas kernels: 23.9 us -> 18 us  [attend_back(): pl.pallas_call(functools.partial(attend_back_kernel, start), grid=(clips,...]
    ppermute x34, waiting for transfers between devices: 20 us -> 24.7 us  [exchange(): return lax.ppermute(x, AXES, [(i, i ^ mask) for i in range(size)])]
    pallas_call x1, Pallas kernels: 9.67 us -> 5.8 us  [token_back(): pl.pallas_call(token_back_kernel, grid=(n // tile,), in_specs=[rows_spec(...]
    convert_element_type x4, other arithmetic: 6.14 us -> 2.42 us  [add(): return parts[0].astype(BF16)]
    pallas_call x1, Pallas kernels: 10.3 us -> 6.92 us  [output(): pl.pallas_call(output_kernel, grid=(n // tile,), in_specs=[rows_spec(tile...]
    pallas_call x1, Pallas kernels: 10.9 us -> 7.64 us  [project_back(): pl.pallas_call(functools.partial(project_back_kernel, relative), grid=(n...]
    unnamed x47 -> x83, local copies, waits for them, and re-layouts: 3.48 us -> 5.05 us
  transfers between devices with their start and end apart: 34 -> 34, of which waited for: 10 -> 13; matrix products, arithmetic and copies ran while one was open for 2% -> 1% of each run, Pallas kernels for 40% -> 34%
where the time goes in v1:
time: 173 us
  Pallas kernels  105 us (61%)
  starting transfers between devices  33.7 us (19%)
  waiting for transfers between devices  24.7 us (14%)
  local copies, waits for them, and re-layouts  5.06 us (3%)
  other arithmetic  3.54 us (2%)
    pallas_call x1, Pallas kernels, mlp(): pl.pallas_call(functools.partial(mlp_kernel, masks, relative), grid=(n //...  42.3 us
    ppermute x34, starting transfers between devices, exchange(): return lax.ppermute(x, AXES, [(i, i ^ mask) for i in range(size)])  33.7 us
    ppermute x34, waiting for transfers between devices, exchange(): return lax.ppermute(x, AXES, [(i, i ^ mask) for i in range(size)])  24.7 us
    pallas_call x1, Pallas kernels, attend(): pl.pallas_call(functools.partial(attend_kernel, masks), grid=(n // PATCHE...  20.1 us
    pallas_call x2, Pallas kernels, attend_back(): pl.pallas_call(functools.partial(attend_back_kernel, start), grid=(clips,...  18 us
    pallas_call x1, Pallas kernels, project_back(): pl.pallas_call(functools.partial(project_back_kernel, relative), grid=(n...  7.64 us
    pallas_call x1, Pallas kernels, output(): pl.pallas_call(output_kernel, grid=(n // tile,), in_specs=[rows_spec(tile...  6.92 us
    pallas_call x1, Pallas kernels, token_back(): pl.pallas_call(token_back_kernel, grid=(n // tile,), in_specs=[rows_spec(...  5.8 us
  transfers between devices with their start and end apart: 34, of which 13 were waited for; matrix products, arithmetic and copies ran while one was open for 1% of the time, Pallas kernels for 34%

profile of v1, /device:TPU:0, one launch (start us, length us, event | category | flops | bytes accessed | tf_op | source)
XLA Modules:
  0.0 172.9 jit_solution(8794009359055202745)
XLA Ops:
  0.7 1.8 %pack.1 = (bf16[16,1664]{1,0:T(8,128)(2,1)}, bf16[16,4608]{1,0:T(8,128)(2,1)}) custom-call(bf16[16]{0:T(256)(128)(2,1)} %refs_0_.1, bf16[16]{0:T(256)(128)(2,1)} %refs_1_.1, bf16[16]{0:T(256)(128)(2,1)} %refs_2_.1, bf16[16]{0:T(256)(128)(2,1)} %refs_3_.1, bf16[16]{0:T(256)(128)(2,1)} %refs_4_.1, bf16[16]{0:T(256)(128)(2,1)} %refs_5_.2, ...), custom_call_target="tpu_custom_call" | custom-call | tf_op jit(solution)/shard_map/pack/pallas_call | solution.py:253
  2.4 5.0 %collective-permute-start.2 = (bf16[16,1664]{1,0:T(8,128)(2,1)}, bf16[16,1664]{1,0:T(8,128)(2,1)S(1)}, u32[]{:S(2)}, u32[]{:S(2)}) collective-permute-start(bf16[16,1664]{1,0:T(8,128)(2,1)} %get-tuple-element.101), channel_id=1, source_target_pairs={{0,24},{1,25},{2,26},{3,27},{4,28},{5,29},{6,30},{7,31},{8,16},{9,... | collective-permute-start | bytes 159752 | tf_op jit(solution)/shard_map/ppermute | solution.py:959
  7.5 0.6 collective-permute-start
  8.1 3.8 %collective-permute-start.8 = (bf16[16,4608]{1,0:T(8,128)(2,1)}, bf16[16,4608]{1,0:T(8,128)(2,1)S(1)}, u32[]{:S(2)}, u32[]{:S(2)}) collective-permute-start(bf16[16,4608]{1,0:T(8,128)(2,1)} %get-tuple-element.107), channel_id=1, source_target_pairs={{0,24},{1,25},{2,26},{3,27},{4,28},{5,29},{6,30},{7,31},{8,16},{9,... | collective-permute-start | bytes 442376 | tf_op jit(solution)/shard_map/ppermute | solution.py:959
  11.9 0.8 constant_dynamic-update-slice_fusion.3
  12.7 3.8 %collective-permute-done.1 = bf16[16,1664]{1,0:T(8,128)(2,1)S(1)} collective-permute-done((bf16[16,1664]{1,0:T(8,128)(2,1)}, bf16[16,1664]{1,0:T(8,128)(2,1)S(1)}, u32[]{:S(2)}, u32[]{:S(2)}) %collective-permute-start.1) | collective-permute-done | bytes 53280 | tf_op jit(solution)/shard_map/ppermute | solution.py:959
  16.5 2.5 %collective-permute-start.5 = (bf16[64,1664]{1,0:T(8,128)(2,1)S(1)}, bf16[64,1664]{1,0:T(8,128)(2,1)S(1)}, u32[]{:S(2)}, u32[]{:S(2)}) collective-permute-start(bf16[64,1664]{1,0:T(8,128)(2,1)S(1)} %constant_dynamic-update-slice_fusion.refs_0_), channel_id=1, source_target_pairs={{0,5},{1,4},{2,7},{3,6},{4,1},{5,0},{6,3},{7,2},{8,13},{9,12},{10,... | collective-permute-start | bytes 638984 | tf_op jit(solution)/shard_map/ppermute | solution.py:959
  19.1 0.5 collective-permute-start.4
  19.6 0.5 collective-permute-start.3
  20.1 1.3 collective-permute-start.6
  21.4 5.0 %collective-permute-done.7 = bf16[16,4608]{1,0:T(8,128)(2,1)S(1)} collective-permute-done((bf16[16,4608]{1,0:T(8,128)(2,1)}, bf16[16,4608]{1,0:T(8,128)(2,1)S(1)}, u32[]{:S(2)}, u32[]{:S(2)}) %collective-permute-start.7) | collective-permute-done | bytes 147488 | tf_op jit(solution)/shard_map/ppermute | solution.py:959
  26.5 0.6 collective-permute-done.6
  27.1 1.1 pad_maximum_fusion.refs_0_
  28.8 2.4 %collective-permute-start.15 = (bf16[64,4608]{1,0:T(8,128)(2,1)S(1)}, bf16[64,4608]{1,0:T(8,128)(2,1)S(1)}, u32[]{:S(2)}, u32[]{:S(2)}) collective-permute-start(bf16[64,4608]{1,0:T(8,128)(2,1)S(1)} %pad_maximum_fusion.refs_0_), channel_id=1, source_target_pairs={{0,5},{1,4},{2,7},{3,6},{4,1},{5,0},{6,3},{7,2},{8,13},{9,12},{10,... | collective-permute-start | bytes 1769480 | tf_op jit(solution)/shard_map/ppermute | solution.py:959
  31.7 0.5 collective-permute-start.13
  33.1 0.8 collective-permute-done.11.refs_6_
  34.1 0.7 copy-done.37
  34.8 20.1 %attend.1 = (bf16[2048,1536]{1,0:T(8,128)(2,1)}, f32[2048,256]{1,0:T(8,128)}, bf16[2048,512]{1,0:T(8,128)(2,1)}, bf16[512,1664]{1,0:T(8,128)(2,1)}, f32[16,512]{1,0:T(8,128)}) custom-call(s32[2,4]{1,0:T(2,128)} %bitcast.5, s32[4]{0:T(128)} %count_ref.1, bf16[2048,512]{1,0:T(8,128)(2,1)} %refs_5_.3, bf16[16,49]{1,0:T(8,128)(2,1)} %bitcast.9, ...), custom_call_target="tpu_custom_call" | custom-call | flops 2800000000 | bytes 1048576 | tf_op jit(solution)/shard_map/attend/pallas_call | solution.py:762
  54.9 2.7 %collective-permute-done.14.refs_2_ = bf16[64,4608]{1,0:T(8,128)(2,1)S(1)} collective-permute-done((bf16[64,4608]{1,0:T(8,128)(2,1)S(1)}, bf16[64,4608]{1,0:T(8,128)(2,1)S(1)}, u32[]{:S(2)}, u32[]{:S(2)}) %collective-permute-start.14) | collective-permute-done | bytes 589856 | tf_op jit(solution)/shard_map/ppermute | solution.py:959
  57.8 0.5 collective-permute-start.18
  58.3 1.4 collective-permute-done.17.refs_5_
  59.8 0.8 collective-permute-done.18.refs_6_
  60.6 0.8 collective-permute-done.19.refs_7_
  61.5 0.8 copy-done.31
  62.3 42.3 %mlp.1 = (bf16[2048,512]{1,0:T(8,128)(2,1)}, bf16[2048,512]{1,0:T(8,128)(2,1)}, bf16[2048,512]{1,0:T(8,128)(2,1)}, bf16[2048,512]{1,0:T(8,128)(2,1)}, f32[2048,5...) custom-call(bf16[2048,512]{1,0:T(8,128)(2,1)} %refs_5_.3, ...), custom_call_target="tpu_custom_call" | custom-call | flops 5000000000 | bytes 1048576 | tf_op jit(solution)/shard_map/mlp/pallas_call | solution.py:802
  104.8 1.6 copy-done.2
  106.4 4.7 %attend_back.2 = (bf16[2048,1536]{1,0:T(8,128)(2,1)S(1)}, f32[64,256]{1,0:T(8,128)S(1)}) custom-call(s32[2,4]{1,0:T(2,128)S(1)} %bitcast.6, bf16[2048,1536]{1,0:T(8,128)(2,1)S(1)} %bitcast.4, f32[2048,256]{1,0:T(8,128)S(1)} %copy-done.1, bf16[2048,512]{1,0:T(8,128)(2,1)S(1)} %copy-done.2, f32[2048,256]{1,0:T(8,128)S(1)} %copy-done.1), custom_call_target="tpu_custom_call" | custom-call | flops 700000000 | bytes 1048576 | tf_op jit(solution)/shard_map/attend_back/pallas_call | solution.py:841
  111.2 0.5 add_convert_fusion
  111.8 1.6 collective-permute-start.21
  113.4 0.8 collective-permute-start.22
  114.1 1.2 collective-permute-start.23
  115.4 13.3 %attend_back.3 = (bf16[2048,1536]{1,0:T(8,128)(2,1)S(1)}, f32[64,256]{1,0:T(8,128)S(1)}) custom-call(s32[2,4]{1,0:T(2,128)S(1)} %bitcast.7, bf16[2048,1536]{1,0:T(8,128)(2,1)S(1)} %bitcast.4, f32[2048,256]{1,0:T(8,128)S(1)} %copy-done.1, bf16[2048,512]{1,0:T(8,128)(2,1)S(1)} %copy-done.3, ...), custom_call_target="tpu_custom_call", output_to_operand_aliasing={{0}: (4, {})} | custom-call | flops 2100000000 | bytes 1048576 | tf_op jit(solution)/shard_map/attend_back/pallas_call | solution.py:841
  128.7 5.8 %token_back.1 = f32[2048,512]{1,0:T(8,128)} custom-call(bf16[2048,1536]{1,0:T(8,128)(2,1)S(1)} %get-tuple-element.132.gqn_ref, bf16[2048,512]{1,0:T(8,128)(2,1)S(1)} %copy-done, f32[2048,512]{1,0:T(8,128)S(1)} %copy-done.5, bf16[512,1664]{1,0:T(8,128)(2,1)S(1)} %copy-done.4, f32[16,512]{1,0:T(8,128)S(1)} %copy-done.13), custom_call_target="tpu_custom_call" | custom-call | flops 1000000000 | bytes 1048576 | tf_op jit(solution)/shard_map/token_back/pallas_call | solution.py:892
  134.6 7.6 %project_back.1 = (bf16[256,1664]{1,0:T(8,128)(2,1)S(1)}, bf16[256,1664]{1,0:T(8,128)(2,1)S(1)}) custom-call(bf16[2048,1536]{1,0:T(8,128)(2,1)S(1)} %get-tuple-element.132.gqn_ref, bf16[2048,512]{1,0:T(8,128)(2,1)S(1)} %copy-done, bf16[512,1664]{1,0:T(8,128)(2,1)S(1)} %copy-done.4, f32[16,512]{1,0:T(8,128)S(1)} %copy-done.14, ...), custom_call_target="tpu_custom_call" | custom-call | flops 1000000000 | bytes 1048576 | tf_op jit(solution)/shard_map/project_back/pallas_call | solution.py:869
  142.3 2.4 %collective-permute-done.24 = bf16[256,1664]{1,0:T(8,128)(2,1)S(1)} collective-permute-done((bf16[256,1664]{1,0:T(8,128)(2,1)S(1)}, bf16[256,1664]{1,0:T(8,128)(2,1)S(1)}, u32[]{:S(2)}, u32[]{:S(2)}) %collective-permute-start.24) | collective-permute-done | bytes 852000 | tf_op jit(solution)/shard_map/ppermute | solution.py:959
  144.9 1.8 %collective-permute-start.27 = (bf16[64,1664]{1,0:T(8,128)(2,1)S(1)}, bf16[64,1664]{1,0:T(8,128)(2,1)S(1)}, u32[]{:S(2)}, u32[]{:S(2)}) collective-permute-start(bf16[64,1664]{1,0:T(8,128)(2,1)S(1)} %get-tuple-element.195), channel_id=1, source_target_pairs={{0,5},{1,4},{2,7},{3,6},{4,1},{5,0},{6,3},{7,2},{8,13},{9,12},{10,... | collective-permute-start | bytes 638984 | tf_op jit(solution)/shard_map/ppermute | solution.py:959
  146.7 1.2 collective-permute-start.26
  147.9 0.5 collective-permute-start.25
  148.4 1.0 add_convert_fusion.8
  149.4 2.3 %collective-permute-start.33 = (bf16[16,4608]{1,0:T(8,128)(2,1)S(1)}, bf16[16,4608]{1,0:T(8,128)(2,1)S(1)}, u32[]{:S(2)}, u32[]{:S(2)}) collective-permute-start(bf16[16,4608]{1,0:T(8,128)(2,1)S(1)} %get-tuple-element.190), channel_id=1, source_target_pairs={{0,24},{1,25},{2,26},{3,27},{4,28},{5,29},{6,30},{7,31},{8,16},{9,... | collective-permute-start | bytes 442376 | tf_op jit(solution)/shard_map/ppermute | solution.py:959
  151.7 2.3 %collective-permute-done.27 = bf16[64,1664]{1,0:T(8,128)(2,1)S(1)} collective-permute-done((bf16[64,1664]{1,0:T(8,128)(2,1)S(1)}, bf16[64,1664]{1,0:T(8,128)(2,1)S(1)}, u32[]{:S(2)}, u32[]{:S(2)}) %collective-permute-start.27) | collective-permute-done | bytes 213024 | tf_op jit(solution)/shard_map/ppermute | solution.py:959
  154.0 3.7 %collective-permute-done.26 = bf16[64,1664]{1,0:T(8,128)(2,1)S(1)} collective-permute-done((bf16[64,1664]{1,0:T(8,128)(2,1)S(1)}, bf16[64,1664]{1,0:T(8,128)(2,1)S(1)}, u32[]{:S(2)}, u32[]{:S(2)}) %collective-permute-start.26) | collective-permute-done | bytes 213024 | tf_op jit(solution)/shard_map/ppermute | solution.py:959
  157.8 0.7 add_convert_fusion.12
  158.6 2.8 %collective-permute-start.29 = (bf16[16,1664]{1,0:T(8,128)(2,1)S(1)}, bf16[16,1664]{1,0:T(8,128)(2,1)S(1)}, u32[]{:S(2)}, u32[]{:S(2)}) collective-permute-start(bf16[16,1664]{1,0:T(8,128)(2,1)S(1)} %get-tuple-element.150), channel_id=1, source_target_pairs={{0,16},{1,17},{2,18},{3,19},{4,20},{5,21},{6,22},{7,23},{8,24},{9,... | collective-permute-start | bytes 159752 | tf_op jit(solution)/shard_map/ppermute | solution.py:959
  161.3 1.6 collective-permute-start.30
  162.9 6.9 %output.1 = bf16[2048,512]{1,0:T(8,128)(2,1)} custom-call(bf16[2048,512]{1,0:T(8,128)(2,1)S(1)} %copy-done.7, bf16[2048,512]{1,0:T(8,128)(2,1)S(1)} %copy-done.8, bf16[2048,512]{1,0:T(8,128)(2,1)S(1)} %copy-done.9, bf16[2048,512]{1,0:T(8,128)(2,1)S(1)} %copy-done.10, bf16[2048,512]{1,0:T(8,128)(2,1)S(1)} %copy-done.6, bf16[2048,512]{1,0:T(8,128)(2,1)S(1)} %copy-done, ...), custom_call_target="tpu_custom_call" | custom-call | flops 1000000000 | bytes 1048576 | tf_op jit(solution)/shard_map/output/pallas_call | solution.py:908
  170.0 0.6 copy-done.19
  170.7 2.1 %finish.1 = (f32[16,1536]{1,0:T(8,128)}, f32[16,512]{1,0:T(8,128)}, f32[16,2048]{1,0:T(8,128)}, f32[64,512]{1,0:T(8,128)}, f32[16]{0:T(128)}, /*index=5*/f32[16]...) custom-call(bf16[16,1664]{1,0:T(8,128)(2,1)} %get-tuple-element.164., ...), custom_call_target="tpu_custom_call" | custom-call | tf_op jit(solution)/shard_map/finish/pallas_call | solution.py:945
  (119 shorter events, 3.2 us)
Async XLA Ops:
  2.4 14.1 %collective-permute-start.2 = (bf16[16,1664]{1,0:T(8,128)(2,1)}, bf16[16,1664]{1,0:T(8,128)(2,1)S(1)}, u32[]{:S(2)}, u32[]{:S(2)}) collective-permute-start(bf16[16,1664]{1,0:T(8,128)(2,1)} %get-tuple-element.101), channel_id=1, source_target_pairs={{0,24},{1,25},{2,26},{3,27},{4,28},{5,29},{6,30},{7,31},{8,16},{9,... | collective-permute-start | bytes 159752 | tf_op jit(solution)/shard_map/ppermute | solution.py:959
  7.5 9.0 %collective-permute-start.1 = (bf16[16,1664]{1,0:T(8,128)(2,1)}, bf16[16,1664]{1,0:T(8,128)(2,1)S(1)}, u32[]{:S(2)}, u32[]{:S(2)}) collective-permute-start(bf16[16,1664]{1,0:T(8,128)(2,1)} %get-tuple-element.101), channel_id=1, source_target_pairs={{0,16},{1,17},{2,18},{3,19},{4,20},{5,21},{6,22},{7,23},{8,24},{9,... | collective-permute-start | bytes 159752 | tf_op jit(solution)/shard_map/ppermute | solution.py:959
  7.5 5.2 %collective-permute-start = (bf16[16,1664]{1,0:T(8,128)(2,1)}, bf16[16,1664]{1,0:T(8,128)(2,1)S(1)}, u32[]{:S(2)}, u32[]{:S(2)}) collective-permute-start(bf16[16,1664]{1,0:T(8,128)(2,1)} %get-tuple-element.101), channel_id=1, source_target_pairs={{0,8},{1,9},{2,10},{3,11},{4,12},{5,13},{6,14},{7,15},{8,0},{9,1},... | collective-permute-start | bytes 159752 | tf_op jit(solution)/shard_map/ppermute | solution.py:959
  8.1 12.0 %collective-permute-start.8 = (bf16[16,4608]{1,0:T(8,128)(2,1)}, bf16[16,4608]{1,0:T(8,128)(2,1)S(1)}, u32[]{:S(2)}, u32[]{:S(2)}) collective-permute-start(bf16[16,4608]{1,0:T(8,128)(2,1)} %get-tuple-element.107), channel_id=1, source_target_pairs={{0,24},{1,25},{2,26},{3,27},{4,28},{5,29},{6,30},{7,31},{8,16},{9,... | collective-permute-start | bytes 442376 | tf_op jit(solution)/shard_map/ppermute | solution.py:959
  16.5 18.2 %copy-start.24 = (bf16[64,1664]{1,0:T(8,128)(2,1)}, bf16[64,1664]{1,0:T(8,128)(2,1)S(1)}, u32[]{:S(2)}) copy-start(bf16[64,1664]{1,0:T(8,128)(2,1)S(1)} %constant_dynamic-update-slice_fusion.refs_0_) | copy-start | bytes 638980
  16.5 10.5 %collective-permute-start.5 = (bf16[64,1664]{1,0:T(8,128)(2,1)S(1)}, bf16[64,1664]{1,0:T(8,128)(2,1)S(1)}, u32[]{:S(2)}, u32[]{:S(2)}) collective-permute-start(bf16[64,1664]{1,0:T(8,128)(2,1)S(1)} %constant_dynamic-update-slice_fusion.refs_0_), channel_id=1, source_target_pairs={{0,5},{1,4},{2,7},{3,6},{4,1},{5,0},{6,3},{7,2},{8,13},{9,12},{10,... | collective-permute-start | bytes 638984 | tf_op jit(solution)/shard_map/ppermute | solution.py:959
  19.1 8.0 %collective-permute-start.4 = (bf16[64,1664]{1,0:T(8,128)(2,1)S(1)}, bf16[64,1664]{1,0:T(8,128)(2,1)S(1)}, u32[]{:S(2)}, u32[]{:S(2)}) collective-permute-start(bf16[64,1664]{1,0:T(8,128)(2,1)S(1)} %constant_dynamic-update-slice_fusion.refs_0_), channel_id=1, source_target_pairs={{0,1},{1,0},{2,3},{3,2},{4,5},{5,4},{6,7},{7,6},{8,9},{9,8},{10,11... | collective-permute-start | bytes 638984 | tf_op jit(solution)/shard_map/ppermute | solution.py:959
  19.6 7.5 %collective-permute-start.3 = (bf16[64,1664]{1,0:T(8,128)(2,1)S(1)}, bf16[64,1664]{1,0:T(8,128)(2,1)S(1)}, u32[]{:S(2)}, u32[]{:S(2)}) collective-permute-start(bf16[64,1664]{1,0:T(8,128)(2,1)S(1)} %constant_dynamic-update-slice_fusion.refs_0_), channel_id=1, source_target_pairs={{0,4},{1,5},{2,6},{3,7},{4,0},{5,1},{6,2},{7,3},{8,12},{9,13},{10,... | collective-permute-start | bytes 638984 | tf_op jit(solution)/shard_map/ppermute | solution.py:959
  20.1 6.4 %collective-permute-start.7 = (bf16[16,4608]{1,0:T(8,128)(2,1)}, bf16[16,4608]{1,0:T(8,128)(2,1)S(1)}, u32[]{:S(2)}, u32[]{:S(2)}) collective-permute-start(bf16[16,4608]{1,0:T(8,128)(2,1)} %get-tuple-element.107), channel_id=1, source_target_pairs={{0,16},{1,17},{2,18},{3,19},{4,20},{5,21},{6,22},{7,23},{8,24},{9,... | collective-permute-start | bytes 442376 | tf_op jit(solution)/shard_map/ppermute | solution.py:959
  20.1 6.9 %collective-permute-start.6 = (bf16[16,4608]{1,0:T(8,128)(2,1)}, bf16[16,4608]{1,0:T(8,128)(2,1)S(1)}, u32[]{:S(2)}, u32[]{:S(2)}) collective-permute-start(bf16[16,4608]{1,0:T(8,128)(2,1)} %get-tuple-element.107), channel_id=1, source_target_pairs={{0,8},{1,9},{2,10},{3,11},{4,12},{5,13},{6,14},{7,15},{8,0},{9,1},... | collective-permute-start | bytes 442376 | tf_op jit(solution)/shard_map/ppermute | solution.py:959
  28.2 26.7 %copy-start.17 = (bf16[64,4608]{1,0:T(8,128)(2,1)}, bf16[64,4608]{1,0:T(8,128)(2,1)S(1)}, u32[]{:S(2)}) copy-start(bf16[64,4608]{1,0:T(8,128)(2,1)S(1)} %pad_maximum_fusion.refs_0_) | copy-start | bytes 1769476
  28.2 4.1 %collective-permute-start.9 = (bf16[64,1664]{1,0:T(8,128)(2,1)S(1)}, bf16[64,1664]{1,0:T(8,128)(2,1)S(1)}, u32[]{:S(2)}, u32[]{:S(2)}) collective-permute-start(bf16[64,1664]{1,0:T(8,128)(2,1)S(1)} %constant_dynamic-update-slice_fusion.refs_0_), channel_id=1, source_target_pairs={{0,2},{1,3},{2,0},{3,1},{4,6},{5,7},{6,4},{7,5},{8,10},{9,11},{10,... | collective-permute-start | bytes 638984 | tf_op jit(solution)/shard_map/ppermute | solution.py:959
  28.3 4.0 %collective-permute-start.10 = (bf16[64,1664]{1,0:T(8,128)(2,1)S(1)}, bf16[64,1664]{1,0:T(8,128)(2,1)S(1)}, u32[]{:S(2)}, u32[]{:S(2)}) collective-permute-start(bf16[64,1664]{1,0:T(8,128)(2,1)S(1)} %collective-permute-done.3.refs_1_), channel_id=1, source_target_pairs={{0,2},{1,3},{2,0},{3,1},{4,6},{5,7},{6,4},{7,5},{8,10},{9,11},{10,... | collective-permute-start | bytes 638984 | tf_op jit(solution)/shard_map/ppermute | solution.py:959
  28.8 26.1 %collective-permute-start.15 = (bf16[64,4608]{1,0:T(8,128)(2,1)S(1)}, bf16[64,4608]{1,0:T(8,128)(2,1)S(1)}, u32[]{:S(2)}, u32[]{:S(2)}) collective-permute-start(bf16[64,4608]{1,0:T(8,128)(2,1)S(1)} %pad_maximum_fusion.refs_0_), channel_id=1, source_target_pairs={{0,5},{1,4},{2,7},{3,6},{4,1},{5,0},{6,3},{7,2},{8,13},{9,12},{10,... | collective-permute-start | bytes 1769480 | tf_op jit(solution)/shard_map/ppermute | solution.py:959
  31.2 26.4 %collective-permute-start.14 = (bf16[64,4608]{1,0:T(8,128)(2,1)S(1)}, bf16[64,4608]{1,0:T(8,128)(2,1)S(1)}, u32[]{:S(2)}, u32[]{:S(2)}) collective-permute-start(bf16[64,4608]{1,0:T(8,128)(2,1)S(1)} %pad_maximum_fusion.refs_0_), channel_id=1, source_target_pairs={{0,1},{1,0},{2,3},{3,2},{4,5},{5,4},{6,7},{7,6},{8,9},{9,8},{10,11... | collective-permute-start | bytes 1769480 | tf_op jit(solution)/shard_map/ppermute | solution.py:959
  31.7 26.0 %collective-permute-start.13 = (bf16[64,4608]{1,0:T(8,128)(2,1)S(1)}, bf16[64,4608]{1,0:T(8,128)(2,1)S(1)}, u32[]{:S(2)}, u32[]{:S(2)}) collective-permute-start(bf16[64,4608]{1,0:T(8,128)(2,1)S(1)} %pad_maximum_fusion.refs_0_), channel_id=1, source_target_pairs={{0,4},{1,5},{2,6},{3,7},{4,0},{5,1},{6,2},{7,3},{8,12},{9,13},{10,... | collective-permute-start | bytes 1769480 | tf_op jit(solution)/shard_map/ppermute | solution.py:959
  32.3 1.6 collective-permute-start.11
  32.3 1.7 %collective-permute-start.12 = (bf16[64,1664]{1,0:T(8,128)(2,1)S(1)}, bf16[64,1664]{1,0:T(8,128)(2,1)S(1)}, u32[]{:S(2)}, u32[]{:S(2)}) collective-permute-start(bf16[64,1664]{1,0:T(8,128)(2,1)S(1)} %collective-permute-done.5.refs_3_), channel_id=1, source_target_pairs={{0,2},{1,3},{2,0},{3,1},{4,6},{5,7},{6,4},{7,5},{8,10},{9,11},{10,... | collective-permute-start | bytes 638984 | tf_op jit(solution)/shard_map/ppermute | solution.py:959
  33.9 24.4 %collective-permute-start.16 = (bf16[64,4608]{1,0:T(8,128)(2,1)S(1)}, bf16[64,4608]{1,0:T(8,128)(2,1)S(1)}, u32[]{:S(2)}, u32[]{:S(2)}) collective-permute-start(bf16[64,4608]{1,0:T(8,128)(2,1)S(1)} %pad_maximum_fusion.refs_0_), channel_id=1, source_target_pairs={{0,2},{1,3},{2,0},{3,1},{4,6},{5,7},{6,4},{7,5},{8,10},{9,11},{10,... | collective-permute-start | bytes 1769480 | tf_op jit(solution)/shard_map/ppermute | solution.py:959
  57.7 2.0 %collective-permute-start.17 = (bf16[64,4608]{1,0:T(8,128)(2,1)S(1)}, bf16[64,4608]{1,0:T(8,128)(2,1)S(1)}, u32[]{:S(2)}, u32[]{:S(2)}) collective-permute-start(bf16[64,4608]{1,0:T(8,128)(2,1)S(1)} %collective-permute-done.13.refs_1_), channel_id=1, source_target_pairs={{0,2},{1,3},{2,0},{3,1},{4,6},{5,7},{6,4},{7,5},{8,10},{9,11},{10,... | collective-permute-start | bytes 1769480 | tf_op jit(solution)/shard_map/ppermute | solution.py:959
  57.8 2.8 %collective-permute-start.18 = (bf16[64,4608]{1,0:T(8,128)(2,1)S(1)}, bf16[64,4608]{1,0:T(8,128)(2,1)S(1)}, u32[]{:S(2)}, u32[]{:S(2)}) collective-permute-start(bf16[64,4608]{1,0:T(8,128)(2,1)S(1)} %collective-permute-done.14.refs_2_), channel_id=1, source_target_pairs={{0,2},{1,3},{2,0},{3,1},{4,6},{5,7},{6,4},{7,5},{8,10},{9,11},{10,... | collective-permute-start | bytes 1769480 | tf_op jit(solution)/shard_map/ppermute | solution.py:959
  58.3 3.2 %collective-permute-start.19 = (bf16[64,4608]{1,0:T(8,128)(2,1)S(1)}, bf16[64,4608]{1,0:T(8,128)(2,1)S(1)}, u32[]{:S(2)}, u32[]{:S(2)}) collective-permute-start(bf16[64,4608]{1,0:T(8,128)(2,1)S(1)} %collective-permute-done.15.refs_3_), channel_id=1, source_target_pairs={{0,2},{1,3},{2,0},{3,1},{4,6},{5,7},{6,4},{7,5},{8,10},{9,11},{10,... | collective-permute-start | bytes 1769480 | tf_op jit(solution)/shard_map/ppermute | solution.py:959
  62.3 42.5 %slice-start = ((s8[6291456]{0:T(1024)(128)(4,1)}), s8[4194304]{0:T(1024)(128)(4,1)S(1)}, s32[]{:S(2)}) async-start(s8[6291456]{0:T(1024)(128)(4,1)} %bitcast.3), calls=%async_computation | async-start | bytes 8388608
  62.3 42.5 %slice-start.1 = ((s8[6291456]{0:T(1024)(128)(4,1)}), s8[2097152]{0:T(1024)(128)(4,1)S(1)}, s32[]{:S(2)}) async-start(s8[6291456]{0:T(1024)(128)(4,1)} %bitcast.3), calls=%async_computation.1 | async-start | bytes 4194304
  62.3 42.5 %copy-start.1 = (f32[2048,256]{1,0:T(8,128)S(1)}, f32[2048,256]{1,0:T(8,128)}, u32[]{:S(2)}) copy-start(f32[2048,256]{1,0:T(8,128)} %get-tuple-element.116.prob_ref._) | copy-start | bytes 6291460
  62.3 42.5 %copy-start.15 = (s32[4,2]{0,1:T(2,128)S(1)}, s32[4,2]{0,1:T(2,128)}, u32[]{:S(2)}) copy-start(s32[4,2]{0,1:T(2,128)} %param.21) | copy-start | bytes 100
  104.6 6.6 %collective-permute-start.20 = (bf16[256,4608]{1,0:T(8,128)(2,1)}, bf16[256,4608]{1,0:T(8,128)(2,1)S(1)}, u32[]{:S(2)}, u32[]{:S(2)}) collective-permute-start(bf16[256,4608]{1,0:T(8,128)(2,1)} %get-tuple-element.127), channel_id=1, source_target_pairs={{0,2},{1,3},{2,0},{3,1},{4,6},{5,7},{6,4},{7,5},{8,10},{9,11},{10,... | collective-permute-start | bytes 7077896 | tf_op jit(solution)/shard_map/ppermute | solution.py:959
  111.8 16.9 %copy-start = (bf16[2048,512]{1,0:T(8,128)(2,1)S(1)}, bf16[2048,512]{1,0:T(8,128)(2,1)}, u32[]{:S(2)}) copy-start(bf16[2048,512]{1,0:T(8,128)(2,1)} %refs_5_.3) | copy-start | bytes 6291460
  111.8 30.4 %collective-permute-start.21 = (bf16[64,4608]{1,0:T(8,128)(2,1)S(1)}, bf16[64,4608]{1,0:T(8,128)(2,1)S(1)}, u32[]{:S(2)}, u32[]{:S(2)}) collective-permute-start(bf16[64,4608]{1,0:T(8,128)(2,1)S(1)} %get-tuple-element.139), channel_id=1, source_target_pairs={{0,4},{1,5},{2,6},{3,7},{4,0},{5,1},{6,2},{7,3},{8,12},{9,13},{10,... | collective-permute-start | bytes 1769480 | tf_op jit(solution)/shard_map/ppermute | solution.py:959
  113.4 28.8 %collective-permute-start.22 = (bf16[64,4608]{1,0:T(8,128)(2,1)S(1)}, bf16[64,4608]{1,0:T(8,128)(2,1)S(1)}, u32[]{:S(2)}, u32[]{:S(2)}) collective-permute-start(bf16[64,4608]{1,0:T(8,128)(2,1)S(1)} %get-tuple-element.140), channel_id=1, source_target_pairs={{0,1},{1,0},{2,3},{3,2},{4,5},{5,4},{6,7},{7,6},{8,9},{9,8},{10,11... | collective-permute-start | bytes 1769480 | tf_op jit(solution)/shard_map/ppermute | solution.py:959
  114.1 28.1 %collective-permute-start.23 = (bf16[64,4608]{1,0:T(8,128)(2,1)S(1)}, bf16[64,4608]{1,0:T(8,128)(2,1)S(1)}, u32[]{:S(2)}, u32[]{:S(2)}) collective-permute-start(bf16[64,4608]{1,0:T(8,128)(2,1)S(1)} %get-tuple-element.141), channel_id=1, source_target_pairs={{0,5},{1,4},{2,7},{3,6},{4,1},{5,0},{6,3},{7,2},{8,13},{9,12},{10,... | collective-permute-start | bytes 1769480 | tf_op jit(solution)/shard_map/ppermute | solution.py:959
  134.5 28.4 %copy-start.9 = (bf16[2048,512]{1,0:T(8,128)(2,1)S(1)}, bf16[2048,512]{1,0:T(8,128)(2,1)}, u32[]{:S(2)}) copy-start(bf16[2048,512]{1,0:T(8,128)(2,1)} %get-tuple-element.158.refs_2_) | copy-start | bytes 6291460
  134.5 28.4 %copy-start.10 = (bf16[2048,512]{1,0:T(8,128)(2,1)S(1)}, bf16[2048,512]{1,0:T(8,128)(2,1)}, u32[]{:S(2)}) copy-start(bf16[2048,512]{1,0:T(8,128)(2,1)} %get-tuple-element.159.refs_3_) | copy-start | bytes 6291460
  134.5 28.4 %copy-start.11 = (bf16[2048,512]{1,0:T(8,128)(2,1)S(1)}, bf16[2048,512]{1,0:T(8,128)(2,1)}, u32[]{:S(2)}) copy-start(bf16[2048,512]{1,0:T(8,128)(2,1)} %get-tuple-element.161.refs_7_) | copy-start | bytes 6291460
  134.5 28.4 %copy-start.12 = (bf16[512,512]{1,0:T(8,128)(2,1)S(1)}, bf16[512,512]{1,0:T(8,128)(2,1)}, u32[]{:S(2)}) copy-start(bf16[512,512]{1,0:T(8,128)(2,1)} %get-tuple-element.160.refs_6_) | copy-start | bytes 1572868
  142.2 2.4 %collective-permute-start.24 = (bf16[256,1664]{1,0:T(8,128)(2,1)S(1)}, bf16[256,1664]{1,0:T(8,128)(2,1)S(1)}, u32[]{:S(2)}, u32[]{:S(2)}) collective-permute-start(bf16[256,1664]{1,0:T(8,128)(2,1)S(1)} %get-tuple-element.143), channel_id=1, source_target_pairs={{0,2},{1,3},{2,0},{3,1},{4,6},{5,7},{6,4},{7,5},{8,10},{9,11},{10,... | collective-permute-start | bytes 2555912 | tf_op jit(solution)/shard_map/ppermute | solution.py:959
  144.7 18.2 %copy-start.7 = (bf16[2048,512]{1,0:T(8,128)(2,1)S(1)}, bf16[2048,512]{1,0:T(8,128)(2,1)}, u32[]{:S(2)}) copy-start(bf16[2048,512]{1,0:T(8,128)(2,1)} %get-tuple-element.156.refs_0_) | copy-start | bytes 6291460
  144.7 18.2 %copy-start.8 = (bf16[2048,512]{1,0:T(8,128)(2,1)S(1)}, bf16[2048,512]{1,0:T(8,128)(2,1)}, u32[]{:S(2)}) copy-start(bf16[2048,512]{1,0:T(8,128)(2,1)} %get-tuple-element.157.refs_1_) | copy-start | bytes 6291460
  144.9 18.1 %copy-start.6 = (bf16[2048,512]{1,0:T(8,128)(2,1)S(1)}, bf16[2048,512]{1,0:T(8,128)(2,1)}, u32[]{:S(2)}) copy-start(bf16[2048,512]{1,0:T(8,128)(2,1)} %get-tuple-element.119.ctx_ref.refs_4_) | copy-start | bytes 6291460
  144.9 9.1 %collective-permute-start.27 = (bf16[64,1664]{1,0:T(8,128)(2,1)S(1)}, bf16[64,1664]{1,0:T(8,128)(2,1)S(1)}, u32[]{:S(2)}, u32[]{:S(2)}) collective-permute-start(bf16[64,1664]{1,0:T(8,128)(2,1)S(1)} %get-tuple-element.195), channel_id=1, source_target_pairs={{0,5},{1,4},{2,7},{3,6},{4,1},{5,0},{6,3},{7,2},{8,13},{9,12},{10,... | collective-permute-start | bytes 638984 | tf_op jit(solution)/shard_map/ppermute | solution.py:959
  146.7 11.0 %collective-permute-start.26 = (bf16[64,1664]{1,0:T(8,128)(2,1)S(1)}, bf16[64,1664]{1,0:T(8,128)(2,1)S(1)}, u32[]{:S(2)}, u32[]{:S(2)}) collective-permute-start(bf16[64,1664]{1,0:T(8,128)(2,1)S(1)} %get-tuple-element.196), channel_id=1, source_target_pairs={{0,1},{1,0},{2,3},{3,2},{4,5},{5,4},{6,7},{7,6},{8,9},{9,8},{10,11... | collective-permute-start | bytes 638984 | tf_op jit(solution)/shard_map/ppermute | solution.py:959
  147.9 9.9 %collective-permute-start.25 = (bf16[64,1664]{1,0:T(8,128)(2,1)S(1)}, bf16[64,1664]{1,0:T(8,128)(2,1)S(1)}, u32[]{:S(2)}, u32[]{:S(2)}) collective-permute-start(bf16[64,1664]{1,0:T(8,128)(2,1)S(1)} %get-tuple-element.197), channel_id=1, source_target_pairs={{0,4},{1,5},{2,6},{3,7},{4,0},{5,1},{6,2},{7,3},{8,12},{9,13},{10,... | collective-permute-start | bytes 638984 | tf_op jit(solution)/shard_map/ppermute | solution.py:959
  149.4 11.9 %collective-permute-start.33 = (bf16[16,4608]{1,0:T(8,128)(2,1)S(1)}, bf16[16,4608]{1,0:T(8,128)(2,1)S(1)}, u32[]{:S(2)}, u32[]{:S(2)}) collective-permute-start(bf16[16,4608]{1,0:T(8,128)(2,1)S(1)} %get-tuple-element.190), channel_id=1, source_target_pairs={{0,24},{1,25},{2,26},{3,27},{4,28},{5,29},{6,30},{7,31},{8,16},{9,... | collective-permute-start | bytes 442376 | tf_op jit(solution)/shard_map/ppermute | solution.py:959
  151.7 18.2 %collective-permute-start.32 = (bf16[16,4608]{1,0:T(8,128)(2,1)S(1)}, bf16[16,4608]{1,0:T(8,128)(2,1)S(1)}, u32[]{:S(2)}, u32[]{:S(2)}) collective-permute-start(bf16[16,4608]{1,0:T(8,128)(2,1)S(1)} %get-tuple-element.191), channel_id=1, source_target_pairs={{0,16},{1,17},{2,18},{3,19},{4,20},{5,21},{6,22},{7,23},{8,24},{9,... | collective-permute-start | bytes 442376 | tf_op jit(solution)/shard_map/ppermute | solution.py:959
  154.0 15.9 %collective-permute-start.31 = (bf16[16,4608]{1,0:T(8,128)(2,1)S(1)}, bf16[16,4608]{1,0:T(8,128)(2,1)S(1)}, u32[]{:S(2)}, u32[]{:S(2)}) collective-permute-start(bf16[16,4608]{1,0:T(8,128)(2,1)S(1)} %get-tuple-element.192), channel_id=1, source_target_pairs={{0,8},{1,9},{2,10},{3,11},{4,12},{5,13},{6,14},{7,15},{8,0},{9,1},... | collective-permute-start | bytes 442376 | tf_op jit(solution)/shard_map/ppermute | solution.py:959
  158.5 11.4 %collective-permute-start.28 = (bf16[16,1664]{1,0:T(8,128)(2,1)S(1)}, bf16[16,1664]{1,0:T(8,128)(2,1)S(1)}, u32[]{:S(2)}, u32[]{:S(2)}) collective-permute-start(bf16[16,1664]{1,0:T(8,128)(2,1)S(1)} %get-tuple-element.149), channel_id=1, source_target_pairs={{0,8},{1,9},{2,10},{3,11},{4,12},{5,13},{6,14},{7,15},{8,0},{9,1},... | collective-permute-start | bytes 159752 | tf_op jit(solution)/shard_map/ppermute | solution.py:959
  158.6 11.4 %collective-permute-start.29 = (bf16[16,1664]{1,0:T(8,128)(2,1)S(1)}, bf16[16,1664]{1,0:T(8,128)(2,1)S(1)}, u32[]{:S(2)}, u32[]{:S(2)}) collective-permute-start(bf16[16,1664]{1,0:T(8,128)(2,1)S(1)} %get-tuple-element.150), channel_id=1, source_target_pairs={{0,16},{1,17},{2,18},{3,19},{4,20},{5,21},{6,22},{7,23},{8,24},{9,... | collective-permute-start | bytes 159752 | tf_op jit(solution)/shard_map/ppermute | solution.py:959
  161.3 8.6 %collective-permute-start.30 = (bf16[16,1664]{1,0:T(8,128)(2,1)S(1)}, bf16[16,1664]{1,0:T(8,128)(2,1)S(1)}, u32[]{:S(2)}, u32[]{:S(2)}) collective-permute-start(bf16[16,1664]{1,0:T(8,128)(2,1)S(1)} %get-tuple-element.151), channel_id=1, source_target_pairs={{0,24},{1,25},{2,26},{3,27},{4,28},{5,29},{6,30},{7,31},{8,16},{9,... | collective-permute-start | bytes 159752 | tf_op jit(solution)/shard_map/ppermute | solution.py:959
  (26 other events, 125.7 us)

commit v2 on v1

--- a/solution.py
+++ b/solution.py
@@ -715,7 +715,7 @@
 
 
 def output_kernel(*refs):
-    gelu_refs, (ctx_ref, tok_ref, wp_ref, wd_ref, vec_ref, out_ref) = refs[:4], refs[4:]
+    gelu_refs, (ctx_ref, tok_ref, wp_ref, wd_ref, vec_ref, _, out_ref) = refs[:4], refs[4:]
     tile, width = tok_ref.shape
     half = width // 2
     bias = vec_ref[6:7, :] + vec_ref[7:8, :]
@@ -903,19 +903,23 @@
     )(gqn, tokens, gmid, w_qkv, vec)
 
 
-def output(gelu, ctx, tokens, wp, wd, vec, tile=512):
+def output(gelu, ctx, tokens, wp, wd, vec, into, start, count, tile=512):
     n, width = tokens.shape
+
+    def spec(cols):
+        return pl.BlockSpec((tile, cols), lambda i: (i + start, 0))
+
     return pl.pallas_call(
         output_kernel,
-        grid=(n // tile,),
-        in_specs=[rows_spec(tile, width)] * 6
-        + [whole_spec(x.shape) for x in (wp, wd, vec)],
-        out_specs=rows_spec(tile, width),
+        grid=(count,),
+        in_specs=[spec(width)] * 6 + [whole_spec(x.shape) for x in (wp, wd, vec)] + [ANY_SPEC],
+        out_specs=spec(width),
         out_shape=struct((n, width), BF16),
+        input_output_aliases={} if into is None else {9: 0},
         compiler_params=params(24),
         cost_estimate=cost(1000000000, n * width),
         name="output",
-    )(*gelu, ctx, tokens, wp, wd, vec)
+    )(*gelu, ctx, tokens, wp, wd, vec, ctx if into is None else into)
 
 
 def finish_kernel(*refs):
@@ -949,7 +953,7 @@
             struct((4 * UNIT, width), F32),
             *[struct((UNIT,), F32)] * 8, struct((4 * UNIT,), F32), struct((HEADS, RELS), F32),
         ],
-        compiler_params=pltpu.CompilerParams(vmem_limit_bytes=60 * 1024 * 1024),
+        compiler_params=pltpu.CompilerParams(vmem_limit_bytes=16 * 1024 * 1024),
         name="finish",
     )(*first, *second)
 
@@ -1041,7 +1045,8 @@
     gqn, gpos_b = attend_back(shifts, q, prob, gctx, gqn, 2, 2)
     (gfirst,) = project_back(gqn, tokens, w_qkv, small, gpos_a, gpos_b, False)
     gtok = token_back(gqn, tokens, gmid, w_qkv, vec)
-    out = output(gelu, ctx, tokens, wp, wd, vec)
+    out = output(gelu, ctx, tokens, wp, wd, vec, None, 0, 2)
+    out = output(gelu, ctx, tokens, wp, wd, vec, out, 2, 2)
     width = 512
     e = gfirst[:, 1536:]
     mats = [gfirst[:, :1536], gsecond[:, :width], gsecond[:, width : 5 * width], by_row(gsecond[:, 5 * width :].reshape(-1, 4, width))]
@@ -1064,7 +1069,6 @@
         first = spread_far(first, COLUMN)
         second = spread_far(second, COLUMN)
         first = spread_far(jnp.concatenate(first), PLANE)
-        first, second = lax.optimization_barrier((first, second))
         first, second = lax.optimization_barrier((first, jnp.concatenate(second)))
         second = spread_far(second, PLANE)
         first = spread_core(first)
@@ -1091,10 +1095,16 @@
     if stepped:
         gfirst, gsecond = lax.optimization_barrier((gfirst, gsecond))
         gsecond = meet_far(add_blocks(gsecond), COLUMN)
-        gfirst = meet_far(meet_core(*gfirst), PLANE)
-        gfirst, gelu = lax.optimization_barrier((add_blocks(gfirst), gelu))
+        gfirst = meet_core(*gfirst)
+        gfirst, gelu = lax.optimization_barrier((gfirst, gelu))
+        gfirst = meet_far(gfirst, PLANE)
+    tiles = tokens.shape[0] // 512
+    out = output(gelu, ctx, tokens, wp, wd, vec, None, 0, tiles // 2)
+    if stepped:
+        gfirst, out = lax.optimization_barrier((gfirst, out))
+        gfirst, out = lax.optimization_barrier((add_blocks(gfirst), out))
         gfirst = meet_far(gfirst, COLUMN)
-    out = output(gelu, ctx, tokens, wp, wd, vec)
+    out = output(gelu, ctx, tokens, wp, wd, vec, out, tiles // 2, tiles - tiles // 2)
     if stepped:
         gfirst, gsecond, out = lax.optimization_barrier((gfirst, gsecond, out))
         grads = finish(gfirst, gsecond)

time: 173 us -> 169 us (0.977)
  waiting for transfers between devices: 24.7 us -> 21.5 us
    ppermute x34, waiting for transfers between devices: 24.7 us -> 21.5 us  [exchange(): return lax.ppermute(x, AXES, [(i, i ^ mask) for i in range(size)])]
    pallas_call x1 -> x2, Pallas kernels: 6.92 us -> 7.7 us  [output(): pl.pallas_call(output_kernel, grid=(count,), in_specs=[spec(width)] * 6 +...]
    unnamed x83 -> x71, local copies, waits for them, and re-layouts: 5.05 us -> 4.33 us
  transfers between devices with their start and end apart: 34 -> 34, of which waited for: 13 -> 14; matrix products, arithmetic and copies ran while one was open for 1% -> 1% of each run, Pallas kernels for 34% -> 35%
where the time goes in v2:
time: 169 us
  Pallas kernels  104 us (62%)
  starting transfers between devices  35.4 us (21%)
  waiting for transfers between devices  21.5 us (13%)
  local copies, waits for them, and re-layouts  4.34 us (3%)
  other arithmetic  2.09 us (1%)
    pallas_call x1, Pallas kernels, mlp(): pl.pallas_call(functools.partial(mlp_kernel, masks, relative), grid=(n //...  42.3 us
    ppermute x34, starting transfers between devices, exchange(): return lax.ppermute(x, AXES, [(i, i ^ mask) for i in range(size)])  35.4 us
    ppermute x34, waiting for transfers between devices, exchange(): return lax.ppermute(x, AXES, [(i, i ^ mask) for i in range(size)])  21.5 us
    pallas_call x1, Pallas kernels, attend(): pl.pallas_call(functools.partial(attend_kernel, masks), grid=(n // PATCHE...  20.1 us
    pallas_call x2, Pallas kernels, attend_back(): pl.pallas_call(functools.partial(attend_back_kernel, start), grid=(clips,...  18 us
    pallas_call x2, Pallas kernels, output(): pl.pallas_call(output_kernel, grid=(count,), in_specs=[spec(width)] * 6 +...  7.7 us
    pallas_call x1, Pallas kernels, project_back(): pl.pallas_call(functools.partial(project_back_kernel, relative), grid=(n...  7.64 us
    pallas_call x1, Pallas kernels, token_back(): pl.pallas_call(token_back_kernel, grid=(n // tile,), in_specs=[rows_spec(...  5.8 us
  transfers between devices with their start and end apart: 34, of which 14 were waited for; matrix products, arithmetic and copies ran while one was open for 1% of the time, Pallas kernels for 35%

profile of v2, /device:TPU:0, one launch (start us, length us, event | category | flops | bytes accessed | tf_op | source)
XLA Modules:
  0.0 168.8 jit_solution(16972283282913503246)
XLA Ops:
  0.7 1.8 %pack.1 = (bf16[16,1664]{1,0:T(8,128)(2,1)}, bf16[16,4608]{1,0:T(8,128)(2,1)}) custom-call(bf16[16]{0:T(256)(128)(2,1)} %refs_0_.1, bf16[16]{0:T(256)(128)(2,1)} %refs_1_.1, bf16[16]{0:T(256)(128)(2,1)} %refs_2_.1, bf16[16]{0:T(256)(128)(2,1)} %refs_3_.1, bf16[16]{0:T(256)(128)(2,1)} %refs_4_.1, bf16[16]{0:T(256)(128)(2,1)} %refs_5_.3, ...), custom_call_target="tpu_custom_call" | custom-call | tf_op jit(solution)/shard_map/pack/pallas_call | solution.py:253
  2.4 5.0 %collective-permute-start.2 = (bf16[16,1664]{1,0:T(8,128)(2,1)}, bf16[16,1664]{1,0:T(8,128)(2,1)S(1)}, u32[]{:S(2)}, u32[]{:S(2)}) collective-permute-start(bf16[16,1664]{1,0:T(8,128)(2,1)} %get-tuple-element.103), channel_id=1, source_target_pairs={{0,24},{1,25},{2,26},{3,27},{4,28},{5,29},{6,30},{7,31},{8,16},{9,... | collective-permute-start | bytes 159752 | tf_op jit(solution)/shard_map/ppermute | solution.py:963
  7.5 0.6 collective-permute-start
  8.1 3.8 %collective-permute-start.8 = (bf16[16,4608]{1,0:T(8,128)(2,1)}, bf16[16,4608]{1,0:T(8,128)(2,1)S(1)}, u32[]{:S(2)}, u32[]{:S(2)}) collective-permute-start(bf16[16,4608]{1,0:T(8,128)(2,1)} %get-tuple-element.104), channel_id=1, source_target_pairs={{0,24},{1,25},{2,26},{3,27},{4,28},{5,29},{6,30},{7,31},{8,16},{9,... | collective-permute-start | bytes 442376 | tf_op jit(solution)/shard_map/ppermute | solution.py:963
  11.9 0.8 constant_dynamic-update-slice_fusion.3
  12.7 0.9 collective-permute-start.6
  13.6 4.6 %collective-permute-done.1 = bf16[16,1664]{1,0:T(8,128)(2,1)S(1)} collective-permute-done((bf16[16,1664]{1,0:T(8,128)(2,1)}, bf16[16,1664]{1,0:T(8,128)(2,1)S(1)}, u32[]{:S(2)}, u32[]{:S(2)}) %collective-permute-start.1) | collective-permute-done | bytes 53280 | tf_op jit(solution)/shard_map/ppermute | solution.py:963
  18.2 2.5 %collective-permute-start.5 = (bf16[64,1664]{1,0:T(8,128)(2,1)S(1)}, bf16[64,1664]{1,0:T(8,128)(2,1)S(1)}, u32[]{:S(2)}, u32[]{:S(2)}) collective-permute-start(bf16[64,1664]{1,0:T(8,128)(2,1)S(1)} %constant_dynamic-update-slice_fusion.refs_0_), channel_id=1, source_target_pairs={{0,5},{1,4},{2,7},{3,6},{4,1},{5,0},{6,3},{7,2},{8,13},{9,12},{10,... | collective-permute-start | bytes 638984 | tf_op jit(solution)/shard_map/ppermute | solution.py:963
  21.2 0.5 collective-permute-start.3
  21.8 3.3 %collective-permute-done.7 = bf16[16,4608]{1,0:T(8,128)(2,1)S(1)} collective-permute-done((bf16[16,4608]{1,0:T(8,128)(2,1)}, bf16[16,4608]{1,0:T(8,128)(2,1)S(1)}, u32[]{:S(2)}, u32[]{:S(2)}) %collective-permute-start.7) | collective-permute-done | bytes 147488 | tf_op jit(solution)/shard_map/ppermute | solution.py:963
  25.1 0.9 pad_maximum_fusion.refs_0_
  26.1 1.2 collective-permute-done.4.refs_2_
  27.9 2.0 %collective-permute-start.15 = (bf16[64,4608]{1,0:T(8,128)(2,1)S(1)}, bf16[64,4608]{1,0:T(8,128)(2,1)S(1)}, u32[]{:S(2)}, u32[]{:S(2)}) collective-permute-start(bf16[64,4608]{1,0:T(8,128)(2,1)S(1)} %pad_maximum_fusion.refs_0_), channel_id=1, source_target_pairs={{0,5},{1,4},{2,7},{3,6},{4,1},{5,0},{6,3},{7,2},{8,13},{9,12},{10,... | collective-permute-start | bytes 1769480 | tf_op jit(solution)/shard_map/ppermute | solution.py:963
  29.9 1.0 collective-permute-start.14
  32.2 0.8 collective-permute-done.11.refs_6_
  33.2 0.7 copy-done.31
  33.9 20.1 %attend.1 = (bf16[2048,1536]{1,0:T(8,128)(2,1)}, f32[2048,256]{1,0:T(8,128)}, bf16[2048,512]{1,0:T(8,128)(2,1)}, bf16[512,1664]{1,0:T(8,128)(2,1)}, f32[16,512]{1,0:T(8,128)}) custom-call(s32[2,4]{1,0:T(2,128)} %bitcast.5, s32[4]{0:T(128)} %count_ref.1, bf16[2048,512]{1,0:T(8,128)(2,1)} %refs_5_.5, bf16[16,49]{1,0:T(8,128)(2,1)} %bitcast.9, ...), custom_call_target="tpu_custom_call" | custom-call | flops 2800000000 | bytes 1048576 | tf_op jit(solution)/shard_map/attend/pallas_call | solution.py:762
  54.0 2.7 %collective-permute-done.14.refs_2_ = bf16[64,4608]{1,0:T(8,128)(2,1)S(1)} collective-permute-done((bf16[64,4608]{1,0:T(8,128)(2,1)S(1)}, bf16[64,4608]{1,0:T(8,128)(2,1)S(1)}, u32[]{:S(2)}, u32[]{:S(2)}) %collective-permute-start.14) | collective-permute-done | bytes 589856 | tf_op jit(solution)/shard_map/ppermute | solution.py:963
  57.4 1.4 collective-permute-done.17.refs_5_
  58.9 0.8 collective-permute-done.18.refs_6_
  59.7 0.8 collective-permute-done.19.refs_7_
  60.6 0.8 copy-done.25
  61.4 42.3 %mlp.1 = (bf16[2048,512]{1,0:T(8,128)(2,1)}, bf16[2048,512]{1,0:T(8,128)(2,1)}, bf16[2048,512]{1,0:T(8,128)(2,1)}, bf16[2048,512]{1,0:T(8,128)(2,1)}, f32[2048,5...) custom-call(bf16[2048,512]{1,0:T(8,128)(2,1)} %refs_5_.5, ...), custom_call_target="tpu_custom_call" | custom-call | flops 5000000000 | bytes 1048576 | tf_op jit(solution)/shard_map/mlp/pallas_call | solution.py:802
  103.9 1.6 copy-done.8
  105.5 4.7 %attend_back.2 = (bf16[2048,1536]{1,0:T(8,128)(2,1)S(1)}, f32[64,256]{1,0:T(8,128)S(1)}) custom-call(s32[2,4]{1,0:T(2,128)S(1)} %bitcast.6, bf16[2048,1536]{1,0:T(8,128)(2,1)S(1)} %bitcast.4, f32[2048,256]{1,0:T(8,128)S(1)} %copy-done.2, bf16[2048,512]{1,0:T(8,128)(2,1)S(1)} %copy-done.8, f32[2048,256]{1,0:T(8,128)S(1)} %copy-done.2), custom_call_target="tpu_custom_call" | custom-call | flops 700000000 | bytes 1048576 | tf_op jit(solution)/shard_map/attend_back/pallas_call | solution.py:841
  110.3 0.5 add_convert_fusion
  110.9 1.5 collective-permute-start.21
  112.4 0.8 collective-permute-start.22
  113.2 1.2 collective-permute-start.23
  114.5 13.3 %attend_back.3 = (bf16[2048,1536]{1,0:T(8,128)(2,1)S(1)}, f32[64,256]{1,0:T(8,128)S(1)}) custom-call(s32[2,4]{1,0:T(2,128)S(1)} %bitcast.7, bf16[2048,1536]{1,0:T(8,128)(2,1)S(1)} %bitcast.4, f32[2048,256]{1,0:T(8,128)S(1)} %copy-done.2, bf16[2048,512]{1,0:T(8,128)(2,1)S(1)} %copy-done.9, ...), custom_call_target="tpu_custom_call", output_to_operand_aliasing={{0}: (4, {})} | custom-call | flops 2100000000 | bytes 1048576 | tf_op jit(solution)/shard_map/attend_back/pallas_call | solution.py:841
  127.8 5.8 %token_back.1 = f32[2048,512]{1,0:T(8,128)} custom-call(bf16[2048,1536]{1,0:T(8,128)(2,1)S(1)} %get-tuple-element.126.gqn_ref, bf16[2048,512]{1,0:T(8,128)(2,1)S(1)} %copy-done, f32[2048,512]{1,0:T(8,128)S(1)} %copy-done.11, bf16[512,1664]{1,0:T(8,128)(2,1)S(1)} %copy-done.10, f32[16,512]{1,0:T(8,128)S(1)} %copy-done.13), custom_call_target="tpu_custom_call" | custom-call | flops 1000000000 | bytes 1048576 | tf_op jit(solution)/shard_map/token_back/pallas_call | solution.py:892
  133.7 7.6 %project_back.1 = (bf16[256,1664]{1,0:T(8,128)(2,1)S(1)}, bf16[256,1664]{1,0:T(8,128)(2,1)S(1)}) custom-call(bf16[2048,1536]{1,0:T(8,128)(2,1)S(1)} %get-tuple-element.126.gqn_ref, bf16[2048,512]{1,0:T(8,128)(2,1)S(1)} %copy-done, bf16[512,1664]{1,0:T(8,128)(2,1)S(1)} %copy-done.10, f32[16,512]{1,0:T(8,128)S(1)} %copy-done.14, ...), custom_call_target="tpu_custom_call" | custom-call | flops 1000000000 | bytes 1048576 | tf_op jit(solution)/shard_map/project_back/pallas_call | solution.py:869
  141.4 2.4 %collective-permute-done.24 = bf16[256,1664]{1,0:T(8,128)(2,1)S(1)} collective-permute-done((bf16[256,1664]{1,0:T(8,128)(2,1)S(1)}, bf16[256,1664]{1,0:T(8,128)(2,1)S(1)}, u32[]{:S(2)}, u32[]{:S(2)}) %collective-permute-start.24) | collective-permute-done | bytes 852000 | tf_op jit(solution)/shard_map/ppermute | solution.py:963
  144.0 1.5 collective-permute-start.25
  145.5 0.8 collective-permute-start.26
  146.3 1.2 collective-permute-start.27
  147.8 2.1 %collective-permute-start.33 = (bf16[16,4608]{1,0:T(8,128)(2,1)S(1)}, bf16[16,4608]{1,0:T(8,128)(2,1)S(1)}, u32[]{:S(2)}, u32[]{:S(2)}) collective-permute-start(bf16[16,4608]{1,0:T(8,128)(2,1)S(1)} %get-tuple-element.194), channel_id=1, source_target_pairs={{0,24},{1,25},{2,26},{3,27},{4,28},{5,29},{6,30},{7,31},{8,16},{9,... | collective-permute-start | bytes 442376 | tf_op jit(solution)/shard_map/ppermute | solution.py:963
  149.9 1.2 collective-permute-start.32
  151.2 3.9 %output.2.refs_9_ = bf16[2048,512]{1,0:T(8,128)(2,1)} custom-call(bf16[2048,512]{1,0:T(8,128)(2,1)S(1)} %copy-done.3, bf16[2048,512]{1,0:T(8,128)(2,1)S(1)} %copy-done.4, bf16[2048,512]{1,0:T(8,128)(2,1)S(1)} %copy-done.5, bf16[2048,512]{1,0:T(8,128)(2,1)S(1)} %copy-done.6, bf16[2048,512]{1,0:T(8,128)(2,1)S(1)} %copy-done.1, bf16[2048,512]{1,0:T(8,128)(2,1)S(1)} %copy-done, ...), custom_call_target="tpu_custom_call" | custom-call | flops 1000000000 | bytes 1048576 | tf_op jit(solution)/shard_map/output/pallas_call | solution.py:912
  155.1 1.1 collective-permute-start.31
  156.2 0.9 collective-permute-done.26
  157.2 1.9 %collective-permute-start.28 = (bf16[16,1664]{1,0:T(8,128)(2,1)S(1)}, bf16[16,1664]{1,0:T(8,128)(2,1)S(1)}, u32[]{:S(2)}, u32[]{:S(2)}) collective-permute-start(bf16[16,1664]{1,0:T(8,128)(2,1)S(1)} %get-tuple-element.158), channel_id=1, source_target_pairs={{0,8},{1,9},{2,10},{3,11},{4,12},{5,13},{6,14},{7,15},{8,0},{9,1},... | collective-permute-start | bytes 159752 | tf_op jit(solution)/shard_map/ppermute | solution.py:963
  159.1 1.2 collective-permute-start.29
  160.3 1.4 collective-permute-start.30
  161.7 3.8 %output.3 = bf16[2048,512]{1,0:T(8,128)(2,1)} custom-call(bf16[2048,512]{1,0:T(8,128)(2,1)S(1)} %copy-done.3, bf16[2048,512]{1,0:T(8,128)(2,1)S(1)} %copy-done.4, bf16[2048,512]{1,0:T(8,128)(2,1)S(1)} %copy-done.5, bf16[2048,512]{1,0:T(8,128)(2,1)S(1)} %copy-done.6, bf16[2048,512]{1,0:T(8,128)(2,1)S(1)} %copy-done.1, ...), custom_call_target="tpu_custom_call", output_to_operand_aliasing={{}: (9, {})} | custom-call | flops 1000000000 | bytes 1048576 | tf_op jit(solution)/shard_map/output/pallas_call | solution.py:912
  165.5 1.2 collective-permute-done.32.refs_6_
  166.7 1.0 collective-permute-done.29.refs_2_
  167.7 0.9 finish.1
  (108 shorter events, 4.3 us)
Async XLA Ops:
  2.4 15.8 %collective-permute-start.2 = (bf16[16,1664]{1,0:T(8,128)(2,1)}, bf16[16,1664]{1,0:T(8,128)(2,1)S(1)}, u32[]{:S(2)}, u32[]{:S(2)}) collective-permute-start(bf16[16,1664]{1,0:T(8,128)(2,1)} %get-tuple-element.103), channel_id=1, source_target_pairs={{0,24},{1,25},{2,26},{3,27},{4,28},{5,29},{6,30},{7,31},{8,16},{9,... | collective-permute-start | bytes 159752 | tf_op jit(solution)/shard_map/ppermute | solution.py:963
  7.5 10.7 %collective-permute-start.1 = (bf16[16,1664]{1,0:T(8,128)(2,1)}, bf16[16,1664]{1,0:T(8,128)(2,1)S(1)}, u32[]{:S(2)}, u32[]{:S(2)}) collective-permute-start(bf16[16,1664]{1,0:T(8,128)(2,1)} %get-tuple-element.103), channel_id=1, source_target_pairs={{0,16},{1,17},{2,18},{3,19},{4,20},{5,21},{6,22},{7,23},{8,24},{9,... | collective-permute-start | bytes 159752 | tf_op jit(solution)/shard_map/ppermute | solution.py:963
  7.5 5.2 %collective-permute-start = (bf16[16,1664]{1,0:T(8,128)(2,1)}, bf16[16,1664]{1,0:T(8,128)(2,1)S(1)}, u32[]{:S(2)}, u32[]{:S(2)}) collective-permute-start(bf16[16,1664]{1,0:T(8,128)(2,1)} %get-tuple-element.103), channel_id=1, source_target_pairs={{0,8},{1,9},{2,10},{3,11},{4,12},{5,13},{6,14},{7,15},{8,0},{9,1},... | collective-permute-start | bytes 159752 | tf_op jit(solution)/shard_map/ppermute | solution.py:963
  8.1 13.1 %collective-permute-start.8 = (bf16[16,4608]{1,0:T(8,128)(2,1)}, bf16[16,4608]{1,0:T(8,128)(2,1)S(1)}, u32[]{:S(2)}, u32[]{:S(2)}) collective-permute-start(bf16[16,4608]{1,0:T(8,128)(2,1)} %get-tuple-element.104), channel_id=1, source_target_pairs={{0,24},{1,25},{2,26},{3,27},{4,28},{5,29},{6,30},{7,31},{8,16},{9,... | collective-permute-start | bytes 442376 | tf_op jit(solution)/shard_map/ppermute | solution.py:963
  11.9 13.2 %collective-permute-start.7 = (bf16[16,4608]{1,0:T(8,128)(2,1)}, bf16[16,4608]{1,0:T(8,128)(2,1)S(1)}, u32[]{:S(2)}, u32[]{:S(2)}) collective-permute-start(bf16[16,4608]{1,0:T(8,128)(2,1)} %get-tuple-element.104), channel_id=1, source_target_pairs={{0,16},{1,17},{2,18},{3,19},{4,20},{5,21},{6,22},{7,23},{8,24},{9,... | collective-permute-start | bytes 442376 | tf_op jit(solution)/shard_map/ppermute | solution.py:963
  12.7 12.4 %collective-permute-start.6 = (bf16[16,4608]{1,0:T(8,128)(2,1)}, bf16[16,4608]{1,0:T(8,128)(2,1)S(1)}, u32[]{:S(2)}, u32[]{:S(2)}) collective-permute-start(bf16[16,4608]{1,0:T(8,128)(2,1)} %get-tuple-element.104), channel_id=1, source_target_pairs={{0,8},{1,9},{2,10},{3,11},{4,12},{5,13},{6,14},{7,15},{8,0},{9,1},... | collective-permute-start | bytes 442376 | tf_op jit(solution)/shard_map/ppermute | solution.py:963
  18.2 15.7 %copy-start.18 = (bf16[64,1664]{1,0:T(8,128)(2,1)}, bf16[64,1664]{1,0:T(8,128)(2,1)S(1)}, u32[]{:S(2)}) copy-start(bf16[64,1664]{1,0:T(8,128)(2,1)S(1)} %constant_dynamic-update-slice_fusion.refs_0_) | copy-start | bytes 638980
  18.2 7.8 %collective-permute-start.5 = (bf16[64,1664]{1,0:T(8,128)(2,1)S(1)}, bf16[64,1664]{1,0:T(8,128)(2,1)S(1)}, u32[]{:S(2)}, u32[]{:S(2)}) collective-permute-start(bf16[64,1664]{1,0:T(8,128)(2,1)S(1)} %constant_dynamic-update-slice_fusion.refs_0_), channel_id=1, source_target_pairs={{0,5},{1,4},{2,7},{3,6},{4,1},{5,0},{6,3},{7,2},{8,13},{9,12},{10,... | collective-permute-start | bytes 638984 | tf_op jit(solution)/shard_map/ppermute | solution.py:963
  20.7 6.6 %collective-permute-start.4 = (bf16[64,1664]{1,0:T(8,128)(2,1)S(1)}, bf16[64,1664]{1,0:T(8,128)(2,1)S(1)}, u32[]{:S(2)}, u32[]{:S(2)}) collective-permute-start(bf16[64,1664]{1,0:T(8,128)(2,1)S(1)} %constant_dynamic-update-slice_fusion.refs_0_), channel_id=1, source_target_pairs={{0,1},{1,0},{2,3},{3,2},{4,5},{5,4},{6,7},{7,6},{8,9},{9,8},{10,11... | collective-permute-start | bytes 638984 | tf_op jit(solution)/shard_map/ppermute | solution.py:963
  21.2 6.2 %collective-permute-start.3 = (bf16[64,1664]{1,0:T(8,128)(2,1)S(1)}, bf16[64,1664]{1,0:T(8,128)(2,1)S(1)}, u32[]{:S(2)}, u32[]{:S(2)}) collective-permute-start(bf16[64,1664]{1,0:T(8,128)(2,1)S(1)} %constant_dynamic-update-slice_fusion.refs_0_), channel_id=1, source_target_pairs={{0,4},{1,5},{2,6},{3,7},{4,0},{5,1},{6,2},{7,3},{8,12},{9,13},{10,... | collective-permute-start | bytes 638984 | tf_op jit(solution)/shard_map/ppermute | solution.py:963
  26.0 28.0 %copy-start.17 = (bf16[64,4608]{1,0:T(8,128)(2,1)}, bf16[64,4608]{1,0:T(8,128)(2,1)S(1)}, u32[]{:S(2)}) copy-start(bf16[64,4608]{1,0:T(8,128)(2,1)S(1)} %pad_maximum_fusion.refs_0_) | copy-start | bytes 1769476
  27.4 4.0 %collective-permute-start.9 = (bf16[64,1664]{1,0:T(8,128)(2,1)S(1)}, bf16[64,1664]{1,0:T(8,128)(2,1)S(1)}, u32[]{:S(2)}, u32[]{:S(2)}) collective-permute-start(bf16[64,1664]{1,0:T(8,128)(2,1)S(1)} %constant_dynamic-update-slice_fusion.refs_0_), channel_id=1, source_target_pairs={{0,2},{1,3},{2,0},{3,1},{4,6},{5,7},{6,4},{7,5},{8,10},{9,11},{10,... | collective-permute-start | bytes 638984 | tf_op jit(solution)/shard_map/ppermute | solution.py:963
  27.4 4.0 %collective-permute-start.10 = (bf16[64,1664]{1,0:T(8,128)(2,1)S(1)}, bf16[64,1664]{1,0:T(8,128)(2,1)S(1)}, u32[]{:S(2)}, u32[]{:S(2)}) collective-permute-start(bf16[64,1664]{1,0:T(8,128)(2,1)S(1)} %collective-permute-done.3.refs_1_), channel_id=1, source_target_pairs={{0,2},{1,3},{2,0},{3,1},{4,6},{5,7},{6,4},{7,5},{8,10},{9,11},{10,... | collective-permute-start | bytes 638984 | tf_op jit(solution)/shard_map/ppermute | solution.py:963
  27.9 26.1 %collective-permute-start.15 = (bf16[64,4608]{1,0:T(8,128)(2,1)S(1)}, bf16[64,4608]{1,0:T(8,128)(2,1)S(1)}, u32[]{:S(2)}, u32[]{:S(2)}) collective-permute-start(bf16[64,4608]{1,0:T(8,128)(2,1)S(1)} %pad_maximum_fusion.refs_0_), channel_id=1, source_target_pairs={{0,5},{1,4},{2,7},{3,6},{4,1},{5,0},{6,3},{7,2},{8,13},{9,12},{10,... | collective-permute-start | bytes 1769480 | tf_op jit(solution)/shard_map/ppermute | solution.py:963
  29.9 26.8 %collective-permute-start.14 = (bf16[64,4608]{1,0:T(8,128)(2,1)S(1)}, bf16[64,4608]{1,0:T(8,128)(2,1)S(1)}, u32[]{:S(2)}, u32[]{:S(2)}) collective-permute-start(bf16[64,4608]{1,0:T(8,128)(2,1)S(1)} %pad_maximum_fusion.refs_0_), channel_id=1, source_target_pairs={{0,1},{1,0},{2,3},{3,2},{4,5},{5,4},{6,7},{7,6},{8,9},{9,8},{10,11... | collective-permute-start | bytes 1769480 | tf_op jit(solution)/shard_map/ppermute | solution.py:963
  30.9 26.0 %collective-permute-start.13 = (bf16[64,4608]{1,0:T(8,128)(2,1)S(1)}, bf16[64,4608]{1,0:T(8,128)(2,1)S(1)}, u32[]{:S(2)}, u32[]{:S(2)}) collective-permute-start(bf16[64,4608]{1,0:T(8,128)(2,1)S(1)} %pad_maximum_fusion.refs_0_), channel_id=1, source_target_pairs={{0,4},{1,5},{2,6},{3,7},{4,0},{5,1},{6,2},{7,3},{8,12},{9,13},{10,... | collective-permute-start | bytes 1769480 | tf_op jit(solution)/shard_map/ppermute | solution.py:963
  31.4 1.6 collective-permute-start.11
  31.4 1.7 %collective-permute-start.12 = (bf16[64,1664]{1,0:T(8,128)(2,1)S(1)}, bf16[64,1664]{1,0:T(8,128)(2,1)S(1)}, u32[]{:S(2)}, u32[]{:S(2)}) collective-permute-start(bf16[64,1664]{1,0:T(8,128)(2,1)S(1)} %collective-permute-done.5.refs_3_), channel_id=1, source_target_pairs={{0,2},{1,3},{2,0},{3,1},{4,6},{5,7},{6,4},{7,5},{8,10},{9,11},{10,... | collective-permute-start | bytes 638984 | tf_op jit(solution)/shard_map/ppermute | solution.py:963
  33.0 24.4 %collective-permute-start.16 = (bf16[64,4608]{1,0:T(8,128)(2,1)S(1)}, bf16[64,4608]{1,0:T(8,128)(2,1)S(1)}, u32[]{:S(2)}, u32[]{:S(2)}) collective-permute-start(bf16[64,4608]{1,0:T(8,128)(2,1)S(1)} %pad_maximum_fusion.refs_0_), channel_id=1, source_target_pairs={{0,2},{1,3},{2,0},{3,1},{4,6},{5,7},{6,4},{7,5},{8,10},{9,11},{10,... | collective-permute-start | bytes 1769480 | tf_op jit(solution)/shard_map/ppermute | solution.py:963
  56.9 2.0 %collective-permute-start.17 = (bf16[64,4608]{1,0:T(8,128)(2,1)S(1)}, bf16[64,4608]{1,0:T(8,128)(2,1)S(1)}, u32[]{:S(2)}, u32[]{:S(2)}) collective-permute-start(bf16[64,4608]{1,0:T(8,128)(2,1)S(1)} %collective-permute-done.13.refs_1_), channel_id=1, source_target_pairs={{0,2},{1,3},{2,0},{3,1},{4,6},{5,7},{6,4},{7,5},{8,10},{9,11},{10,... | collective-permute-start | bytes 1769480 | tf_op jit(solution)/shard_map/ppermute | solution.py:963
  56.9 2.8 %collective-permute-start.18 = (bf16[64,4608]{1,0:T(8,128)(2,1)S(1)}, bf16[64,4608]{1,0:T(8,128)(2,1)S(1)}, u32[]{:S(2)}, u32[]{:S(2)}) collective-permute-start(bf16[64,4608]{1,0:T(8,128)(2,1)S(1)} %collective-permute-done.14.refs_2_), channel_id=1, source_target_pairs={{0,2},{1,3},{2,0},{3,1},{4,6},{5,7},{6,4},{7,5},{8,10},{9,11},{10,... | collective-permute-start | bytes 1769480 | tf_op jit(solution)/shard_map/ppermute | solution.py:963
  57.4 3.2 %collective-permute-start.19 = (bf16[64,4608]{1,0:T(8,128)(2,1)S(1)}, bf16[64,4608]{1,0:T(8,128)(2,1)S(1)}, u32[]{:S(2)}, u32[]{:S(2)}) collective-permute-start(bf16[64,4608]{1,0:T(8,128)(2,1)S(1)} %collective-permute-done.15.refs_3_), channel_id=1, source_target_pairs={{0,2},{1,3},{2,0},{3,1},{4,6},{5,7},{6,4},{7,5},{8,10},{9,11},{10,... | collective-permute-start | bytes 1769480 | tf_op jit(solution)/shard_map/ppermute | solution.py:963
  61.4 42.5 %slice-start = ((s8[6291456]{0:T(1024)(128)(4,1)}), s8[4194304]{0:T(1024)(128)(4,1)S(1)}, s32[]{:S(2)}) async-start(s8[6291456]{0:T(1024)(128)(4,1)} %bitcast.3), calls=%async_computation | async-start | bytes 8388608
  61.4 42.5 %slice-start.1 = ((s8[6291456]{0:T(1024)(128)(4,1)}), s8[2097152]{0:T(1024)(128)(4,1)S(1)}, s32[]{:S(2)}) async-start(s8[6291456]{0:T(1024)(128)(4,1)} %bitcast.3), calls=%async_computation.1 | async-start | bytes 4194304
  61.4 42.5 %copy-start.2 = (f32[2048,256]{1,0:T(8,128)S(1)}, f32[2048,256]{1,0:T(8,128)}, u32[]{:S(2)}) copy-start(f32[2048,256]{1,0:T(8,128)} %get-tuple-element.110.prob_ref._) | copy-start | bytes 6291460
  61.4 42.5 %copy-start.15 = (s32[4,2]{0,1:T(2,128)S(1)}, s32[4,2]{0,1:T(2,128)}, u32[]{:S(2)}) copy-start(s32[4,2]{0,1:T(2,128)} %param.21) | copy-start | bytes 100
  103.7 6.6 %collective-permute-start.20 = (bf16[256,4608]{1,0:T(8,128)(2,1)}, bf16[256,4608]{1,0:T(8,128)(2,1)S(1)}, u32[]{:S(2)}, u32[]{:S(2)}) collective-permute-start(bf16[256,4608]{1,0:T(8,128)(2,1)} %get-tuple-element.121), channel_id=1, source_target_pairs={{0,2},{1,3},{2,0},{3,1},{4,6},{5,7},{6,4},{7,5},{8,10},{9,11},{10,... | collective-permute-start | bytes 7077896 | tf_op jit(solution)/shard_map/ppermute | solution.py:963
  110.9 16.9 %copy-start = (bf16[2048,512]{1,0:T(8,128)(2,1)S(1)}, bf16[2048,512]{1,0:T(8,128)(2,1)}, u32[]{:S(2)}) copy-start(bf16[2048,512]{1,0:T(8,128)(2,1)} %refs_5_.5) | copy-start | bytes 6291460
  110.9 16.9 %copy-start.10 = (bf16[512,1664]{1,0:T(8,128)(2,1)S(1)}, bf16[512,1664]{1,0:T(8,128)(2,1)}, u32[]{:S(2)}) copy-start(bf16[512,1664]{1,0:T(8,128)(2,1)} %get-tuple-element.125.w_ref) | copy-start | bytes 5111812
  110.9 16.9 %copy-start.13 = (f32[16,512]{1,0:T(8,128)S(1)}, f32[16,512]{1,0:T(8,128)}, u32[]{:S(2)}) copy-start(f32[16,512]{1,0:T(8,128)} %get-tuple-element.114.vec_ref.refs_8_) | copy-start | bytes 98308
  110.9 30.4 %collective-permute-start.21 = (bf16[64,4608]{1,0:T(8,128)(2,1)S(1)}, bf16[64,4608]{1,0:T(8,128)(2,1)S(1)}, u32[]{:S(2)}, u32[]{:S(2)}) collective-permute-start(bf16[64,4608]{1,0:T(8,128)(2,1)S(1)} %get-tuple-element.133), channel_id=1, source_target_pairs={{0,4},{1,5},{2,6},{3,7},{4,0},{5,1},{6,2},{7,3},{8,12},{9,13},{10,... | collective-permute-start | bytes 1769480 | tf_op jit(solution)/shard_map/ppermute | solution.py:963
  112.4 28.9 %collective-permute-start.22 = (bf16[64,4608]{1,0:T(8,128)(2,1)S(1)}, bf16[64,4608]{1,0:T(8,128)(2,1)S(1)}, u32[]{:S(2)}, u32[]{:S(2)}) collective-permute-start(bf16[64,4608]{1,0:T(8,128)(2,1)S(1)} %get-tuple-element.134), channel_id=1, source_target_pairs={{0,1},{1,0},{2,3},{3,2},{4,5},{5,4},{6,7},{7,6},{8,9},{9,8},{10,11... | collective-permute-start | bytes 1769480 | tf_op jit(solution)/shard_map/ppermute | solution.py:963
  113.2 28.1 %collective-permute-start.23 = (bf16[64,4608]{1,0:T(8,128)(2,1)S(1)}, bf16[64,4608]{1,0:T(8,128)(2,1)S(1)}, u32[]{:S(2)}, u32[]{:S(2)}) collective-permute-start(bf16[64,4608]{1,0:T(8,128)(2,1)S(1)} %get-tuple-element.135), channel_id=1, source_target_pairs={{0,5},{1,4},{2,7},{3,6},{4,1},{5,0},{6,3},{7,2},{8,13},{9,12},{10,... | collective-permute-start | bytes 1769480 | tf_op jit(solution)/shard_map/ppermute | solution.py:963
  114.5 13.3 %copy-start.11 = (f32[2048,512]{1,0:T(8,128)S(1)}, f32[2048,512]{1,0:T(8,128)}, u32[]{:S(2)}) copy-start(f32[2048,512]{1,0:T(8,128)} %get-tuple-element.124.gmid_ref) | copy-start | bytes 12582916
  133.6 17.5 %copy-start.4 = (bf16[2048,512]{1,0:T(8,128)(2,1)S(1)}, bf16[2048,512]{1,0:T(8,128)(2,1)}, u32[]{:S(2)}) copy-start(bf16[2048,512]{1,0:T(8,128)(2,1)} %get-tuple-element.147.refs_1_) | copy-start | bytes 6291460
  133.6 17.5 %copy-start.5 = (bf16[2048,512]{1,0:T(8,128)(2,1)S(1)}, bf16[2048,512]{1,0:T(8,128)(2,1)}, u32[]{:S(2)}) copy-start(bf16[2048,512]{1,0:T(8,128)(2,1)} %get-tuple-element.148.refs_2_) | copy-start | bytes 6291460
  133.6 17.5 %copy-start.6 = (bf16[2048,512]{1,0:T(8,128)(2,1)S(1)}, bf16[2048,512]{1,0:T(8,128)(2,1)}, u32[]{:S(2)}) copy-start(bf16[2048,512]{1,0:T(8,128)(2,1)} %get-tuple-element.149.refs_3_) | copy-start | bytes 6291460
  133.6 17.5 %copy-start.7 = (bf16[2048,512]{1,0:T(8,128)(2,1)S(1)}, bf16[2048,512]{1,0:T(8,128)(2,1)}, u32[]{:S(2)}) copy-start(bf16[2048,512]{1,0:T(8,128)(2,1)} %get-tuple-element.151.refs_7_) | copy-start | bytes 6291460
  141.3 2.4 %collective-permute-start.24 = (bf16[256,1664]{1,0:T(8,128)(2,1)S(1)}, bf16[256,1664]{1,0:T(8,128)(2,1)S(1)}, u32[]{:S(2)}, u32[]{:S(2)}) collective-permute-start(bf16[256,1664]{1,0:T(8,128)(2,1)S(1)} %get-tuple-element.137), channel_id=1, source_target_pairs={{0,2},{1,3},{2,0},{3,1},{4,6},{5,7},{6,4},{7,5},{8,10},{9,11},{10,... | collective-permute-start | bytes 2555912 | tf_op jit(solution)/shard_map/ppermute | solution.py:963
  144.0 11.1 %collective-permute-start.25 = (bf16[64,1664]{1,0:T(8,128)(2,1)S(1)}, bf16[64,1664]{1,0:T(8,128)(2,1)S(1)}, u32[]{:S(2)}, u32[]{:S(2)}) collective-permute-start(bf16[64,1664]{1,0:T(8,128)(2,1)S(1)} %get-tuple-element.143), channel_id=1, source_target_pairs={{0,4},{1,5},{2,6},{3,7},{4,0},{5,1},{6,2},{7,3},{8,12},{9,13},{10,... | collective-permute-start | bytes 638984 | tf_op jit(solution)/shard_map/ppermute | solution.py:963
  145.5 11.6 %collective-permute-start.26 = (bf16[64,1664]{1,0:T(8,128)(2,1)S(1)}, bf16[64,1664]{1,0:T(8,128)(2,1)S(1)}, u32[]{:S(2)}, u32[]{:S(2)}) collective-permute-start(bf16[64,1664]{1,0:T(8,128)(2,1)S(1)} %get-tuple-element.144), channel_id=1, source_target_pairs={{0,1},{1,0},{2,3},{3,2},{4,5},{5,4},{6,7},{7,6},{8,9},{9,8},{10,11... | collective-permute-start | bytes 638984 | tf_op jit(solution)/shard_map/ppermute | solution.py:963
  146.3 10.8 %collective-permute-start.27 = (bf16[64,1664]{1,0:T(8,128)(2,1)S(1)}, bf16[64,1664]{1,0:T(8,128)(2,1)S(1)}, u32[]{:S(2)}, u32[]{:S(2)}) collective-permute-start(bf16[64,1664]{1,0:T(8,128)(2,1)S(1)} %get-tuple-element.145), channel_id=1, source_target_pairs={{0,5},{1,4},{2,7},{3,6},{4,1},{5,0},{6,3},{7,2},{8,13},{9,12},{10,... | collective-permute-start | bytes 638984 | tf_op jit(solution)/shard_map/ppermute | solution.py:963
  147.8 12.4 %collective-permute-start.33 = (bf16[16,4608]{1,0:T(8,128)(2,1)S(1)}, bf16[16,4608]{1,0:T(8,128)(2,1)S(1)}, u32[]{:S(2)}, u32[]{:S(2)}) collective-permute-start(bf16[16,4608]{1,0:T(8,128)(2,1)S(1)} %get-tuple-element.194), channel_id=1, source_target_pairs={{0,24},{1,25},{2,26},{3,27},{4,28},{5,29},{6,30},{7,31},{8,16},{9,... | collective-permute-start | bytes 442376 | tf_op jit(solution)/shard_map/ppermute | solution.py:963
  149.9 16.8 %collective-permute-start.32 = (bf16[16,4608]{1,0:T(8,128)(2,1)S(1)}, bf16[16,4608]{1,0:T(8,128)(2,1)S(1)}, u32[]{:S(2)}, u32[]{:S(2)}) collective-permute-start(bf16[16,4608]{1,0:T(8,128)(2,1)S(1)} %get-tuple-element.195), channel_id=1, source_target_pairs={{0,16},{1,17},{2,18},{3,19},{4,20},{5,21},{6,22},{7,23},{8,24},{9,... | collective-permute-start | bytes 442376 | tf_op jit(solution)/shard_map/ppermute | solution.py:963
  155.1 11.7 %collective-permute-start.31 = (bf16[16,4608]{1,0:T(8,128)(2,1)S(1)}, bf16[16,4608]{1,0:T(8,128)(2,1)S(1)}, u32[]{:S(2)}, u32[]{:S(2)}) collective-permute-start(bf16[16,4608]{1,0:T(8,128)(2,1)S(1)} %get-tuple-element.196), channel_id=1, source_target_pairs={{0,8},{1,9},{2,10},{3,11},{4,12},{5,13},{6,14},{7,15},{8,0},{9,1},... | collective-permute-start | bytes 442376 | tf_op jit(solution)/shard_map/ppermute | solution.py:963
  157.2 9.5 %collective-permute-start.28 = (bf16[16,1664]{1,0:T(8,128)(2,1)S(1)}, bf16[16,1664]{1,0:T(8,128)(2,1)S(1)}, u32[]{:S(2)}, u32[]{:S(2)}) collective-permute-start(bf16[16,1664]{1,0:T(8,128)(2,1)S(1)} %get-tuple-element.158), channel_id=1, source_target_pairs={{0,8},{1,9},{2,10},{3,11},{4,12},{5,13},{6,14},{7,15},{8,0},{9,1},... | collective-permute-start | bytes 159752 | tf_op jit(solution)/shard_map/ppermute | solution.py:963
  159.1 8.6 %collective-permute-start.29 = (bf16[16,1664]{1,0:T(8,128)(2,1)S(1)}, bf16[16,1664]{1,0:T(8,128)(2,1)S(1)}, u32[]{:S(2)}, u32[]{:S(2)}) collective-permute-start(bf16[16,1664]{1,0:T(8,128)(2,1)S(1)} %get-tuple-element.159), channel_id=1, source_target_pairs={{0,16},{1,17},{2,18},{3,19},{4,20},{5,21},{6,22},{7,23},{8,24},{9,... | collective-permute-start | bytes 159752 | tf_op jit(solution)/shard_map/ppermute | solution.py:963
  160.3 7.4 %collective-permute-start.30 = (bf16[16,1664]{1,0:T(8,128)(2,1)S(1)}, bf16[16,1664]{1,0:T(8,128)(2,1)S(1)}, u32[]{:S(2)}, u32[]{:S(2)}) collective-permute-start(bf16[16,1664]{1,0:T(8,128)(2,1)S(1)} %get-tuple-element.160), channel_id=1, source_target_pairs={{0,24},{1,25},{2,26},{3,27},{4,28},{5,29},{6,30},{7,31},{8,16},{9,... | collective-permute-start | bytes 159752 | tf_op jit(solution)/shard_map/ppermute | solution.py:963
  (20 other events, 86.0 us)

commit v3 on v2

--- a/solution.py
+++ b/solution.py
@@ -463,12 +463,14 @@
             gact_ref[m : m + half, k : k + half] += part
 
     def down_grad(c, m, k):
-        at = c * chunk + m
-        accd_ref[at : at + half, k : k + half] += dot_tn(gelu_refs[c][:, m : m + half], cot_ref[:, k : k + half])
+        if k == 0:
+            at = c * chunk + m
+            accd_ref[at : at + half, :] += dot_tn(gelu_refs[c][:, m : m + half], cot_ref[...])
 
     def up_grad(c, m, k):
-        at = c * chunk + k
-        accu_ref[m : m + half, at : at + half] += dot_tn(act_ref[:, m : m + half], gh_refs[c][:, k : k + half])
+        if k == 0:
+            at = c * chunk
+            accu_ref[m : m + half, at : at + chunk] += dot_tn(act_ref[:, m : m + half], gh_refs[c][...])
 
     def all_of(fn, c):
         return [functools.partial(fn, c, m, k) for k in (0, half) for m in (0, half)]
@@ -1069,7 +1071,7 @@
         first = spread_far(first, COLUMN)
         second = spread_far(second, COLUMN)
         first = spread_far(jnp.concatenate(first), PLANE)
-        first, second = lax.optimization_barrier((first, jnp.concatenate(second)))
+        first[0], second = lax.optimization_barrier((first[0], jnp.concatenate(second)))
         second = spread_far(second, PLANE)
         first = spread_core(first)
     else:

time: 169 us -> 167 us (0.988)
  waiting for transfers between devices: 21.5 us -> 19 us
    ppermute x34, waiting for transfers between devices: 21.5 us -> 19 us  [exchange(): return lax.ppermute(x, AXES, [(i, i ^ mask) for i in range(size)])]
  transfers between devices with their start and end apart: 34 -> 34, of which waited for: 14 -> 12; matrix products, arithmetic and copies ran while one was open for 1% -> 1% of each run, Pallas kernels for 35% -> 36%
where the time goes in v3:
time: 167 us; the launch traced here: 166 us
  Pallas kernels  104 us (62%)
  starting transfers between devices  35.4 us (21%)
  waiting for transfers between devices  19 us (11%)
  local copies, waits for them, and re-layouts  4.34 us (3%)
  other arithmetic  2.09 us (1%)
    pallas_call x1, Pallas kernels, mlp(): pl.pallas_call(functools.partial(mlp_kernel, masks, relative), grid=(n //...  42.1 us
    ppermute x34, starting transfers between devices, exchange(): return lax.ppermute(x, AXES, [(i, i ^ mask) for i in range(size)])  35.4 us
    pallas_call x1, Pallas kernels, attend(): pl.pallas_call(functools.partial(attend_kernel, masks), grid=(n // PATCHE...  20.1 us
    ppermute x34, waiting for transfers between devices, exchange(): return lax.ppermute(x, AXES, [(i, i ^ mask) for i in range(size)])  19 us
    pallas_call x2, Pallas kernels, attend_back(): pl.pallas_call(functools.partial(attend_back_kernel, start), grid=(clips,...  18 us
    pallas_call x2, Pallas kernels, output(): pl.pallas_call(output_kernel, grid=(count,), in_specs=[spec(width)] * 6 +...  7.7 us
    pallas_call x1, Pallas kernels, project_back(): pl.pallas_call(functools.partial(project_back_kernel, relative), grid=(n...  7.64 us
    pallas_call x1, Pallas kernels, token_back(): pl.pallas_call(token_back_kernel, grid=(n // tile,), in_specs=[rows_spec(...  5.8 us
  transfers between devices with their start and end apart: 34, of which 12 were waited for; matrix products, arithmetic and copies ran while one was open for 1% of the time, Pallas kernels for 36%

profile of v3, /device:TPU:0, one launch (start us, length us, event | category | flops | bytes accessed | tf_op | source)
XLA Modules:
  0.0 166.2 jit_solution(17359864989698577606)
XLA Ops:
  0.7 1.8 %pack.1 = (bf16[16,1664]{1,0:T(8,128)(2,1)}, bf16[16,4608]{1,0:T(8,128)(2,1)}) custom-call(bf16[16]{0:T(256)(128)(2,1)} %refs_0_.1, bf16[16]{0:T(256)(128)(2,1)} %refs_1_.1, bf16[16]{0:T(256)(128)(2,1)} %refs_2_.1, bf16[16]{0:T(256)(128)(2,1)} %refs_3_.1, bf16[16]{0:T(256)(128)(2,1)} %refs_4_.1, bf16[16]{0:T(256)(128)(2,1)} %refs_5_.3, ...), custom_call_target="tpu_custom_call" | custom-call | tf_op jit(solution)/shard_map/pack/pallas_call | solution.py:253
  2.4 5.0 %collective-permute-start.2 = (bf16[16,1664]{1,0:T(8,128)(2,1)}, bf16[16,1664]{1,0:T(8,128)(2,1)S(1)}, u32[]{:S(2)}, u32[]{:S(2)}) collective-permute-start(bf16[16,1664]{1,0:T(8,128)(2,1)} %get-tuple-element.100), channel_id=1, source_target_pairs={{0,24},{1,25},{2,26},{3,27},{4,28},{5,29},{6,30},{7,31},{8,16},{9,... | collective-permute-start | bytes 159752 | tf_op jit(solution)/shard_map/ppermute | solution.py:965
  7.5 0.6 collective-permute-start
  8.1 3.8 %collective-permute-start.5 = (bf16[16,4608]{1,0:T(8,128)(2,1)}, bf16[16,4608]{1,0:T(8,128)(2,1)S(1)}, u32[]{:S(2)}, u32[]{:S(2)}) collective-permute-start(bf16[16,4608]{1,0:T(8,128)(2,1)} %get-tuple-element.101), channel_id=1, source_target_pairs={{0,24},{1,25},{2,26},{3,27},{4,28},{5,29},{6,30},{7,31},{8,16},{9,... | collective-permute-start | bytes 442376 | tf_op jit(solution)/shard_map/ppermute | solution.py:965
  11.9 0.8 constant_dynamic-update-slice_fusion.3
  12.7 0.9 collective-permute-start.3
  13.6 4.6 %collective-permute-done.1 = bf16[16,1664]{1,0:T(8,128)(2,1)S(1)} collective-permute-done((bf16[16,1664]{1,0:T(8,128)(2,1)}, bf16[16,1664]{1,0:T(8,128)(2,1)S(1)}, u32[]{:S(2)}, u32[]{:S(2)}) %collective-permute-start.1) | collective-permute-done | bytes 53280 | tf_op jit(solution)/shard_map/ppermute | solution.py:965
  18.2 2.5 %collective-permute-start.8 = (bf16[64,1664]{1,0:T(8,128)(2,1)S(1)}, bf16[64,1664]{1,0:T(8,128)(2,1)S(1)}, u32[]{:S(2)}, u32[]{:S(2)}) collective-permute-start(bf16[64,1664]{1,0:T(8,128)(2,1)S(1)} %constant_dynamic-update-slice_fusion.refs_0_), channel_id=1, source_target_pairs={{0,5},{1,4},{2,7},{3,6},{4,1},{5,0},{6,3},{7,2},{8,13},{9,12},{10,... | collective-permute-start | bytes 638984 | tf_op jit(solution)/shard_map/ppermute | solution.py:965
  20.7 0.5 collective-permute-start.7
  21.2 0.5 collective-permute-start.6
  21.8 3.3 %collective-permute-done.4 = bf16[16,4608]{1,0:T(8,128)(2,1)S(1)} collective-permute-done((bf16[16,4608]{1,0:T(8,128)(2,1)}, bf16[16,4608]{1,0:T(8,128)(2,1)S(1)}, u32[]{:S(2)}, u32[]{:S(2)}) %collective-permute-start.4) | collective-permute-done | bytes 147488 | tf_op jit(solution)/shard_map/ppermute | solution.py:965
  25.1 0.9 pad_maximum_fusion.refs_0_
  26.6 2.4 %collective-permute-start.15 = (bf16[64,4608]{1,0:T(8,128)(2,1)S(1)}, bf16[64,4608]{1,0:T(8,128)(2,1)S(1)}, u32[]{:S(2)}, u32[]{:S(2)}) collective-permute-start(bf16[64,4608]{1,0:T(8,128)(2,1)S(1)} %pad_maximum_fusion.refs_0_), channel_id=1, source_target_pairs={{0,5},{1,4},{2,7},{3,6},{4,1},{5,0},{6,3},{7,2},{8,13},{9,12},{10,... | collective-permute-start | bytes 1769480 | tf_op jit(solution)/shard_map/ppermute | solution.py:965
  29.1 0.5 collective-permute-start.14
  29.6 0.5 collective-permute-start.13
  30.2 0.5 collective-permute-start.10
  30.9 0.8 collective-permute-done.11.refs_6_
  31.9 0.7 copy-done.31
  32.6 20.1 %attend.1 = (bf16[2048,1536]{1,0:T(8,128)(2,1)}, f32[2048,256]{1,0:T(8,128)}, bf16[2048,512]{1,0:T(8,128)(2,1)}, bf16[512,1664]{1,0:T(8,128)(2,1)}, f32[16,512]{1,0:T(8,128)}) custom-call(s32[2,4]{1,0:T(2,128)} %bitcast.5, s32[4]{0:T(128)} %count_ref.1, bf16[2048,512]{1,0:T(8,128)(2,1)} %refs_5_.5, bf16[16,49]{1,0:T(8,128)(2,1)} %bitcast.9, ...), custom_call_target="tpu_custom_call" | custom-call | flops 2800000000 | bytes 1048576 | tf_op jit(solution)/shard_map/attend/pallas_call | solution.py:764
  52.8 2.7 %collective-permute-done.14.refs_2_ = bf16[64,4608]{1,0:T(8,128)(2,1)S(1)} collective-permute-done((bf16[64,4608]{1,0:T(8,128)(2,1)S(1)}, bf16[64,4608]{1,0:T(8,128)(2,1)S(1)}, u32[]{:S(2)}, u32[]{:S(2)}) %collective-permute-start.14) | collective-permute-done | bytes 589856 | tf_op jit(solution)/shard_map/ppermute | solution.py:965
  55.6 0.5 collective-permute-start.18
  56.2 1.4 collective-permute-done.17.refs_5_
  57.6 0.8 collective-permute-done.18.refs_6_
  58.5 0.8 collective-permute-done.19.refs_7_
  59.3 0.8 copy-done.25
  60.2 42.1 %mlp.1 = (bf16[2048,512]{1,0:T(8,128)(2,1)}, bf16[2048,512]{1,0:T(8,128)(2,1)}, bf16[2048,512]{1,0:T(8,128)(2,1)}, bf16[2048,512]{1,0:T(8,128)(2,1)}, f32[2048,5...) custom-call(bf16[2048,512]{1,0:T(8,128)(2,1)} %refs_5_.5, ...), custom_call_target="tpu_custom_call" | custom-call | flops 5000000000 | bytes 1048576 | tf_op jit(solution)/shard_map/mlp/pallas_call | solution.py:804
  102.5 1.6 copy-done.8
  104.1 4.7 %attend_back.2 = (bf16[2048,1536]{1,0:T(8,128)(2,1)S(1)}, f32[64,256]{1,0:T(8,128)S(1)}) custom-call(s32[2,4]{1,0:T(2,128)S(1)} %bitcast.6, bf16[2048,1536]{1,0:T(8,128)(2,1)S(1)} %bitcast.4, f32[2048,256]{1,0:T(8,128)S(1)} %copy-done.2, bf16[2048,512]{1,0:T(8,128)(2,1)S(1)} %copy-done.8, f32[2048,256]{1,0:T(8,128)S(1)} %copy-done.2), custom_call_target="tpu_custom_call" | custom-call | flops 700000000 | bytes 1048576 | tf_op jit(solution)/shard_map/attend_back/pallas_call | solution.py:843
  108.9 0.5 add_convert_fusion
  109.5 1.6 collective-permute-start.21
  111.1 0.8 collective-permute-start.22
  111.9 1.2 collective-permute-start.23
  113.1 13.3 %attend_back.3 = (bf16[2048,1536]{1,0:T(8,128)(2,1)S(1)}, f32[64,256]{1,0:T(8,128)S(1)}) custom-call(s32[2,4]{1,0:T(2,128)S(1)} %bitcast.7, bf16[2048,1536]{1,0:T(8,128)(2,1)S(1)} %bitcast.4, f32[2048,256]{1,0:T(8,128)S(1)} %copy-done.2, bf16[2048,512]{1,0:T(8,128)(2,1)S(1)} %copy-done.9, ...), custom_call_target="tpu_custom_call", output_to_operand_aliasing={{0}: (4, {})} | custom-call | flops 2100000000 | bytes 1048576 | tf_op jit(solution)/shard_map/attend_back/pallas_call | solution.py:843
  126.4 5.8 %token_back.1 = f32[2048,512]{1,0:T(8,128)} custom-call(bf16[2048,1536]{1,0:T(8,128)(2,1)S(1)} %get-tuple-element.120.gqn_ref, bf16[2048,512]{1,0:T(8,128)(2,1)S(1)} %copy-done, f32[2048,512]{1,0:T(8,128)S(1)} %copy-done.11, bf16[512,1664]{1,0:T(8,128)(2,1)S(1)} %copy-done.10, f32[16,512]{1,0:T(8,128)S(1)} %copy-done.13), custom_call_target="tpu_custom_call" | custom-call | flops 1000000000 | bytes 1048576 | tf_op jit(solution)/shard_map/token_back/pallas_call | solution.py:894
  132.2 7.6 %project_back.1 = (bf16[256,1664]{1,0:T(8,128)(2,1)S(1)}, bf16[256,1664]{1,0:T(8,128)(2,1)S(1)}) custom-call(bf16[2048,1536]{1,0:T(8,128)(2,1)S(1)} %get-tuple-element.120.gqn_ref, bf16[2048,512]{1,0:T(8,128)(2,1)S(1)} %copy-done, bf16[512,1664]{1,0:T(8,128)(2,1)S(1)} %copy-done.10, f32[16,512]{1,0:T(8,128)S(1)} %copy-done.14, ...), custom_call_target="tpu_custom_call" | custom-call | flops 1000000000 | bytes 1048576 | tf_op jit(solution)/shard_map/project_back/pallas_call | solution.py:871
  140.0 2.4 %collective-permute-done.24 = bf16[256,1664]{1,0:T(8,128)(2,1)S(1)} collective-permute-done((bf16[256,1664]{1,0:T(8,128)(2,1)S(1)}, bf16[256,1664]{1,0:T(8,128)(2,1)S(1)}, u32[]{:S(2)}, u32[]{:S(2)}) %collective-permute-start.24) | collective-permute-done | bytes 852000 | tf_op jit(solution)/shard_map/ppermute | solution.py:965
  142.6 1.6 collective-permute-start.25
  144.2 0.8 collective-permute-start.26
  144.9 1.2 collective-permute-start.27
  146.4 2.7 %collective-permute-start.33 = (bf16[16,4608]{1,0:T(8,128)(2,1)S(1)}, bf16[16,4608]{1,0:T(8,128)(2,1)S(1)}, u32[]{:S(2)}, u32[]{:S(2)}) collective-permute-start(bf16[16,4608]{1,0:T(8,128)(2,1)S(1)} %get-tuple-element.188), channel_id=1, source_target_pairs={{0,24},{1,25},{2,26},{3,27},{4,28},{5,29},{6,30},{7,31},{8,16},{9,... | collective-permute-start | bytes 442376 | tf_op jit(solution)/shard_map/ppermute | solution.py:965
  149.2 3.9 %output.2.refs_9_ = bf16[2048,512]{1,0:T(8,128)(2,1)} custom-call(bf16[2048,512]{1,0:T(8,128)(2,1)S(1)} %copy-done.3, bf16[2048,512]{1,0:T(8,128)(2,1)S(1)} %copy-done.4, bf16[2048,512]{1,0:T(8,128)(2,1)S(1)} %copy-done.5, bf16[2048,512]{1,0:T(8,128)(2,1)S(1)} %copy-done.6, bf16[2048,512]{1,0:T(8,128)(2,1)S(1)} %copy-done.1, bf16[2048,512]{1,0:T(8,128)(2,1)S(1)} %copy-done, ...), custom_call_target="tpu_custom_call" | custom-call | flops 1000000000 | bytes 1048576 | tf_op jit(solution)/shard_map/output/pallas_call | solution.py:914
  153.1 1.7 %collective-permute-start.31 = (bf16[16,4608]{1,0:T(8,128)(2,1)S(1)}, bf16[16,4608]{1,0:T(8,128)(2,1)S(1)}, u32[]{:S(2)}, u32[]{:S(2)}) collective-permute-start(bf16[16,4608]{1,0:T(8,128)(2,1)S(1)} %get-tuple-element.190), channel_id=1, source_target_pairs={{0,8},{1,9},{2,10},{3,11},{4,12},{5,13},{6,14},{7,15},{8,0},{9,1},... | collective-permute-start | bytes 442376 | tf_op jit(solution)/shard_map/ppermute | solution.py:965
  154.8 0.9 collective-permute-done.26
  155.9 3.2 %collective-permute-start.29 = (bf16[16,1664]{1,0:T(8,128)(2,1)S(1)}, bf16[16,1664]{1,0:T(8,128)(2,1)S(1)}, u32[]{:S(2)}, u32[]{:S(2)}) collective-permute-start(bf16[16,1664]{1,0:T(8,128)(2,1)S(1)} %get-tuple-element.153), channel_id=1, source_target_pairs={{0,16},{1,17},{2,18},{3,19},{4,20},{5,21},{6,22},{7,23},{8,24},{9,... | collective-permute-start | bytes 159752 | tf_op jit(solution)/shard_map/ppermute | solution.py:965
  159.1 1.2 collective-permute-start.30
  160.3 3.8 %output.3 = bf16[2048,512]{1,0:T(8,128)(2,1)} custom-call(bf16[2048,512]{1,0:T(8,128)(2,1)S(1)} %copy-done.3, bf16[2048,512]{1,0:T(8,128)(2,1)S(1)} %copy-done.4, bf16[2048,512]{1,0:T(8,128)(2,1)S(1)} %copy-done.5, bf16[2048,512]{1,0:T(8,128)(2,1)S(1)} %copy-done.6, bf16[2048,512]{1,0:T(8,128)(2,1)S(1)} %copy-done.1, ...), custom_call_target="tpu_custom_call", output_to_operand_aliasing={{}: (9, {})} | custom-call | flops 1000000000 | bytes 1048576 | tf_op jit(solution)/shard_map/output/pallas_call | solution.py:914
  164.2 0.9 collective-permute-done.30.refs_3_
  165.1 0.9 finish.1
  (108 shorter events, 2.4 us)
Async XLA Ops:
  2.4 15.8 %collective-permute-start.2 = (bf16[16,1664]{1,0:T(8,128)(2,1)}, bf16[16,1664]{1,0:T(8,128)(2,1)S(1)}, u32[]{:S(2)}, u32[]{:S(2)}) collective-permute-start(bf16[16,1664]{1,0:T(8,128)(2,1)} %get-tuple-element.100), channel_id=1, source_target_pairs={{0,24},{1,25},{2,26},{3,27},{4,28},{5,29},{6,30},{7,31},{8,16},{9,... | collective-permute-start | bytes 159752 | tf_op jit(solution)/shard_map/ppermute | solution.py:965
  7.5 10.7 %collective-permute-start.1 = (bf16[16,1664]{1,0:T(8,128)(2,1)}, bf16[16,1664]{1,0:T(8,128)(2,1)S(1)}, u32[]{:S(2)}, u32[]{:S(2)}) collective-permute-start(bf16[16,1664]{1,0:T(8,128)(2,1)} %get-tuple-element.100), channel_id=1, source_target_pairs={{0,16},{1,17},{2,18},{3,19},{4,20},{5,21},{6,22},{7,23},{8,24},{9,... | collective-permute-start | bytes 159752 | tf_op jit(solution)/shard_map/ppermute | solution.py:965
  7.5 5.2 %collective-permute-start = (bf16[16,1664]{1,0:T(8,128)(2,1)}, bf16[16,1664]{1,0:T(8,128)(2,1)S(1)}, u32[]{:S(2)}, u32[]{:S(2)}) collective-permute-start(bf16[16,1664]{1,0:T(8,128)(2,1)} %get-tuple-element.100), channel_id=1, source_target_pairs={{0,8},{1,9},{2,10},{3,11},{4,12},{5,13},{6,14},{7,15},{8,0},{9,1},... | collective-permute-start | bytes 159752 | tf_op jit(solution)/shard_map/ppermute | solution.py:965
  8.1 13.1 %collective-permute-start.5 = (bf16[16,4608]{1,0:T(8,128)(2,1)}, bf16[16,4608]{1,0:T(8,128)(2,1)S(1)}, u32[]{:S(2)}, u32[]{:S(2)}) collective-permute-start(bf16[16,4608]{1,0:T(8,128)(2,1)} %get-tuple-element.101), channel_id=1, source_target_pairs={{0,24},{1,25},{2,26},{3,27},{4,28},{5,29},{6,30},{7,31},{8,16},{9,... | collective-permute-start | bytes 442376 | tf_op jit(solution)/shard_map/ppermute | solution.py:965
  11.9 13.2 %collective-permute-start.4 = (bf16[16,4608]{1,0:T(8,128)(2,1)}, bf16[16,4608]{1,0:T(8,128)(2,1)S(1)}, u32[]{:S(2)}, u32[]{:S(2)}) collective-permute-start(bf16[16,4608]{1,0:T(8,128)(2,1)} %get-tuple-element.101), channel_id=1, source_target_pairs={{0,16},{1,17},{2,18},{3,19},{4,20},{5,21},{6,22},{7,23},{8,24},{9,... | collective-permute-start | bytes 442376 | tf_op jit(solution)/shard_map/ppermute | solution.py:965
  12.7 12.4 %collective-permute-start.3 = (bf16[16,4608]{1,0:T(8,128)(2,1)}, bf16[16,4608]{1,0:T(8,128)(2,1)S(1)}, u32[]{:S(2)}, u32[]{:S(2)}) collective-permute-start(bf16[16,4608]{1,0:T(8,128)(2,1)} %get-tuple-element.101), channel_id=1, source_target_pairs={{0,8},{1,9},{2,10},{3,11},{4,12},{5,13},{6,14},{7,15},{8,0},{9,1},... | collective-permute-start | bytes 442376 | tf_op jit(solution)/shard_map/ppermute | solution.py:965
  18.2 14.4 %copy-start.18 = (bf16[64,1664]{1,0:T(8,128)(2,1)}, bf16[64,1664]{1,0:T(8,128)(2,1)S(1)}, u32[]{:S(2)}) copy-start(bf16[64,1664]{1,0:T(8,128)(2,1)S(1)} %constant_dynamic-update-slice_fusion.refs_0_) | copy-start | bytes 638980
  18.2 7.9 %collective-permute-start.8 = (bf16[64,1664]{1,0:T(8,128)(2,1)S(1)}, bf16[64,1664]{1,0:T(8,128)(2,1)S(1)}, u32[]{:S(2)}, u32[]{:S(2)}) collective-permute-start(bf16[64,1664]{1,0:T(8,128)(2,1)S(1)} %constant_dynamic-update-slice_fusion.refs_0_), channel_id=1, source_target_pairs={{0,5},{1,4},{2,7},{3,6},{4,1},{5,0},{6,3},{7,2},{8,13},{9,12},{10,... | collective-permute-start | bytes 638984 | tf_op jit(solution)/shard_map/ppermute | solution.py:965
  20.7 8.4 %collective-permute-start.7 = (bf16[64,1664]{1,0:T(8,128)(2,1)S(1)}, bf16[64,1664]{1,0:T(8,128)(2,1)S(1)}, u32[]{:S(2)}, u32[]{:S(2)}) collective-permute-start(bf16[64,1664]{1,0:T(8,128)(2,1)S(1)} %constant_dynamic-update-slice_fusion.refs_0_), channel_id=1, source_target_pairs={{0,1},{1,0},{2,3},{3,2},{4,5},{5,4},{6,7},{7,6},{8,9},{9,8},{10,11... | collective-permute-start | bytes 638984 | tf_op jit(solution)/shard_map/ppermute | solution.py:965
  21.2 8.4 %collective-permute-start.6 = (bf16[64,1664]{1,0:T(8,128)(2,1)S(1)}, bf16[64,1664]{1,0:T(8,128)(2,1)S(1)}, u32[]{:S(2)}, u32[]{:S(2)}) collective-permute-start(bf16[64,1664]{1,0:T(8,128)(2,1)S(1)} %constant_dynamic-update-slice_fusion.refs_0_), channel_id=1, source_target_pairs={{0,4},{1,5},{2,6},{3,7},{4,0},{5,1},{6,2},{7,3},{8,12},{9,13},{10,... | collective-permute-start | bytes 638984 | tf_op jit(solution)/shard_map/ppermute | solution.py:965
  26.0 26.7 %copy-start.17 = (bf16[64,4608]{1,0:T(8,128)(2,1)}, bf16[64,4608]{1,0:T(8,128)(2,1)S(1)}, u32[]{:S(2)}) copy-start(bf16[64,4608]{1,0:T(8,128)(2,1)S(1)} %pad_maximum_fusion.refs_0_) | copy-start | bytes 1769476
  26.1 4.1 %collective-permute-start.9 = (bf16[64,1664]{1,0:T(8,128)(2,1)S(1)}, bf16[64,1664]{1,0:T(8,128)(2,1)S(1)}, u32[]{:S(2)}, u32[]{:S(2)}) collective-permute-start(bf16[64,1664]{1,0:T(8,128)(2,1)S(1)} %constant_dynamic-update-slice_fusion.refs_0_), channel_id=1, source_target_pairs={{0,2},{1,3},{2,0},{3,1},{4,6},{5,7},{6,4},{7,5},{8,10},{9,11},{10,... | collective-permute-start | bytes 638984 | tf_op jit(solution)/shard_map/ppermute | solution.py:965
  26.2 4.0 %collective-permute-start.12 = (bf16[64,1664]{1,0:T(8,128)(2,1)S(1)}, bf16[64,1664]{1,0:T(8,128)(2,1)S(1)}, u32[]{:S(2)}, u32[]{:S(2)}) collective-permute-start(bf16[64,1664]{1,0:T(8,128)(2,1)S(1)} %collective-permute-done.8.refs_3_), channel_id=1, source_target_pairs={{0,2},{1,3},{2,0},{3,1},{4,6},{5,7},{6,4},{7,5},{8,10},{9,11},{10,... | collective-permute-start | bytes 638984 | tf_op jit(solution)/shard_map/ppermute | solution.py:965
  26.6 26.1 %collective-permute-start.15 = (bf16[64,4608]{1,0:T(8,128)(2,1)S(1)}, bf16[64,4608]{1,0:T(8,128)(2,1)S(1)}, u32[]{:S(2)}, u32[]{:S(2)}) collective-permute-start(bf16[64,4608]{1,0:T(8,128)(2,1)S(1)} %pad_maximum_fusion.refs_0_), channel_id=1, source_target_pairs={{0,5},{1,4},{2,7},{3,6},{4,1},{5,0},{6,3},{7,2},{8,13},{9,12},{10,... | collective-permute-start | bytes 1769480 | tf_op jit(solution)/shard_map/ppermute | solution.py:965
  29.1 26.4 %collective-permute-start.14 = (bf16[64,4608]{1,0:T(8,128)(2,1)S(1)}, bf16[64,4608]{1,0:T(8,128)(2,1)S(1)}, u32[]{:S(2)}, u32[]{:S(2)}) collective-permute-start(bf16[64,4608]{1,0:T(8,128)(2,1)S(1)} %pad_maximum_fusion.refs_0_), channel_id=1, source_target_pairs={{0,1},{1,0},{2,3},{3,2},{4,5},{5,4},{6,7},{7,6},{8,9},{9,8},{10,11... | collective-permute-start | bytes 1769480 | tf_op jit(solution)/shard_map/ppermute | solution.py:965
  29.6 26.0 %collective-permute-start.13 = (bf16[64,4608]{1,0:T(8,128)(2,1)S(1)}, bf16[64,4608]{1,0:T(8,128)(2,1)S(1)}, u32[]{:S(2)}, u32[]{:S(2)}) collective-permute-start(bf16[64,4608]{1,0:T(8,128)(2,1)S(1)} %pad_maximum_fusion.refs_0_), channel_id=1, source_target_pairs={{0,4},{1,5},{2,6},{3,7},{4,0},{5,1},{6,2},{7,3},{8,12},{9,13},{10,... | collective-permute-start | bytes 1769480 | tf_op jit(solution)/shard_map/ppermute | solution.py:965
  30.1 1.6 collective-permute-start.11
  30.2 1.7 %collective-permute-start.10 = (bf16[64,1664]{1,0:T(8,128)(2,1)S(1)}, bf16[64,1664]{1,0:T(8,128)(2,1)S(1)}, u32[]{:S(2)}, u32[]{:S(2)}) collective-permute-start(bf16[64,1664]{1,0:T(8,128)(2,1)S(1)} %collective-permute-done.6.refs_1_), channel_id=1, source_target_pairs={{0,2},{1,3},{2,0},{3,1},{4,6},{5,7},{6,4},{7,5},{8,10},{9,11},{10,... | collective-permute-start | bytes 638984 | tf_op jit(solution)/shard_map/ppermute | solution.py:965
  31.7 24.4 %collective-permute-start.16 = (bf16[64,4608]{1,0:T(8,128)(2,1)S(1)}, bf16[64,4608]{1,0:T(8,128)(2,1)S(1)}, u32[]{:S(2)}, u32[]{:S(2)}) collective-permute-start(bf16[64,4608]{1,0:T(8,128)(2,1)S(1)} %pad_maximum_fusion.refs_0_), channel_id=1, source_target_pairs={{0,2},{1,3},{2,0},{3,1},{4,6},{5,7},{6,4},{7,5},{8,10},{9,11},{10,... | collective-permute-start | bytes 1769480 | tf_op jit(solution)/shard_map/ppermute | solution.py:965
  55.6 2.0 %collective-permute-start.17 = (bf16[64,4608]{1,0:T(8,128)(2,1)S(1)}, bf16[64,4608]{1,0:T(8,128)(2,1)S(1)}, u32[]{:S(2)}, u32[]{:S(2)}) collective-permute-start(bf16[64,4608]{1,0:T(8,128)(2,1)S(1)} %collective-permute-done.13.refs_1_), channel_id=1, source_target_pairs={{0,2},{1,3},{2,0},{3,1},{4,6},{5,7},{6,4},{7,5},{8,10},{9,11},{10,... | collective-permute-start | bytes 1769480 | tf_op jit(solution)/shard_map/ppermute | solution.py:965
  55.6 2.8 %collective-permute-start.18 = (bf16[64,4608]{1,0:T(8,128)(2,1)S(1)}, bf16[64,4608]{1,0:T(8,128)(2,1)S(1)}, u32[]{:S(2)}, u32[]{:S(2)}) collective-permute-start(bf16[64,4608]{1,0:T(8,128)(2,1)S(1)} %collective-permute-done.14.refs_2_), channel_id=1, source_target_pairs={{0,2},{1,3},{2,0},{3,1},{4,6},{5,7},{6,4},{7,5},{8,10},{9,11},{10,... | collective-permute-start | bytes 1769480 | tf_op jit(solution)/shard_map/ppermute | solution.py:965
  56.1 3.2 %collective-permute-start.19 = (bf16[64,4608]{1,0:T(8,128)(2,1)S(1)}, bf16[64,4608]{1,0:T(8,128)(2,1)S(1)}, u32[]{:S(2)}, u32[]{:S(2)}) collective-permute-start(bf16[64,4608]{1,0:T(8,128)(2,1)S(1)} %collective-permute-done.15.refs_3_), channel_id=1, source_target_pairs={{0,2},{1,3},{2,0},{3,1},{4,6},{5,7},{6,4},{7,5},{8,10},{9,11},{10,... | collective-permute-start | bytes 1769480 | tf_op jit(solution)/shard_map/ppermute | solution.py:965
  60.1 42.4 %slice-start = ((s8[6291456]{0:T(1024)(128)(4,1)}), s8[4194304]{0:T(1024)(128)(4,1)S(1)}, s32[]{:S(2)}) async-start(s8[6291456]{0:T(1024)(128)(4,1)} %bitcast.3), calls=%async_computation | async-start | bytes 8388608
  60.1 42.4 %slice-start.1 = ((s8[6291456]{0:T(1024)(128)(4,1)}), s8[2097152]{0:T(1024)(128)(4,1)S(1)}, s32[]{:S(2)}) async-start(s8[6291456]{0:T(1024)(128)(4,1)} %bitcast.3), calls=%async_computation.1 | async-start | bytes 4194304
  60.2 42.4 %copy-start.2 = (f32[2048,256]{1,0:T(8,128)S(1)}, f32[2048,256]{1,0:T(8,128)}, u32[]{:S(2)}) copy-start(f32[2048,256]{1,0:T(8,128)} %get-tuple-element.104.prob_ref._) | copy-start | bytes 6291460
  60.2 42.4 %copy-start.15 = (s32[4,2]{0,1:T(2,128)S(1)}, s32[4,2]{0,1:T(2,128)}, u32[]{:S(2)}) copy-start(s32[4,2]{0,1:T(2,128)} %param.21) | copy-start | bytes 100
  102.3 6.6 %collective-permute-start.20 = (bf16[256,4608]{1,0:T(8,128)(2,1)}, bf16[256,4608]{1,0:T(8,128)(2,1)S(1)}, u32[]{:S(2)}, u32[]{:S(2)}) collective-permute-start(bf16[256,4608]{1,0:T(8,128)(2,1)} %get-tuple-element.115), channel_id=1, source_target_pairs={{0,2},{1,3},{2,0},{3,1},{4,6},{5,7},{6,4},{7,5},{8,10},{9,11},{10,... | collective-permute-start | bytes 7077896 | tf_op jit(solution)/shard_map/ppermute | solution.py:965
  109.5 16.9 %copy-start = (bf16[2048,512]{1,0:T(8,128)(2,1)S(1)}, bf16[2048,512]{1,0:T(8,128)(2,1)}, u32[]{:S(2)}) copy-start(bf16[2048,512]{1,0:T(8,128)(2,1)} %refs_5_.5) | copy-start | bytes 6291460
  109.5 16.9 %copy-start.10 = (bf16[512,1664]{1,0:T(8,128)(2,1)S(1)}, bf16[512,1664]{1,0:T(8,128)(2,1)}, u32[]{:S(2)}) copy-start(bf16[512,1664]{1,0:T(8,128)(2,1)} %get-tuple-element.119.w_ref) | copy-start | bytes 5111812
  109.5 16.9 %copy-start.13 = (f32[16,512]{1,0:T(8,128)S(1)}, f32[16,512]{1,0:T(8,128)}, u32[]{:S(2)}) copy-start(f32[16,512]{1,0:T(8,128)} %get-tuple-element.108.vec_ref.refs_8_) | copy-start | bytes 98308
  109.5 30.4 %collective-permute-start.21 = (bf16[64,4608]{1,0:T(8,128)(2,1)S(1)}, bf16[64,4608]{1,0:T(8,128)(2,1)S(1)}, u32[]{:S(2)}, u32[]{:S(2)}) collective-permute-start(bf16[64,4608]{1,0:T(8,128)(2,1)S(1)} %get-tuple-element.127), channel_id=1, source_target_pairs={{0,4},{1,5},{2,6},{3,7},{4,0},{5,1},{6,2},{7,3},{8,12},{9,13},{10,... | collective-permute-start | bytes 1769480 | tf_op jit(solution)/shard_map/ppermute | solution.py:965
  111.1 28.8 %collective-permute-start.22 = (bf16[64,4608]{1,0:T(8,128)(2,1)S(1)}, bf16[64,4608]{1,0:T(8,128)(2,1)S(1)}, u32[]{:S(2)}, u32[]{:S(2)}) collective-permute-start(bf16[64,4608]{1,0:T(8,128)(2,1)S(1)} %get-tuple-element.128), channel_id=1, source_target_pairs={{0,1},{1,0},{2,3},{3,2},{4,5},{5,4},{6,7},{7,6},{8,9},{9,8},{10,11... | collective-permute-start | bytes 1769480 | tf_op jit(solution)/shard_map/ppermute | solution.py:965
  111.9 28.1 %collective-permute-start.23 = (bf16[64,4608]{1,0:T(8,128)(2,1)S(1)}, bf16[64,4608]{1,0:T(8,128)(2,1)S(1)}, u32[]{:S(2)}, u32[]{:S(2)}) collective-permute-start(bf16[64,4608]{1,0:T(8,128)(2,1)S(1)} %get-tuple-element.129), channel_id=1, source_target_pairs={{0,5},{1,4},{2,7},{3,6},{4,1},{5,0},{6,3},{7,2},{8,13},{9,12},{10,... | collective-permute-start | bytes 1769480 | tf_op jit(solution)/shard_map/ppermute | solution.py:965
  113.1 13.3 %copy-start.11 = (f32[2048,512]{1,0:T(8,128)S(1)}, f32[2048,512]{1,0:T(8,128)}, u32[]{:S(2)}) copy-start(f32[2048,512]{1,0:T(8,128)} %get-tuple-element.118.gmid_ref) | copy-start | bytes 12582916
  132.2 16.9 %copy-start.4 = (bf16[2048,512]{1,0:T(8,128)(2,1)S(1)}, bf16[2048,512]{1,0:T(8,128)(2,1)}, u32[]{:S(2)}) copy-start(bf16[2048,512]{1,0:T(8,128)(2,1)} %get-tuple-element.141.refs_1_) | copy-start | bytes 6291460
  132.2 16.9 %copy-start.5 = (bf16[2048,512]{1,0:T(8,128)(2,1)S(1)}, bf16[2048,512]{1,0:T(8,128)(2,1)}, u32[]{:S(2)}) copy-start(bf16[2048,512]{1,0:T(8,128)(2,1)} %get-tuple-element.142.refs_2_) | copy-start | bytes 6291460
  132.2 16.9 %copy-start.6 = (bf16[2048,512]{1,0:T(8,128)(2,1)S(1)}, bf16[2048,512]{1,0:T(8,128)(2,1)}, u32[]{:S(2)}) copy-start(bf16[2048,512]{1,0:T(8,128)(2,1)} %get-tuple-element.143.refs_3_) | copy-start | bytes 6291460
  132.2 16.9 %copy-start.7 = (bf16[2048,512]{1,0:T(8,128)(2,1)S(1)}, bf16[2048,512]{1,0:T(8,128)(2,1)}, u32[]{:S(2)}) copy-start(bf16[2048,512]{1,0:T(8,128)(2,1)} %get-tuple-element.145.refs_7_) | copy-start | bytes 6291460
  139.9 2.4 %collective-permute-start.24 = (bf16[256,1664]{1,0:T(8,128)(2,1)S(1)}, bf16[256,1664]{1,0:T(8,128)(2,1)S(1)}, u32[]{:S(2)}, u32[]{:S(2)}) collective-permute-start(bf16[256,1664]{1,0:T(8,128)(2,1)S(1)} %get-tuple-element.131), channel_id=1, source_target_pairs={{0,2},{1,3},{2,0},{3,1},{4,6},{5,7},{6,4},{7,5},{8,10},{9,11},{10,... | collective-permute-start | bytes 2555912 | tf_op jit(solution)/shard_map/ppermute | solution.py:965
  142.6 10.5 %collective-permute-start.25 = (bf16[64,1664]{1,0:T(8,128)(2,1)S(1)}, bf16[64,1664]{1,0:T(8,128)(2,1)S(1)}, u32[]{:S(2)}, u32[]{:S(2)}) collective-permute-start(bf16[64,1664]{1,0:T(8,128)(2,1)S(1)} %get-tuple-element.137), channel_id=1, source_target_pairs={{0,4},{1,5},{2,6},{3,7},{4,0},{5,1},{6,2},{7,3},{8,12},{9,13},{10,... | collective-permute-start | bytes 638984 | tf_op jit(solution)/shard_map/ppermute | solution.py:965
  144.2 11.6 %collective-permute-start.26 = (bf16[64,1664]{1,0:T(8,128)(2,1)S(1)}, bf16[64,1664]{1,0:T(8,128)(2,1)S(1)}, u32[]{:S(2)}, u32[]{:S(2)}) collective-permute-start(bf16[64,1664]{1,0:T(8,128)(2,1)S(1)} %get-tuple-element.138), channel_id=1, source_target_pairs={{0,1},{1,0},{2,3},{3,2},{4,5},{5,4},{6,7},{7,6},{8,9},{9,8},{10,11... | collective-permute-start | bytes 638984 | tf_op jit(solution)/shard_map/ppermute | solution.py:965
  144.9 10.8 %collective-permute-start.27 = (bf16[64,1664]{1,0:T(8,128)(2,1)S(1)}, bf16[64,1664]{1,0:T(8,128)(2,1)S(1)}, u32[]{:S(2)}, u32[]{:S(2)}) collective-permute-start(bf16[64,1664]{1,0:T(8,128)(2,1)S(1)} %get-tuple-element.139), channel_id=1, source_target_pairs={{0,5},{1,4},{2,7},{3,6},{4,1},{5,0},{6,3},{7,2},{8,13},{9,12},{10,... | collective-permute-start | bytes 638984 | tf_op jit(solution)/shard_map/ppermute | solution.py:965
  146.4 12.7 %collective-permute-start.33 = (bf16[16,4608]{1,0:T(8,128)(2,1)S(1)}, bf16[16,4608]{1,0:T(8,128)(2,1)S(1)}, u32[]{:S(2)}, u32[]{:S(2)}) collective-permute-start(bf16[16,4608]{1,0:T(8,128)(2,1)S(1)} %get-tuple-element.188), channel_id=1, source_target_pairs={{0,24},{1,25},{2,26},{3,27},{4,28},{5,29},{6,30},{7,31},{8,16},{9,... | collective-permute-start | bytes 442376 | tf_op jit(solution)/shard_map/ppermute | solution.py:965
  149.1 15.0 %collective-permute-start.32 = (bf16[16,4608]{1,0:T(8,128)(2,1)S(1)}, bf16[16,4608]{1,0:T(8,128)(2,1)S(1)}, u32[]{:S(2)}, u32[]{:S(2)}) collective-permute-start(bf16[16,4608]{1,0:T(8,128)(2,1)S(1)} %get-tuple-element.189), channel_id=1, source_target_pairs={{0,16},{1,17},{2,18},{3,19},{4,20},{5,21},{6,22},{7,23},{8,24},{9,... | collective-permute-start | bytes 442376 | tf_op jit(solution)/shard_map/ppermute | solution.py:965
  153.1 11.1 %collective-permute-start.31 = (bf16[16,4608]{1,0:T(8,128)(2,1)S(1)}, bf16[16,4608]{1,0:T(8,128)(2,1)S(1)}, u32[]{:S(2)}, u32[]{:S(2)}) collective-permute-start(bf16[16,4608]{1,0:T(8,128)(2,1)S(1)} %get-tuple-element.190), channel_id=1, source_target_pairs={{0,8},{1,9},{2,10},{3,11},{4,12},{5,13},{6,14},{7,15},{8,0},{9,1},... | collective-permute-start | bytes 442376 | tf_op jit(solution)/shard_map/ppermute | solution.py:965
  155.8 8.4 %collective-permute-start.28 = (bf16[16,1664]{1,0:T(8,128)(2,1)S(1)}, bf16[16,1664]{1,0:T(8,128)(2,1)S(1)}, u32[]{:S(2)}, u32[]{:S(2)}) collective-permute-start(bf16[16,1664]{1,0:T(8,128)(2,1)S(1)} %get-tuple-element.152), channel_id=1, source_target_pairs={{0,8},{1,9},{2,10},{3,11},{4,12},{5,13},{6,14},{7,15},{8,0},{9,1},... | collective-permute-start | bytes 159752 | tf_op jit(solution)/shard_map/ppermute | solution.py:965
  155.9 8.3 %collective-permute-start.29 = (bf16[16,1664]{1,0:T(8,128)(2,1)S(1)}, bf16[16,1664]{1,0:T(8,128)(2,1)S(1)}, u32[]{:S(2)}, u32[]{:S(2)}) collective-permute-start(bf16[16,1664]{1,0:T(8,128)(2,1)S(1)} %get-tuple-element.153), channel_id=1, source_target_pairs={{0,16},{1,17},{2,18},{3,19},{4,20},{5,21},{6,22},{7,23},{8,24},{9,... | collective-permute-start | bytes 159752 | tf_op jit(solution)/shard_map/ppermute | solution.py:965
  159.1 6.0 %collective-permute-start.30 = (bf16[16,1664]{1,0:T(8,128)(2,1)S(1)}, bf16[16,1664]{1,0:T(8,128)(2,1)S(1)}, u32[]{:S(2)}, u32[]{:S(2)}) collective-permute-start(bf16[16,1664]{1,0:T(8,128)(2,1)S(1)} %get-tuple-element.154), channel_id=1, source_target_pairs={{0,24},{1,25},{2,26},{3,27},{4,28},{5,29},{6,30},{7,31},{8,16},{9,... | collective-permute-start | bytes 159752 | tf_op jit(solution)/shard_map/ppermute | solution.py:965
  (20 other events, 76.4 us)
